TPU v7x, 32 devices: a whole 2x2x4 slice. The times are simulated.
32 devices in a mesh: dp: 2 (over x), seq: 4 (over y, core), wt: 4 (over z).
Axes of the slice: x: 2, y: 2, z: 4, core: 2. Of those that a mesh axis runs over, the one named last changes fastest.
Arguments:
- tokens: bfloat16 [8, 1536, 1536], P(('dp', 'wt'), 'seq'), may hold values from -6 to 6
- cotangent: bfloat16 [8, 1536, 1536], P(('dp', 'wt'), 'seq'), may hold values from -6 to 6
- routes: int32 [8, 1536, 8], P(('dp', 'wt'), 'seq'), may hold values from 0 to 19, all different within a row; in each aligned block of 384 rows (0 to 383, 384 to 767, ..., all dimensions but the last counted through in order) at most 192 rows name the same one
- lengths: int32 [8, 8], P(('dp', 'wt')), may hold values from 1 to 192, 512 in all within a row
- group_adapter_index: int32 [8], P(('dp', 'wt')), may hold values from 0 to 7
- attention_norm_gain: bfloat16 [1536], replicated, may hold values from 0.5 to 1.5
- query_weight: bfloat16 [1536, 1536], P(('dp', 'wt')), may hold values from -0.15625 to 0.15625
- key_value_weight: bfloat16 [1536, 1024], P(('dp', 'wt')), may hold values from -0.15625 to 0.15625
- output_weight: bfloat16 [1536, 1536], P(('dp', 'wt')), may hold values from -1.25 to 1.25
- mixture_norm_gain: bfloat16 [1536], replicated, may hold values from 0.5 to 1.5
- router_weight: bfloat16 [1536, 20], P(('dp', 'wt')), may hold values from -0.078125 to 0.078125
- expert_gate_up_weight: bfloat16 [20, 1536, 1024], P('seq', ('dp', 'wt')), may hold values from -0.15625 to 0.15625
- expert_down_weight: bfloat16 [20, 512, 1536], P('seq', ('dp', 'wt')), may hold values from -0.25 to 0.25
- attention_first_factors: bfloat16 [8, 1536, 48], replicated, may hold values from -0.15625 to 0.15625
- query_second_factor: bfloat16 [8, 16, 1536], replicated, may hold values from -0.75 to 0.75
- key_value_second_factors: bfloat16 [8, 2, 16, 512], replicated, may hold values from -0.75 to 0.75
- output_first_factor: bfloat16 [8, 1536, 16], replicated, may hold values from -1.25 to 1.25
- output_second_factor: bfloat16 [8, 16, 1536], replicated, may hold values from -0.75 to 0.75
- mixture_first_factors: bfloat16 [8, 1536, 48], replicated, may hold values from -0.15625 to 0.15625
- router_second_factor: bfloat16 [8, 16, 20], replicated, may hold values from -0.75 to 0.75
- gate_up_second_factors: bfloat16 [8, 2, 16, 512], replicated, may hold values from -0.75 to 0.75
- down_first_factor: bfloat16 [8, 512, 16], replicated, may hold values from -0.25 to 0.25
- down_second_factor: bfloat16 [8, 16, 1536], replicated, may hold values from -0.75 to 0.75
Outputs:
- output: bfloat16 [8, 1536, 1536], P(('dp', 'wt'), 'seq')
- input_grad: float32 [8, 1536, 1536], P(('dp', 'wt'), 'seq')
- grad_attn_lora_a: float32 [8, 1536, 48], P('wt')
- grad_query_lora_b: float32 [8, 16, 1536], P('wt')
- grad_keyvalue_lora_b: float32 [8, 2, 16, 512], P('wt')
- grad_output_lora_a: float32 [8, 1536, 16], P('wt')
- grad_output_lora_b: float32 [8, 16, 1536], P('wt')
- grad_moe_lora_a: float32 [8, 1536, 48], P('wt')
- grad_router_lora_b: float32 [8, 16, 20], P('wt')
- grad_gate_up_lora_b: float32 [8, 2, 16, 512], P('wt')
- grad_down_lora_a: float32 [8, 512, 16], P('wt')
- grad_down_lora_b: float32 [8, 16, 1536], P('wt')
Inputs may be any that keep to these rules, and one draw needn't show every extreme that they name: `routes`: in each aligned block of 384 rows (the rows of one device) no expert is named by more than 192 rows, a bound that some block reaches. `lengths`: each row sums to 512, and its largest entry is 192.
All inputs are finite; a program needn't handle non-finite values.
Results may differ from a plain program's by a relative error of at most 0.018.
Values may be sent and summed in bfloat16 or wider, within the bound.
No kernel may reach another device: no remote copies, remote signals or barrier semaphores. Data moves between devices by JAX's collectives and lax.ppermute only.
A program may use at most 320 MiB of HBM per device.

v0:
```python
import math

import jax
import jax.numpy as jnp
from jax import lax
from jax.sharding import PartitionSpec as P

MODEL_WIDTH = 1536
HEADS = 24
KV_HEADS = 8
HEAD = 64
TOPK = 8
ADAPTER_RANK = 16
ADAPTER_COUNT = 8
EXP_DEV = 5
PROMPT_LEAST = 1024
PROMPT_DEV = 128
QUERY_FEATURES = 1536
KEY_FEATURES = 512


EPS = 1e-05
NEG = -1e30
PRECISE_MODE = lax.Precision.HIGHEST


def simple_product(left, right):
    return jnp.dot(left, right, preferred_element_type=jnp.float32)


def precise_product(left, right):
    return jnp.dot(left, right, precision=PRECISE_MODE, preferred_element_type=jnp.float32)


def norm_forward(value_rows, gain_row):
    inverse = lax.rsqrt(jnp.mean(value_rows * value_rows, axis=-1, keepdims=True) + EPS)
    return (value_rows * inverse * gain_row, inverse)


def norm_backward(value_rows, inverse, gain_row, upstream):
    scaled = upstream * gain_row
    inner_mean = jnp.mean(value_rows * scaled, axis=-1, keepdims=True)
    return inverse * scaled - value_rows * (inverse * inverse * inverse) * inner_mean


def layout(lengths_row, prompt_len, total_len):
    ends = jnp.cumsum(lengths_row)
    starts = ends - lengths_row
    places = jnp.arange(total_len, dtype=jnp.int32)
    offset = places - prompt_len
    counted = jnp.sum((offset[:, None] >= ends[None, :]).astype(jnp.int32), axis=1)
    inside = offset >= 0
    segment = jnp.where(inside, counted, -1)
    picked = jnp.arange(lengths_row.shape[0], dtype=jnp.int32)[None, :] == counted[:, None]
    begin = jnp.sum(jnp.where(picked, starts[None, :], 0), axis=1)
    position = jnp.where(inside, prompt_len + offset - begin, places)
    return (segment, position)


def rope_tables(position, width):
    half_width = width // 2
    freq = jnp.exp(jnp.arange(half_width, dtype=jnp.float32) * (-2.0 * math.log(10000.0) / width))
    angle = position.astype(jnp.float32)[:, None] * freq[None, :]
    return (jnp.cos(angle), jnp.sin(angle))


def rotate(value_rows, cosine, sine):
    half_width = value_rows.shape[-1] // 2
    first = value_rows[..., :half_width]
    second = value_rows[..., half_width:]
    cos_b = cosine[:, None, :]
    sin_b = sine[:, None, :]
    return jnp.concatenate(
        [first * cos_b - second * sin_b, second * cos_b + first * sin_b], axis=-1
    )


def expert_forward_pass(
    token_rows,
    padded_token_rows,
    gate_up_weight_full,
    down_weight_full,
    chosen_gate_up_second,
    chosen_down_first,
    chosen_down_second,
):
    adapter_rank_size = chosen_gate_up_second.shape[1]
    expert_hidden_width = chosen_gate_up_second.shape[2]
    gate_and_up = jnp.einsum(
        "erd,edf->erf", token_rows, gate_up_weight_full, preferred_element_type=jnp.float32
    )
    adapter_extra = jnp.concatenate(
        [
            jnp.einsum(
                "ziw,wy->ziy",
                padded_token_rows[..., :adapter_rank_size],
                chosen_gate_up_second[0],
                preferred_element_type=jnp.float32,
            ),
            jnp.einsum(
                "ziw,wy->ziy",
                padded_token_rows[..., adapter_rank_size:],
                chosen_gate_up_second[1],
                preferred_element_type=jnp.float32,
            ),
        ],
        -1,
    )
    gate_and_up = gate_and_up + adapter_extra
    expert_activation = (
        jax.nn.silu(gate_and_up[..., :expert_hidden_width]) * gate_and_up[..., expert_hidden_width:]
    ).astype(jnp.bfloat16)
    down_rank_state = jnp.einsum(
        "ijm,mn->ijn", expert_activation, chosen_down_first, preferred_element_type=jnp.float32
    ).astype(jnp.bfloat16)
    result = jnp.einsum(
        "umk,ukz->umz", expert_activation, down_weight_full, preferred_element_type=jnp.float32
    ) + jnp.einsum(
        "afp,pv->afv", down_rank_state, chosen_down_second, preferred_element_type=jnp.float32
    )
    return (gate_and_up, expert_activation, down_rank_state, result.astype(jnp.bfloat16))


def expert_backward(
    output_gradient,
    padded_token_rows,
    gate_and_up,
    expert_activation,
    down_rank_state,
    gate_up_weight_full,
    down_weight_full,
    chosen_gate_up_second,
    chosen_down_first,
    chosen_down_second,
):
    adapter_rank_size = chosen_gate_up_second.shape[1]
    expert_hidden_width = chosen_gate_up_second.shape[2]
    grad_inner = jnp.einsum(
        "erd,efd->erf", output_gradient, down_weight_full, preferred_element_type=jnp.float32
    )
    down_rank_gradient = jnp.einsum(
        "yah,zh->yaz", output_gradient, chosen_down_second, preferred_element_type=jnp.float32
    )
    grad_inner = grad_inner + jnp.einsum(
        "axv,tv->axt",
        down_rank_gradient,
        chosen_down_first.astype(jnp.float32),
        precision=PRECISE_MODE,
    )
    grad_d_b = jnp.einsum(
        "erk,erd->kd", down_rank_state, output_gradient, preferred_element_type=jnp.float32
    )
    grad_d_a = jnp.einsum(
        "erf,erk->fk",
        expert_activation.astype(jnp.float32),
        down_rank_gradient,
        precision=PRECISE_MODE,
    )
    gate_part = gate_and_up[..., :expert_hidden_width]
    up_part = gate_and_up[..., expert_hidden_width:]
    sigma = jax.nn.sigmoid(gate_part)
    grad_gate = grad_inner * up_part * sigma * (1.0 + gate_part * (1.0 - sigma))
    grad_up = grad_inner * gate_part * sigma
    grad_both = jnp.concatenate([grad_gate, grad_up], -1).astype(jnp.bfloat16)
    grad_rows = jnp.einsum(
        "erf,edf->erd", grad_both, gate_up_weight_full, preferred_element_type=jnp.float32
    ).astype(jnp.bfloat16)
    grad_rows_z = jnp.concatenate(
        [
            jnp.einsum(
                "erf,kf->erk",
                grad_both[..., :expert_hidden_width],
                chosen_gate_up_second[0],
                preferred_element_type=jnp.float32,
            ),
            jnp.einsum(
                "erf,kf->erk",
                grad_both[..., expert_hidden_width:],
                chosen_gate_up_second[1],
                preferred_element_type=jnp.float32,
            ),
        ],
        -1,
    ).astype(jnp.bfloat16)
    grad_gu_b = jnp.stack(
        [
            jnp.einsum(
                "erk,erf->kf",
                padded_token_rows[..., :adapter_rank_size],
                grad_both[..., :expert_hidden_width],
                preferred_element_type=jnp.float32,
            ),
            jnp.einsum(
                "erk,erf->kf",
                padded_token_rows[..., adapter_rank_size:],
                grad_both[..., expert_hidden_width:],
                preferred_element_type=jnp.float32,
            ),
        ]
    )
    return (grad_rows, grad_rows_z, grad_gu_b, grad_d_a, grad_d_b)


def shards(
    tokens,
    cotangent,
    routes,
    lengths,
    group_adapter_index,
    attention_norm_gain,
    query_weight,
    key_value_weight,
    output_weight,
    mixture_norm_gain,
    router_weight,
    expert_gate_up_weight,
    expert_down_weight,
    attention_first_factors,
    query_second_factor,
    key_value_second_factors,
    output_first_factor,
    output_second_factor,
    mixture_first_factors,
    router_second_factor,
    gate_up_second_factors,
    down_first_factor,
    down_second_factor,
):
    seq_count = lax.axis_size("seq")
    seq_index = lax.axis_index("seq")
    wt_count = lax.axis_size("wt")
    local_tokens = tokens.shape[1]
    total_len = local_tokens * seq_count
    prompt_len = max(PROMPT_LEAST, PROMPT_DEV * seq_count)
    experts_all = EXP_DEV * seq_count
    capacity = max(2, (local_tokens * TOPK * 5 + 4 * experts_all - 1) // (4 * experts_all))
    capacity = min(local_tokens, (capacity + 7) // 8 * 8)
    qblock = min(512, total_len)
    blocks = total_len // qblock
    kv_local = KV_HEADS // seq_count
    group = HEADS // KV_HEADS
    scale = HEAD ** (-0.5)
    local_width = QUERY_FEATURES // seq_count
    index_now = group_adapter_index[0]

    def select_adapter_bank(bank):
        return lax.dynamic_index_in_dim(bank, index_now, 0, keepdims=False)

    chosen_attention_first = select_adapter_bank(attention_first_factors)
    chosen_query_second = select_adapter_bank(query_second_factor)
    chosen_key_value_second = select_adapter_bank(key_value_second_factors)
    chosen_output_first = select_adapter_bank(output_first_factor)
    chosen_output_second = select_adapter_bank(output_second_factor)
    chosen_mixture_first = select_adapter_bank(mixture_first_factors)
    chosen_router_second = select_adapter_bank(router_second_factor)
    chosen_gate_up_second = select_adapter_bank(gate_up_second_factors)
    chosen_down_first = select_adapter_bank(down_first_factor)
    chosen_down_second = select_adapter_bank(down_second_factor)
    query_matrix, key_value_matrix, output_matrix, router_matrix = (
        lax.all_gather(query_weight, ("dp", "wt"), axis=0, tiled=True),
        lax.all_gather(key_value_weight, ("dp", "wt"), axis=0, tiled=True),
        lax.all_gather(output_weight, ("dp", "wt"), axis=0, tiled=True),
        lax.all_gather(router_weight, ("dp", "wt"), axis=0, tiled=True),
    )
    gate_up_weight_chosen, down_weight_chosen = (
        lax.all_gather(expert_gate_up_weight, ("dp", "wt"), axis=1, tiled=True),
        lax.all_gather(expert_down_weight, ("dp", "wt"), axis=1, tiled=True),
    )
    hidden_input = tokens[0].astype(jnp.float32)
    gain_first = attention_norm_gain.astype(jnp.float32)
    gain_second = mixture_norm_gain.astype(jnp.float32)
    normed_f, inverse_a = norm_forward(hidden_input, gain_first)
    attention_normalized = normed_f.astype(jnp.bfloat16)
    attention_rank_state = simple_product(attention_normalized, chosen_attention_first).astype(
        jnp.bfloat16
    )
    query_before_rotation = simple_product(attention_normalized, query_matrix) + simple_product(
        attention_rank_state[:, :ADAPTER_RANK], chosen_query_second
    )
    key_pre = simple_product(
        attention_normalized, key_value_matrix[:, :KEY_FEATURES]
    ) + simple_product(
        attention_rank_state[:, ADAPTER_RANK : 2 * ADAPTER_RANK], chosen_key_value_second[0]
    )
    value_pre = simple_product(
        attention_normalized, key_value_matrix[:, KEY_FEATURES:]
    ) + simple_product(attention_rank_state[:, 2 * ADAPTER_RANK :], chosen_key_value_second[1])
    segment, position = layout(lengths[0], prompt_len, total_len)
    cos_all, sin_all = rope_tables(position, HEAD)
    cos_here = lax.dynamic_slice_in_dim(cos_all, seq_index * local_tokens, local_tokens, 0)
    sin_here = lax.dynamic_slice_in_dim(sin_all, seq_index * local_tokens, local_tokens, 0)
    query_rot = (
        rotate(query_before_rotation.reshape(local_tokens, HEADS, HEAD), cos_here, sin_here)
        .reshape(local_tokens, QUERY_FEATURES)
        .astype(jnp.bfloat16)
    )
    key_rot = (
        rotate(key_pre.reshape(local_tokens, KV_HEADS, HEAD), cos_here, sin_here)
        .reshape(local_tokens, KEY_FEATURES)
        .astype(jnp.bfloat16)
    )
    value_low = value_pre.astype(jnp.bfloat16)
    q_all, k_all, v_all = (
        lax.all_to_all(query_rot, "seq", split_axis=1, concat_axis=0, tiled=True),
        lax.all_to_all(key_rot, "seq", split_axis=1, concat_axis=0, tiled=True),
        lax.all_to_all(value_low, "seq", split_axis=1, concat_axis=0, tiled=True),
    )
    q_heads = q_all.reshape(blocks, qblock, kv_local, group, HEAD)
    k_heads = k_all.reshape(total_len, kv_local, HEAD)
    v_heads = v_all.reshape(total_len, kv_local, HEAD)
    places = jnp.arange(total_len, dtype=jnp.int32)
    seg_blocks = segment.reshape(blocks, qblock)
    place_blocks = places.reshape(blocks, qblock)

    def masked_scores(q_block, seg_block, place_block):
        scores = (
            jnp.einsum("bhgw,thw->hgbt", q_block, k_heads, preferred_element_type=jnp.float32)
            * scale
        )
        allowed = (places[None, :] <= place_block[:, None]) & (
            (segment[None, :] < 0) | (segment[None, :] == seg_block[:, None])
        )
        return jnp.where(allowed[None, None], scores, NEG)

    def attend(group_entry):
        q_block, seg_block, place_block = group_entry
        scores = masked_scores(q_block, seg_block, place_block)
        peak = jnp.max(scores, axis=-1, keepdims=True)
        shifted = jnp.exp(scores - peak)
        totals = jnp.sum(shifted, axis=-1, keepdims=True)
        probs = (shifted / totals).astype(jnp.bfloat16)
        out_block = jnp.einsum("hgbt,thw->bhgw", probs, v_heads, preferred_element_type=jnp.float32)
        return (out_block, peak + jnp.log(totals))

    attention_output, log_totals = lax.map(attend, (q_heads, seg_blocks, place_blocks))
    attention_output = attention_output.reshape(total_len, local_width).astype(jnp.bfloat16)
    attention_local = lax.all_to_all(
        attention_output, "seq", split_axis=0, concat_axis=1, tiled=True
    )
    output_rank_state = simple_product(attention_local, chosen_output_first).astype(jnp.bfloat16)
    residual_stream = (
        hidden_input
        + simple_product(attention_local, output_matrix)
        + simple_product(output_rank_state, chosen_output_second)
    )
    normed_mf, inverse_m = norm_forward(residual_stream, gain_second)
    mixture_normalized = normed_mf.astype(jnp.bfloat16)
    mixture_rank_state = simple_product(mixture_normalized, chosen_mixture_first).astype(
        jnp.bfloat16
    )
    router_logits = simple_product(mixture_normalized, router_matrix) + simple_product(
        mixture_rank_state[:, :ADAPTER_RANK], chosen_router_second
    )
    route_rows = routes[0]
    choose = (
        route_rows[:, :, None] == jnp.arange(experts_all, dtype=jnp.int32)[None, None, :]
    ).astype(jnp.float32)
    chosen = jnp.einsum("nke,ne->nk", choose, router_logits, precision=PRECISE_MODE)
    gating = jax.nn.softmax(chosen, axis=-1)
    flat = route_rows.reshape(-1)
    onehot = (flat[:, None] == jnp.arange(experts_all, dtype=jnp.int32)[None, :]).astype(jnp.int32)
    ranks = jnp.sum(onehot * (jnp.cumsum(onehot, axis=0) - 1), axis=1)
    slots = flat * capacity + ranks
    owner_rows = jnp.arange(flat.shape[0], dtype=jnp.int32) // TOPK
    owners = jnp.full((experts_all * capacity,), local_tokens, jnp.int32).at[slots].set(owner_rows)
    padded = jnp.concatenate([mixture_normalized, jnp.zeros((1, MODEL_WIDTH), jnp.bfloat16)], 0)
    padded_z = jnp.concatenate(
        [mixture_rank_state[:, ADAPTER_RANK:], jnp.zeros((1, 2 * ADAPTER_RANK), jnp.bfloat16)], 0
    )
    send_rows = padded[owners].reshape(experts_all, capacity, MODEL_WIDTH)
    send_z = padded_z[owners].reshape(experts_all, capacity, 2 * ADAPTER_RANK)
    expert_input, expert_padded_rows = (
        lax.all_to_all(send_rows, "seq", split_axis=0, concat_axis=1, tiled=True),
        lax.all_to_all(send_z, "seq", split_axis=0, concat_axis=1, tiled=True),
    )
    gate_and_up, expert_activation, down_rank_state, expert_result = expert_forward_pass(
        expert_input,
        expert_padded_rows,
        gate_up_weight_chosen,
        down_weight_chosen,
        chosen_gate_up_second,
        chosen_down_first,
        chosen_down_second,
    )
    returned = lax.all_to_all(expert_result, "seq", split_axis=1, concat_axis=0, tiled=True)
    picked = (
        returned.reshape(experts_all * capacity, MODEL_WIDTH)[slots]
        .reshape(local_tokens, TOPK, MODEL_WIDTH)
        .astype(jnp.float32)
    )
    output_rows = residual_stream + jnp.einsum("nk,nkd->nd", gating, picked, precision=PRECISE_MODE)
    upstream = cotangent[0].astype(jnp.float32)
    grad_gating = jnp.einsum("nd,nkd->nk", upstream, picked, precision=PRECISE_MODE)
    grad_picked = (
        (gating[:, :, None] * upstream[:, None, :])
        .astype(jnp.bfloat16)
        .reshape(local_tokens * TOPK, MODEL_WIDTH)
    )
    grad_chosen = gating * (grad_gating - jnp.sum(grad_gating * gating, axis=-1, keepdims=True))
    router_logit_gradient = jnp.einsum("nk,nke->ne", grad_chosen, choose, precision=PRECISE_MODE)
    grad_send = (
        jnp.zeros((experts_all * capacity, MODEL_WIDTH), jnp.bfloat16)
        .at[slots]
        .set(grad_picked)
        .reshape(experts_all, capacity, MODEL_WIDTH)
    )
    expert_gradient = lax.all_to_all(grad_send, "seq", split_axis=0, concat_axis=1, tiled=True)
    grad_rows, grad_rows_z, grad_gu_b, grad_d_a, grad_d_b = expert_backward(
        expert_gradient,
        expert_padded_rows,
        gate_and_up,
        expert_activation,
        down_rank_state,
        gate_up_weight_chosen,
        down_weight_chosen,
        chosen_gate_up_second,
        chosen_down_first,
        chosen_down_second,
    )
    back_rows, back_z = (
        lax.all_to_all(grad_rows, "seq", split_axis=1, concat_axis=0, tiled=True),
        lax.all_to_all(grad_rows_z, "seq", split_axis=1, concat_axis=0, tiled=True),
    )
    rows_total = jnp.sum(
        back_rows.reshape(experts_all * capacity, MODEL_WIDTH)[slots]
        .astype(jnp.float32)
        .reshape(local_tokens, TOPK, MODEL_WIDTH),
        axis=1,
    )
    padded_total_rows = jnp.sum(
        back_z.reshape(experts_all * capacity, 2 * ADAPTER_RANK)[slots]
        .astype(jnp.float32)
        .reshape(local_tokens, TOPK, 2 * ADAPTER_RANK),
        axis=1,
    )
    mixture_rank_gradient = jnp.concatenate(
        [
            precise_product(router_logit_gradient, chosen_router_second.astype(jnp.float32).T),
            padded_total_rows,
        ],
        1,
    )
    grad_r_b = precise_product(
        mixture_rank_state[:, :ADAPTER_RANK].astype(jnp.float32).T, router_logit_gradient
    )
    grad_normed_m = (
        rows_total
        + precise_product(router_logit_gradient, router_matrix.astype(jnp.float32).T)
        + precise_product(mixture_rank_gradient, chosen_mixture_first.astype(jnp.float32).T)
    )
    grad_moe_a = precise_product(mixture_normalized.astype(jnp.float32).T, mixture_rank_gradient)
    grad_residual = upstream + norm_backward(residual_stream, inverse_m, gain_second, grad_normed_m)
    branch_gradient = grad_residual.astype(jnp.bfloat16)
    attention_gradient = jnp.einsum(
        "nd,qd->nq", branch_gradient, output_matrix, preferred_element_type=jnp.float32
    )
    output_rank_gradient = jnp.einsum(
        "ye,ze->yz", branch_gradient, chosen_output_second, preferred_element_type=jnp.float32
    )
    grad_o_b = jnp.einsum(
        "nk,nd->kd", output_rank_state, branch_gradient, preferred_element_type=jnp.float32
    )
    attention_gradient = attention_gradient + precise_product(
        output_rank_gradient, chosen_output_first.astype(jnp.float32).T
    )
    grad_o_a = precise_product(attention_local.astype(jnp.float32).T, output_rank_gradient)
    grad_all = lax.all_to_all(
        attention_gradient.astype(jnp.bfloat16), "seq", split_axis=1, concat_axis=0, tiled=True
    )
    grad_heads = grad_all.reshape(blocks, qblock, kv_local, group, HEAD)

    def attend_back(carry, group_entry):
        key_acc, value_acc = carry
        q_block, grad_block, lse_block, seg_block, place_block = group_entry
        scores = masked_scores(q_block, seg_block, place_block)
        probs = jnp.exp(scores - lse_block)
        grad_probs = jnp.einsum(
            "bhgw,thw->hgbt", grad_block, v_heads, preferred_element_type=jnp.float32
        )
        centre = jnp.sum(grad_probs * probs, axis=-1, keepdims=True)
        grad_scores = (probs * (grad_probs - centre)).astype(jnp.bfloat16)
        grad_query = (
            jnp.einsum("hgbt,thw->bhgw", grad_scores, k_heads, preferred_element_type=jnp.float32)
            * scale
        )
        key_acc = (
            key_acc
            + jnp.einsum("hgbt,bhgw->thw", grad_scores, q_block, preferred_element_type=jnp.float32)
            * scale
        )
        value_acc = value_acc + jnp.einsum(
            "hgbt,bhgw->thw",
            probs.astype(jnp.bfloat16),
            grad_block,
            preferred_element_type=jnp.float32,
        )
        return ((key_acc, value_acc), grad_query)

    zero_kv = jnp.zeros((total_len, kv_local, HEAD), jnp.float32)
    (grad_keys, grad_values), grad_queries = lax.scan(
        attend_back, (zero_kv, zero_kv), (q_heads, grad_heads, log_totals, seg_blocks, place_blocks)
    )
    grad_q_heads = (
        rotate(grad_queries.reshape(total_len, kv_local * group, HEAD), cos_all, -sin_all)
        .reshape(total_len, local_width)
        .astype(jnp.bfloat16)
    )
    grad_k_heads = (
        rotate(grad_keys, cos_all, -sin_all)
        .reshape(total_len, kv_local * HEAD)
        .astype(jnp.bfloat16)
    )
    grad_v_heads = grad_values.reshape(total_len, kv_local * HEAD).astype(jnp.bfloat16)
    query_local_gradient, key_local_gradient, value_local_gradient = (
        lax.all_to_all(grad_q_heads, "seq", split_axis=0, concat_axis=1, tiled=True),
        lax.all_to_all(grad_k_heads, "seq", split_axis=0, concat_axis=1, tiled=True),
        lax.all_to_all(grad_v_heads, "seq", split_axis=0, concat_axis=1, tiled=True),
    )
    attention_rank_gradient = jnp.concatenate(
        [
            jnp.einsum(
                "di,bi->db",
                query_local_gradient,
                chosen_query_second,
                preferred_element_type=jnp.float32,
            ),
            jnp.einsum(
                "di,bi->db",
                key_local_gradient,
                chosen_key_value_second[0],
                preferred_element_type=jnp.float32,
            ),
            jnp.einsum(
                "di,bi->db",
                value_local_gradient,
                chosen_key_value_second[1],
                preferred_element_type=jnp.float32,
            ),
        ],
        1,
    )
    grad_q_b = jnp.einsum(
        "nk,nq->kq",
        attention_rank_state[:, :ADAPTER_RANK],
        query_local_gradient,
        preferred_element_type=jnp.float32,
    )
    grad_kv_b = jnp.stack(
        [
            jnp.einsum(
                "nk,nq->kq",
                attention_rank_state[:, ADAPTER_RANK : 2 * ADAPTER_RANK],
                key_local_gradient,
                preferred_element_type=jnp.float32,
            ),
            jnp.einsum(
                "nk,nq->kq",
                attention_rank_state[:, 2 * ADAPTER_RANK :],
                value_local_gradient,
                preferred_element_type=jnp.float32,
            ),
        ]
    )
    normalized_gradient = jnp.einsum(
        "nq,dq->nd", query_local_gradient, query_matrix, preferred_element_type=jnp.float32
    )
    normalized_gradient = normalized_gradient + jnp.einsum(
        "nq,dq->nd",
        key_local_gradient,
        key_value_matrix[:, :KEY_FEATURES],
        preferred_element_type=jnp.float32,
    )
    normalized_gradient = normalized_gradient + jnp.einsum(
        "nq,dq->nd",
        value_local_gradient,
        key_value_matrix[:, KEY_FEATURES:],
        preferred_element_type=jnp.float32,
    )
    normalized_gradient = normalized_gradient + precise_product(
        attention_rank_gradient, chosen_attention_first.astype(jnp.float32).T
    )
    grad_qkv_a = precise_product(
        attention_normalized.astype(jnp.float32).T, attention_rank_gradient
    )
    grad_input = grad_residual + norm_backward(
        hidden_input, inverse_a, gain_first, normalized_gradient
    )
    selector = (jnp.arange(ADAPTER_COUNT, dtype=jnp.int32) == index_now).astype(jnp.float32)

    def spread(grad):
        return selector.reshape((ADAPTER_COUNT,) + (1,) * grad.ndim) * grad[None]

    summed = lax.psum(
        (
            spread(grad_qkv_a),
            spread(grad_q_b),
            spread(grad_kv_b),
            spread(grad_o_a),
            spread(grad_o_b),
            spread(grad_moe_a),
            spread(grad_r_b),
            spread(grad_gu_b),
            spread(grad_d_a),
            spread(grad_d_b),
        ),
        ("dp", "seq", "wt"),
    )
    share = ADAPTER_COUNT // wt_count
    first_row = lax.axis_index("wt") * share
    results = tuple(
        (lax.dynamic_slice_in_dim(group_entry, first_row, share, 0) for group_entry in summed)
    )
    return (output_rows[None].astype(jnp.bfloat16), grad_input[None]) + tuple(results)


def solution(mesh):
    placed = (
        P(("dp", "wt"), "seq", None),
        P(("dp", "wt"), "seq", None),
        P(("dp", "wt"), "seq", None),
        P(("dp", "wt"), None),
        P(("dp", "wt")),
        P(),
        P(("dp", "wt"), None),
        P(("dp", "wt"), None),
        P(("dp", "wt"), None),
        P(),
        P(("dp", "wt"), None),
        P("seq", ("dp", "wt"), None),
        P("seq", ("dp", "wt"), None),
        P(),
        P(),
        P(),
        P(),
        P(),
        P(),
        P(),
        P(),
        P(),
        P(),
    )
    return jax.shard_map(
        shards,
        mesh=mesh,
        in_specs=placed,
        out_specs=(
            P(("dp", "wt"), "seq", None),
            P(("dp", "wt"), "seq", None),
            P("wt", None, None),
            P("wt", None, None),
            P("wt", None, None, None),
            P("wt", None, None),
            P("wt", None, None),
            P("wt", None, None),
            P("wt", None, None),
            P("wt", None, None, None),
            P("wt", None, None),
            P("wt", None, None),
        ),
        check_vma=False,
    )
```

profile of v0, /device:TPU:0, one launch (start us, length us, event | category | flops | bytes accessed | tf_op | source)
XLA Modules:
  0.0 1929.9 jit_solution(14785756532432225602)
XLA Ops:
  29.4 44.0 %all-gather.9.cloned.1.call-done = bf16[1536,1024]{1,0:T(8,128)(2,1)} async-done(((bf16[192,1024]{1,0:T(8,128)(2,1)}), bf16[1536,1024]{1,0:T(8,128)(2,1)}) %all-gather.9.cloned.1.call-update) | async-done | bytes 3145744 | tf_op jit(solution)/shard_map/all_gather | solution.py:261
  86.4 67.6 %all-gather.7.cloned.1.call-done = bf16[1536,1536]{1,0:T(8,128)(2,1)} async-done(((bf16[192,1536]{1,0:T(8,128)(2,1)}), bf16[1536,1536]{1,0:T(8,128)(2,1)}) %all-gather.7.cloned.1.call-update) | async-done | bytes 4718608 | tf_op jit(solution)/shard_map/all_gather | solution.py:260
  203.0 57.5 %while.28 = (s32[]{:T(128)}, bf16[3,512,2,3,64]{1,4,3,2,0:T(8,128)(2,1)}, f32[3,2,3,512,1]{3,2,1,4,0:T(4,128)}, s32[3,512]{1,0:T(4,128)}, s32[1536]{0:T(1024)}, ...) while((s32[]{:T(128)}, ...), condition=%wide.region_7.8_spmd.clone, body=%wide.region_4.7_spmd.clone.sunk | while | flops 1267726848 | bytes 61866092 | solution.py:335
  315.1 13.7 gather_fusion
  345.9 119.0 %all-to-all-done.4 = bf16[20,192,1536]{2,1,0:T(8,128)(2,1)} async-done(((bf16[20,192,1536]{2,1,0:T(8,128)(2,1)}), bf16[20,192,1536]{2,1,0:T(8,128)(2,1)}, u32[]{:S(2)}, u32[]{:S(2)}) %all-to-all-start.4) | async-done | bytes 11796512 | tf_op jit(solution)/shard_map/all_to_all | solution.py:373
  475.0 25.6 %maximum_add_fusion = f32[5,768,1024]{2,1,0:T(8,128)} fusion(f32[5,768,512]{2,1,0:T(8,128)} %fusion.128, f32[5,768,512]{2,1,0:T(8,128)} %fusion.131, bf16[5,768,1536]{2,1,0:T(8,128)(2,1)} %bitcast.509, bf16[5,1536,1024]{2,1,0:T(8,128)(2,1)} %all-gather.13.cloned.1.call-done), kind=kOutput, calls=%fused_computation.79 | convolution fusion | flops 12087459840 | bytes 58982400 | tf_op jit(solution)/shard_map/erd,edf->erf/dot_general | solution.py:89
  511.2 56.6 %all-gather.15.cloned.1.call-done = bf16[5,512,1536]{2,1,0:T(8,128)(2,1)} async-done(((bf16[5,64,1536]{2,1,0:T(8,128)(2,1)}), bf16[5,512,1536]{2,1,0:T(8,128)(2,1)}) %all-gather.15.cloned.1.call-update) | async-done | bytes 7864336 | tf_op jit(solution)/shard_map/all_gather | solution.py:267
  567.8 14.5 fusion.224
  582.4 13.6 add_convert_fusion
  596.0 17.6 copy.248
  621.1 30.9 %all-gather = bf16[8,192,20]{1,2,0:T(8,128)(2,1)S(1)} all-gather(bf16[1,192,20]{1,2,0:T(8,128)(2,1)} %bitcast.548), channel_id=1, replica_groups=mesh['dp'=2,'seq'=4,'wt'=4] {'dp','wt'}, dimensions={0}, use_global_device_ids=true | all-gather | bytes 69120 | tf_op jit(solution)/shard_map/all_gather | solution.py:263
  659.1 167.5 %all-to-all-done.6 = bf16[5,768,1536]{2,0,1:T(8,128)(2,1)} async-done(((bf16[5,768,1536]{2,0,1:T(8,128)(2,1)}), bf16[5,768,1536]{2,0,1:T(8,128)(2,1)}, u32[]{:S(2)}, u32[]{:S(2)}) %all-to-all-start.6) | async-done | bytes 11796512 | tf_op jit(solution)/shard_map/all_to_all | solution.py:385
  826.6 14.8 copy.249
  841.5 25.1 %gather_fusion.2 = bf16[3072,1536]{1,0:T(8,128)(2,1)} fusion(bf16[3840,1536]{1,0:T(8,128)(2,1)} %bitcast.496, s32[3072]{0:T(1024)S(1)} %copy-done.51), kind=kCustom, calls=%fused_computation.2 | custom fusion | bytes 18886656 | tf_op jit(solution)/shard_map/gather | solution.py:387
  880.5 22.4 %scatter_custom_fusion.1 = bf16[3840,1536]{1,0:T(8,128)(2,1)} fusion(s32[3072]{0:T(1024)} %bitcast.545, f32[384,1536]{1,0:T(8,128)S(1)} %copy-done.24, f32[3072]{0:T(1024)} %mul.545, bf16[]{:T(256)} %constant.153.clone.1), kind=kCustom, calls=%fused_computation.81 | custom fusion | flops 9437184 | bytes 14168576 | tf_op jit(solution)/shard_map/scatter | solution.py:404
  902.9 134.0 %all_to_all.221 = bf16[20,192,1536]{2,1,0:T(8,128)(2,1)S(1)} all-to-all(bf16[20,192,1536]{2,1,0:T(8,128)(2,1)} %bitcast.504), channel_id=1, replica_groups=mesh['dp'=2,'seq'=4,'wt'=4] {'seq'}, dimensions={0} | all-to-all | bytes 23592960 | tf_op jit(solution)/shard_map/all_to_all | solution.py:407
  1049.2 20.1 %multiply_convert_fusion.1 = (bf16[5,768,512]{2,1,0:T(8,128)(2,1)}, bf16[5,768,512]{2,1,0:T(8,128)(2,1)}) fusion(f32[5,768,1024]{2,1,0:T(8,128)} %maximum_add_fusion, f32[5,768,512]{2,1,0:T(8,128)} %fusion.155, bf16[5,768,1536]{2,1,0:T(8,128)(2,1)} %bitcast.498, bf16[5,512,1536]{2,1,0:T(8,128)(2,1)} %all-gather.15.cloned.1.call-done), kind=kOutput, calls=%fused_computation.92 | convolution fusion | flops 6067322880 | bytes 51118080 | tf_op jit(solution)/shard_map/erd,efd->erf/dot_general | solution.py:138
  1081.0 23.2 %convolution_convert_fusion = bf16[5,768,1536]{2,1,0:T(8,128)(2,1)} fusion(bf16[5,1536,1024]{2,1,0:T(8,128)(2,1)} %all-gather.13.cloned.1.call-done, bf16[5,768,512]{2,1,0:T(8,128)(2,1)} %get-tuple-element.388, bf16[5,768,512]{2,1,0:T(8,128)(2,1)} %get-tuple-element.387), kind=kOutput, calls=%fused_computation.80 | convolution fusion | flops 12101222400 | bytes 35389440 | tf_op jit(solution)/shard_map/erf,edf->erd/dot_general | solution.py:165
  1104.2 17.2 copy.253
  1172.9 161.5 %all-to-all-done.8 = bf16[5,768,1536]{2,0,1:T(8,128)(2,1)} async-done(((bf16[5,768,1536]{2,0,1:T(8,128)(2,1)}), bf16[5,768,1536]{2,0,1:T(8,128)(2,1)}, u32[]{:S(2)}, u32[]{:S(2)}) %all-to-all-start.8) | async-done | bytes 11796512 | tf_op jit(solution)/shard_map/all_to_all | solution.py:421
  1334.5 15.0 copy.254
  1349.4 25.2 %gather_fusion.3 = bf16[3072,1536]{1,0:T(8,128)(2,1)} fusion(bf16[3840,1536]{1,0:T(8,128)(2,1)} %bitcast.495, s32[3072]{0:T(1024)S(1)} %copy-done.52), kind=kCustom, calls=%fused_computation.3 | custom fusion | bytes 18886656 | tf_op jit(solution)/shard_map/gather | solution.py:425
  1432.5 232.2 %while.29 = (s32[]{:T(128)}, f32[1536,2,64]{0,2,1:T(8,128)S(1)}, f32[1536,2,64]{0,2,1:T(8,128)}, f32[3,512,2,3,64]{1,0,4,3,2:T(4,128)}, bf16[3,512,2,3,64]{1,4,3...) while((s32[]{:T(128)}, f32[1536,2,64]{0,2,1:T(8,128)S(1)}, ...), condition=%wide.region_22.23_spmd.clone, body=%wide.region_20.22_spmd.clone.sunk | while | flops 3095001600 | bytes 192398512 | solution.py:500
  1445.5 14.0 fusion.313
  1478.0 16.1 dynamic_update_slice.21
  1522.7 14.0 fusion.313
  1536.7 13.2 fusion.314
  1555.2 16.1 dynamic_update_slice.21
  1600.1 14.1 fusion.313
  1632.7 16.1 dynamic_update_slice.21
  1719.3 41.3 %psum.76 = f32[8,16,20]{2,1,0:T(8,128)} all-reduce(f32[8,16,20]{2,1,0:T(8,128)} %broadcast_multiply_fusion.9), channel_id=1, replica_groups=mesh['dp'=2,'seq'=4,'wt'=4] {'dp','seq','wt'}, use_global_device_ids=true, to_apply=%region_30.31 | all-reduce | flops 2560 | bytes 20480 | tf_op jit(solution)/shard_map/psum | solution.py:593
  1774.0 133.9 %all-reduce.5.cloned.1.call-done = (f32[8,1536,48]{1,2,0:T(8,128)}, f32[8,16,1536]{2,1,0:T(8,128)}, f32[8,2,16,512]{3,2,1,0:T(8,128)}, f32[8,1536,16]{1,2,0:T(8,...) async-done(((f32[8,1536,48]{1,2,0:T(8,128)}, ...) | async-done | bytes 9175056 | tf_op jit(solution)/shard_map/psum | solution.py:593
  (448 shorter events, 605.1 us)
Async XLA Ops:
  7.2 293.2 %copy-start = (bf16[8,1536,48]{1,2,0:T(8,128)(2,1)S(1)}, bf16[8,1536,48]{1,2,0:T(8,128)(2,1)}, u32[]{:S(2)}) copy-start(bf16[8,1536,48]{1,2,0:T(8,128)(2,1)} %param.45) | copy-start | bytes 3538948
  7.2 66.2 %all-gather.9.cloned.1.call-start = ((), (), s32[]{:S(2)}) async-start(), calls=%async_computation.15 | async-start | bytes 3538944 | tf_op jit(solution)/shard_map/all_gather | solution.py:261
  8.0 146.1 %all-gather.7.cloned.1.call-start = ((), (), s32[]{:S(2)}) async-start(), calls=%async_computation.14 | async-start | bytes 5308416 | tf_op jit(solution)/shard_map/all_gather | solution.py:260
  8.7 283.9 %all-gather.11.cloned.1.call-start = ((), (), s32[]{:S(2)}) async-start(), calls=%async_computation.16 | async-start | bytes 5308416 | tf_op jit(solution)/shard_map/all_gather | solution.py:262
  9.5 465.6 %all-gather.13.cloned.1.call-start = ((), (), s32[]{:S(2)}) async-start(), calls=%async_computation.17 | async-start | bytes 17694720 | tf_op jit(solution)/shard_map/all_gather | solution.py:266
  10.0 557.8 %all-gather.15.cloned.1.call-start = ((), (), s32[]{:S(2)}) async-start(), calls=%async_computation.18 | async-start | bytes 8847360 | tf_op jit(solution)/shard_map/all_gather | solution.py:267
  13.2 140.8 %copy-start.78 = (f32[384]{0:T(512)}, f32[384]{0:T(512)S(1)}, u32[]{:S(2)}) copy-start(f32[384]{0:T(512)S(1)} %get-tuple-element.403) | copy-start | bytes 4612
  13.2 140.8 %copy-start.68 = (f32[1536]{0:T(1024)}, f32[1536]{0:T(1024)S(1)}, u32[]{:S(2)}) copy-start(f32[1536]{0:T(1024)S(1)} %convert_element_type.174) | copy-start | bytes 18436
  16.3 61.8 %copy-start.44 = (f32[384,32]{0,1:T(8,128)}, f32[384,32]{0,1:T(8,128)S(1)}, u32[]{:S(2)}) copy-start(f32[384,32]{0,1:T(8,128)S(1)} %constant_dynamic-slice_fusion.16) | copy-start | bytes 147460
  16.3 61.8 %copy-start.45 = (f32[384,32]{0,1:T(8,128)}, f32[384,32]{0,1:T(8,128)S(1)}, u32[]{:S(2)}) copy-start(f32[384,32]{0,1:T(8,128)S(1)} %constant_dynamic-slice_fusion.15) | copy-start | bytes 147460
  17.9 140.6 %copy-start.53 = (bf16[384,48]{0,1:T(8,128)(2,1)}, bf16[384,48]{0,1:T(8,128)(2,1)S(1)}, u32[]{:S(2)}) copy-start(bf16[384,48]{0,1:T(8,128)(2,1)S(1)} %fusion.112) | copy-start | bytes 110596
  28.0 45.4 %copy-start.33 = (s32[20,24,128]{2,1,0:T(8,128)}, s32[20,24,128]{2,1,0:T(8,128)S(1)}, u32[]{:S(2)}) copy-start(s32[20,24,128]{2,1,0:T(8,128)S(1)} %reduce-window.11) | copy-start | bytes 737284
  79.0 84.3 %all-to-all-start.1 = ((bf16[384,4,128]{0,2,1:T(8,128)(2,1)}), bf16[384,4,128]{0,2,1:T(8,128)(2,1)}, u32[]{:S(2)}, u32[]{:S(2)}) async-start(bf16[384,4,128]{0,2,1:T(8,128)(2,1)} %bitcast.15), calls=%async_computation.1 | async-start | bytes 786432 | tf_op jit(solution)/shard_map/all_to_all | solution.py:305
  163.4 11.6 all-to-all-start.2
  175.0 20.0 %all-to-all-start = ((bf16[384,4,384]{0,2,1:T(8,128)(2,1)}), bf16[384,4,384]{0,2,1:T(8,128)(2,1)S(1)}, u32[]{:S(2)}, u32[]{:S(2)}) async-start(bf16[384,4,384]{0,2,1:T(8,128)(2,1)} %bitcast.11), calls=%async_computation | async-start | bytes 2359296 | tf_op jit(solution)/shard_map/all_to_all | solution.py:304
  271.4 19.5 %all-to-all-start.3 = ((bf16[4,384,384]{1,2,0:T(8,128)(2,1)}), bf16[4,384,384]{1,2,0:T(8,128)(2,1)S(1)}, u32[]{:S(2)}, u32[]{:S(2)}) async-start(bf16[4,384,384]{1,2,0:T(8,128)(2,1)} %copy.237), calls=%async_computation.3 | async-start | bytes 2359296 | tf_op jit(solution)/shard_map/all_to_all | solution.py:337
  310.3 18.5 all-to-all-start.5
  328.8 136.2 %all-to-all-start.4 = ((bf16[20,192,1536]{2,1,0:T(8,128)(2,1)}), bf16[20,192,1536]{2,1,0:T(8,128)(2,1)}, u32[]{:S(2)}, u32[]{:S(2)}) async-start(bf16[20,192,1536]{2,1,0:T(8,128)(2,1)} %bitcast.503), calls=%async_computation.4 | async-start | bytes 23592960 | tf_op jit(solution)/shard_map/all_to_all | solution.py:373
  511.2 71.1 %copy-start.38 = (bf16[5,768,16]{1,2,0:T(8,128)(2,1)}, bf16[5,768,16]{1,2,0:T(8,128)(2,1)S(1)}, u32[]{:S(2)}) copy-start(bf16[5,768,16]{1,2,0:T(8,128)(2,1)S(1)} %convolution_convert_fusion.3) | copy-start | bytes 368644
  613.6 40.8 %copy-start.66 = (s32[3072,1]{0,1:T(1,128)S(1)}, s32[3072,1]{0,1:T(1,128)}, u32[]{:S(2)}) copy-start(s32[3072,1]{0,1:T(1,128)} %compare_select_fusion) | copy-start | bytes 36868
  613.6 41.4 %copy-start.27 = (bf16[1,384,1536]{2,1,0:T(8,128)(2,1)S(1)}, bf16[1,384,1536]{2,1,0:T(8,128)(2,1)}, u32[]{:S(2)}) copy-start(bf16[1,384,1536]{2,1,0:T(8,128)(2,1)} %param.28) | copy-start | bytes 3538948
  613.6 213.1 %all-to-all-start.6 = ((bf16[5,768,1536]{2,0,1:T(8,128)(2,1)}), bf16[5,768,1536]{2,0,1:T(8,128)(2,1)}, u32[]{:S(2)}, u32[]{:S(2)}) async-start(bf16[5,768,1536]{2,0,1:T(8,128)(2,1)} %copy.248), calls=%async_computation.6 | async-start | bytes 37748736 | tf_op jit(solution)/shard_map/all_to_all | solution.py:385
  658.2 183.2 %copy-start.37 = (f32[384,8]{1,0:T(8,128)}, f32[384,8]{1,0:T(8,128)S(1)}, u32[]{:S(2)}) copy-start(f32[384,8]{1,0:T(8,128)S(1)} %copy.277) | copy-start | bytes 36868
  1077.2 44.2 %all-to-all-start.9 = ((bf16[4,2,15360]{2,1,0:T(2,128)(2,1)}), bf16[4,2,15360]{2,1,0:T(2,128)(2,1)S(1)}, u32[]{:S(2)}, u32[]{:S(2)}) async-start(bf16[4,2,15360]{2,1,0:T(2,128)(2,1)} %reshape.652), calls=%async_computation.9 | async-start | bytes 491520 | tf_op jit(solution)/shard_map/all_to_all | solution.py:422
  1121.4 213.1 %all-to-all-start.8 = ((bf16[5,768,1536]{2,0,1:T(8,128)(2,1)}), bf16[5,768,1536]{2,0,1:T(8,128)(2,1)}, u32[]{:S(2)}, u32[]{:S(2)}) async-start(bf16[5,768,1536]{2,0,1:T(8,128)(2,1)} %copy.253), calls=%async_computation.8 | async-start | bytes 37748736 | tf_op jit(solution)/shard_map/all_to_all | solution.py:421
  1130.4 279.2 %copy-start.71 = (f32[8]{0:T(128)}, f32[8]{0:T(128)S(1)}, u32[]{:S(2)}) copy-start(f32[8]{0:T(128)S(1)} %compare_convert_fusion) | copy-start | bytes 100
  1133.0 252.9 %copy-start.36 = (f32[384,1,20]{2,1,0:T(1,128)}, f32[384,1,20]{2,1,0:T(1,128)S(1)}, u32[]{:S(2)}) copy-start(f32[384,1,20]{2,1,0:T(1,128)S(1)} %fusion.225) | copy-start | bytes 92164
  1401.7 20.3 %all-to-all-start.10 = ((bf16[384,4,384]{0,2,1:T(8,128)(2,1)}), bf16[384,4,384]{0,2,1:T(8,128)(2,1)}, u32[]{:S(2)}, u32[]{:S(2)}) async-start(bf16[384,4,384]{0,2,1:T(8,128)(2,1)} %bitcast.523), calls=%async_computation.10 | async-start | bytes 2359296 | tf_op jit(solution)/shard_map/all_to_all | solution.py:467
  1666.8 12.3 all-to-all-start.12
  1679.1 10.9 all-to-all-start.13
  1690.0 19.4 %all-to-all-start.11 = ((bf16[4,384,384]{1,2,0:T(8,128)(2,1)}), bf16[4,384,384]{1,2,0:T(8,128)(2,1)S(1)}, u32[]{:S(2)}, u32[]{:S(2)}) async-start(bf16[4,384,384]{1,2,0:T(8,128)(2,1)} %copy.263), calls=%async_computation.11 | async-start | bytes 2359296 | tf_op jit(solution)/shard_map/all_to_all | solution.py:515
  1693.5 214.5 %all-reduce.5.cloned.1.call-start = ((), (), s32[]{:S(2)}) async-start(), calls=%async_computation.19 | async-start | bytes 18350080 | tf_op jit(solution)/shard_map/psum | solution.py:593
  (77 other events, 500.3 us)
Sparse Core Ops, SparseCore 0:
  10.1 63.2 all-gather.8
  75.5 78.5 all-gather.6
  156.1 78.0 all-gather.10
  236.2 212.9 all-gather.12
  451.2 116.5 all-gather.14
  1717.6 190.2 all-reduce.4
where the time goes:
time: 1940 us; the launch traced here: 1930 us
  waiting for transfers between devices  791 us (41%)
  matrix products  377 us (19%)
  local copies, waits for them, and re-layouts  323 us (17%)
  blocking collectives  206 us (11%)
  other arithmetic  156 us (8%)
  starting transfers between devices  60.5 us (3%)
    all_to_all x1, waiting for transfers between devices, shards(): lax.all_to_all(expert_result, 'seq', split_axis=1, concat_axis=0, tiled=T...  168 us
    all_to_all x1, waiting for transfers between devices, shards(): lax.all_to_all(grad_rows, 'seq', split_axis=1, concat_axis=0, tiled=True)  162 us
    all_to_all x1, blocking collectives, shards(): lax.all_to_all(grad_send, 'seq', split_axis=0, concat_axis=1, tiled=True)  134 us
    psum x1, waiting for transfers between devices, shards(): lax.psum((spread(grad_qkv_a), spread(grad_q_b), spread(grad_kv_b), spread...  134 us
    all_to_all x1, waiting for transfers between devices, shards(): lax.all_to_all(send_rows, 'seq', split_axis=0, concat_axis=1, tiled=True)  119 us
    all_gather x1, waiting for transfers between devices, shards(): lax.all_gather(query_weight, ('dp', 'wt'), axis=0, tiled=True)  67.6 us
    all_gather x1, waiting for transfers between devices, shards(): lax.all_gather(expert_down_weight, ('dp', 'wt'), axis=1, tiled=True)  56.6 us
    dynamic_update_slice x6, local copies, waits for them, and re-layouts, shards(): lax.map(attend, (q_heads, seg_blocks, place_blocks))  53.3 us
  transfers between devices with their start and end apart: 19, of which 13 were waited for; matrix products, arithmetic and copies ran while one was open for 18% of the time, Pallas kernels for 0%

commit v1 on v0

v1 whole, which is shorter than its diff:
```python
import functools
import math

import jax
import jax.numpy as jnp
from jax import lax
from jax.experimental import pallas as pl
from jax.experimental.pallas import tpu as pltpu
from jax.sharding import PartitionSpec as P

MODEL_WIDTH = 1536
HEADS = 24
KV_HEADS = 8
HEAD = 64
HIDDEN = 512
ADAPTER_RANK = 16
ADAPTER_COUNT = 8
PROMPT_LEAST = 1024
PROMPT_DEV = 128
KEY_FEATURES = 512
LANES = 128
SMALL_AT = 96

EPS = 1e-05
NEG = -1e30
F32 = jnp.float32
BF16 = jnp.bfloat16
CHUNKS = (5,)
QB = 256


def dot(a, b, dims=((1,), (0,))):
    return lax.dot_general(a, b, (dims, ((), ())), preferred_element_type=F32)


def dot_nt(a, b):
    return dot(a, b, ((1,), (1,)))


def dot_tn(a, b):
    return dot(a, b, ((0,), (0,)))


def swap_core(x, n_seq):
    return lax.ppermute(x, "seq", [(i, i ^ 1) for i in range(n_seq)])


def shift_chip(x, n_seq, k):
    n_y = n_seq // 2
    pairs = [(y * 2 + c, (y + k) % n_y * 2 + c) for y in range(n_y) for c in range(2)]
    return lax.ppermute(x, "seq", pairs)


def gather_seq(x, n_seq):
    n_y = n_seq // 2
    me = lax.axis_index("seq")
    y, c = me // 2, me % 2
    pieces = [(0, 0, x)]
    far = [shift_chip(x, n_seq, k) for k in range(1, n_y)]
    pieces.append((0, 1, swap_core(x, n_seq)))
    for k, piece in enumerate(far, 1):
        pieces.append((k, 0, piece))
        pieces.append((k, 1, swap_core(piece, n_seq)))
    out = jnp.zeros((n_seq,) + x.shape, x.dtype)
    for k, other, piece in pieces:
        at = (y + n_y - k) % n_y * 2 + (c + other) % 2
        out = lax.dynamic_update_slice_in_dim(out, piece[None], at, 0)
    return out


def scatter_seq(x, n_seq):
    n_y = n_seq // 2
    me = lax.axis_index("seq")
    y, c = me // 2, me % 2

    def block(k, core):
        return lax.dynamic_index_in_dim(x, (y + k) % n_y * 2 + core, 0, keepdims=False)

    total = None
    for k in [*range(1, n_y), 0]:
        got = swap_core(block(k, 1 - c), n_seq)
        both = block(k, c).astype(F32) + got.astype(F32)
        if k:
            both = shift_chip(both.astype(x.dtype), n_seq, k).astype(F32)
        total = both if total is None else total + both
    return total


def shift(x, axis, count, k):
    return lax.ppermute(x, axis, [(i, (i + k) % count) for i in range(count)])


def column_fold(x, op):
    rows, width = x.shape
    return op(x.reshape(rows // 8, 8, width), axis=0)


def attend_kernel(
    prompt_blocks, q_ref, k_ref, v_ref, segq_ref, segk_ref, o_ref, p_ref, inv_ref, krow, scores
):
    i = pl.program_id(1)
    group, qb = q_ref.shape[1], q_ref.shape[3]
    width = group * qb

    @pl.when(i == 0)
    def _():
        krow[...] = k_ref[0].astype(F32).T.astype(BF16)

    q = jnp.concatenate([q_ref[0, h] for h in range(group)], axis=1)
    segq = jnp.concatenate([segq_ref[...]] * group, axis=1)
    placeq = i * qb + lax.broadcasted_iota(jnp.int32, (1, width), 1) % qb

    def score(j, peak, masked):
        rows = pl.ds(pl.multiple_of(j * qb, qb), qb)
        s = dot(krow[rows, :], q)
        if masked:
            segk = segk_ref[rows, :]
            placek = j * qb + lax.broadcasted_iota(jnp.int32, (qb, 1), 0)
            keep = (placek <= placeq) & ((segk < 0) | (segk == segq))
            s = jnp.where(keep, s, NEG)
        scores[rows, :] = s
        return jnp.maximum(peak, column_fold(s, jnp.max))

    free = jnp.minimum(i, prompt_blocks)
    peak = jnp.full((8, width), NEG, F32)
    peak = lax.fori_loop(0, free, lambda j, m: score(j, m, False), peak)
    peak = lax.fori_loop(free, i + 1, lambda j, m: score(j, m, True), peak)
    peak = jnp.max(peak, axis=0, keepdims=True)

    def weigh(j, carry):
        total, acc = carry
        rows = pl.ds(pl.multiple_of(j * qb, qb), qb)
        p = jnp.exp(scores[rows, :] - peak)
        low = p.astype(BF16)
        p_ref[0, 0, rows, :] = low
        return total + column_fold(p, jnp.sum), acc + dot(v_ref[0, :, rows], low)

    total, acc = lax.fori_loop(
        0, i + 1, weigh, (jnp.zeros((8, width), F32), jnp.zeros((HEAD, width), F32))
    )
    inverse = 1.0 / jnp.sum(total, axis=0, keepdims=True)
    inv_ref[0, 0] = inverse
    out = (acc * inverse).astype(BF16)
    for h in range(group):
        o_ref[0, h] = out[:, h * qb : (h + 1) * qb]


def attend(qt, kt, vt, segment, prompt_len):
    kv, group, _, total = qt.shape
    blocks = total // QB
    width = group * QB
    pairs = kv * group * total * total // 2
    return pl.pallas_call(
        functools.partial(attend_kernel, prompt_len // QB),
        grid=(kv, blocks),
        in_specs=[
            pl.BlockSpec((1, group, HEAD, QB), lambda b, i: (b, 0, 0, i)),
            pl.BlockSpec((1, HEAD, total), lambda b, i: (b, 0, 0)),
            pl.BlockSpec((1, HEAD, total), lambda b, i: (b, 0, 0)),
            pl.BlockSpec((1, QB), lambda b, i: (0, i)),
            pl.BlockSpec((total, 1), lambda b, i: (0, 0)),
        ],
        out_specs=[
            pl.BlockSpec((1, group, HEAD, QB), lambda b, i: (b, 0, 0, i)),
            pl.BlockSpec((1, 1, total, width), lambda b, i: (b, i, 0, 0)),
            pl.BlockSpec((1, 1, 1, width), lambda b, i: (b, i, 0, 0)),
        ],
        out_shape=[
            jax.ShapeDtypeStruct(qt.shape, BF16),
            jax.ShapeDtypeStruct((kv, blocks, total, width), BF16),
            jax.ShapeDtypeStruct((kv, blocks, 1, width), F32),
        ],
        scratch_shapes=[pltpu.VMEM((total, HEAD), BF16), pltpu.VMEM((total, width), F32)],
        compiler_params=pltpu.CompilerParams(vmem_limit_bytes=40 * 2**20),
        cost_estimate=pl.CostEstimate(
            flops=pairs * HEAD * 4, bytes_accessed=pairs * 4, transcendentals=pairs
        ),
    )(qt, kt, vt, segment[None, :], segment[:, None])


def unrotate(grad, cosine, sine):
    half = HEAD // 2
    first, second = grad[:half], grad[half:]
    return jnp.concatenate(
        [first * cosine + second * sine, second * cosine - first * sine], axis=0
    )


def attend_back_kernel(
    q_ref, k_ref, v_ref, o_ref, do_ref, p_ref, inv_ref, cosq_ref, sinq_ref, cos_ref, sin_ref,
    dq_ref, dk_ref, dv_ref, vrow, dk_acc, dv_acc,
):
    i = pl.program_id(1)
    group, qb = q_ref.shape[1], q_ref.shape[3]
    width = group * qb

    @pl.when(i == 0)
    def _():
        vrow[...] = v_ref[0].astype(F32).T.astype(BF16)
        dk_acc[...] = jnp.zeros_like(dk_acc)
        dv_acc[...] = jnp.zeros_like(dv_acc)

    def side(ref):
        return jnp.concatenate([ref[0, h].astype(F32) for h in range(group)], axis=1)

    do = side(do_ref) * inv_ref[0, 0]
    centre = jnp.sum(side(o_ref) * do, axis=0, keepdims=True)
    do_low = do.astype(BF16)
    do_rows = do.T.astype(BF16)
    q_rows = side(q_ref).T.astype(BF16)

    def step(j, acc):
        rows = pl.ds(pl.multiple_of(j * qb, qb), qb)
        p = p_ref[0, 0, rows, :]
        dp = dot(vrow[rows, :], do_low)
        ds = (p.astype(F32) * (dp - centre)).astype(BF16)
        dk_acc[rows, :] += dot(ds, q_rows)
        dv_acc[rows, :] += dot(p, do_rows)
        return acc + dot(k_ref[0, :, rows], ds)

    dq = lax.fori_loop(0, i + 1, step, jnp.zeros((HEAD, width), F32)) * HEAD**-0.5
    for h in range(group):
        part = dq[:, h * qb : (h + 1) * qb]
        dq_ref[0, h] = unrotate(part, cosq_ref[...], sinq_ref[...]).astype(BF16)

    @pl.when(i == pl.num_programs(1) - 1)
    def _():
        dk_ref[0] = unrotate(dk_acc[...].T, cos_ref[...], sin_ref[...]).astype(BF16)
        dv_ref[0] = dv_acc[...].T.astype(BF16)


def attend_back(qt, kt, vt, ot, dot_, p, inverse, cosine, sine):
    kv, group, _, total = qt.shape
    blocks = total // QB
    width = group * QB
    pairs = kv * group * total * total // 2
    q_spec = pl.BlockSpec((1, group, HEAD, QB), lambda b, i: (b, 0, 0, i))
    k_spec = pl.BlockSpec((1, HEAD, total), lambda b, i: (b, 0, 0))
    return pl.pallas_call(
        attend_back_kernel,
        grid=(kv, blocks),
        in_specs=[
            q_spec, k_spec, k_spec, q_spec, q_spec,
            pl.BlockSpec((1, 1, total, width), lambda b, i: (b, i, 0, 0)),
            pl.BlockSpec((1, 1, 1, width), lambda b, i: (b, i, 0, 0)),
            pl.BlockSpec((HEAD // 2, QB), lambda b, i: (0, i)),
            pl.BlockSpec((HEAD // 2, QB), lambda b, i: (0, i)),
            pl.BlockSpec((HEAD // 2, total), lambda b, i: (0, 0)),
            pl.BlockSpec((HEAD // 2, total), lambda b, i: (0, 0)),
        ],
        out_specs=[q_spec, k_spec, k_spec],
        out_shape=[
            jax.ShapeDtypeStruct(qt.shape, BF16),
            jax.ShapeDtypeStruct(kt.shape, BF16),
            jax.ShapeDtypeStruct(vt.shape, BF16),
        ],
        scratch_shapes=[
            pltpu.VMEM((total, HEAD), BF16),
            pltpu.VMEM((total, HEAD), F32),
            pltpu.VMEM((total, HEAD), F32),
        ],
        compiler_params=pltpu.CompilerParams(vmem_limit_bytes=40 * 2**20),
        cost_estimate=pl.CostEstimate(
            flops=pairs * HEAD * 8, bytes_accessed=pairs * 4, transcendentals=0
        ),
    )(qt, kt, vt, ot, dot_, p, inverse, cosine, sine, cosine, sine)


def pack_experts(gate_up, down):
    parts = [gate_up[..., :HIDDEN], gate_up[..., HIDDEN:]]
    parts += [down[..., m : m + HIDDEN] for m in range(0, MODEL_WIDTH, HIDDEN)]
    return jnp.concatenate(parts, axis=1)


def expert_kernel(
    first, last, shards_count, rows, hidden_rows, experts_all, place_ref, x_ref, dy_ref, gate_ref,
    small_ref, s_ref, gus_ref, dfat_ref, dfa_ref, dsf_ref, back_ref, *refs,
):
    refs = list(refs)
    carried = [] if first else [refs.pop(0) for _ in range(5)]
    shards = [refs.pop(0) for _ in range(shards_count)]
    outs = [refs.pop(0) for _ in range(5)]
    w_up, w_down, zbias, sbias, out_acc, row_acc, aux_acc, wi_acc, db_acc, sem = refs
    count = w_up.shape[0]
    tile = x_ref.shape[0]
    accs = (out_acc, row_acc, aux_acc, wi_acc, db_acc)

    @pl.when(pl.program_id(0) == 0)
    def _():
        copies = []
        for b, shard in enumerate(shards):
            index = place_ref[1 + b]
            up_rows = pl.ds(pl.multiple_of(index * rows, rows), rows)
            down_rows = pl.ds(pl.multiple_of(index * hidden_rows, hidden_rows), hidden_rows)
            for m in range(2):
                copies.append((shard.at[:, pl.ds(m * rows, rows), :],
                               w_up.at[:, up_rows, pl.ds(m * HIDDEN, HIDDEN)]))
            for m in range(MODEL_WIDTH // HIDDEN):
                copies.append((shard.at[:, pl.ds(2 * rows + m * hidden_rows, hidden_rows), :],
                               w_down.at[:, down_rows, pl.ds(m * HIDDEN, HIDDEN)]))
        copies = [pltpu.make_async_copy(a, b, sem.at[n]) for n, (a, b) in enumerate(copies)]
        for copy in copies:
            copy.start()
        for copy in copies:
            copy.wait()

    for n, acc in enumerate(accs):
        acc[...] = jnp.zeros_like(acc) if first else carried[n][...]
    zbias[...] = dot(small_ref[...], gus_ref[...])
    sbias[...] = dot(s_ref[...], dfat_ref[...])
    lane = lax.broadcasted_iota(jnp.int32, (tile, LANES), 1)

    def step(e, _):
        name = place_ref[0] + e
        x, dy = x_ref[...], dy_ref[...]
        both = dot(x, w_up[e]) + zbias[...]
        gate_in, up = both[:, :HIDDEN], both[:, HIDDEN:]
        sigma = jax.nn.sigmoid(gate_in)
        silu = gate_in * sigma
        inner = silu * up
        d_down = dot_nt(dy, w_down[e]) + sbias[...]
        d_gating = jnp.sum(inner * d_down, axis=1, keepdims=True)
        gating = jnp.sum(jnp.where(lane == name, gate_ref[...], 0.0), axis=1, keepdims=True)
        aux_acc[...] += jnp.where((lane == name) | (lane == name + experts_all), d_gating, 0.0)
        gated = gating * inner
        wi_acc[...] += gated
        out_acc[...] += dot(gated.astype(BF16), w_down[e])
        d_inner = gating * d_down
        d_gate = d_inner * up * sigma * (1.0 + gate_in * (1.0 - sigma))
        d_both = jnp.concatenate([d_gate, d_inner * silu], axis=1)
        db_acc[...] += d_both
        row_acc[...] += dot_nt(d_both.astype(BF16), w_up[e])
        return 0

    lax.fori_loop(0, count, step, 0)
    if not last:
        for out, acc in zip(outs, accs):
            out[...] = acc[...]
        return
    low_wi, low_db = wi_acc[...].astype(BF16), db_acc[...].astype(BF16)
    small_d = dot(low_wi, dfa_ref[...]).astype(BF16)
    outs[0][...] = (out_acc[...] + dot(small_d, dsf_ref[...])).astype(BF16)
    aux = aux_acc[...] + dot(low_db, back_ref[...])
    high = aux.astype(BF16)
    rest = (aux - high.astype(F32)).astype(BF16)
    is_rest = (lane >= experts_all) & (lane < 2 * experts_all)
    outs[1][:, :MODEL_WIDTH] = row_acc[...].astype(BF16)
    outs[1][:, MODEL_WIDTH:] = jnp.where(is_rest, rest, high)
    outs[2][...] = small_d
    outs[3][...] = low_wi
    outs[4][...] = low_db


def run_experts(place, x, dy, gates, small, s, mats, carried, shards, experts_all, last, tile):
    total = x.shape[0]
    count, packed_rows, _ = shards[0].shape
    rows = MODEL_WIDTH // len(shards)
    hidden_rows = HIDDEN // len(shards)
    first = carried is None
    widths = (MODEL_WIDTH, MODEL_WIDTH + LANES if last else MODEL_WIDTH, LANES, HIDDEN, 2 * HIDDEN)
    dtype = BF16 if last else F32

    def tiled(width):
        return pl.BlockSpec((tile, width), lambda t, _: (t, 0))

    def whole(shape):
        return pl.BlockSpec(shape, lambda t, _: (0, 0))

    in_widths = (MODEL_WIDTH, MODEL_WIDTH, LANES, LANES, LANES)
    acc_widths = (MODEL_WIDTH, MODEL_WIDTH, LANES, HIDDEN, 2 * HIDDEN)
    specs = [tiled(w) for w in in_widths] + [whole(m.shape) for m in mats]
    specs += [] if first else [tiled(w) for w in acc_widths]
    specs += [pl.BlockSpec(memory_space=pl.ANY)] * len(shards)
    copies = len(shards) * (2 + MODEL_WIDTH // HIDDEN)
    return pl.pallas_call(
        functools.partial(
            expert_kernel, first, last, len(shards), rows, hidden_rows, experts_all
        ),
        grid_spec=pltpu.PrefetchScalarGridSpec(
            num_scalar_prefetch=1,
            grid=(total // tile,),
            in_specs=specs,
            out_specs=[tiled(w) for w in widths],
            scratch_shapes=[
                pltpu.VMEM((count, MODEL_WIDTH, 2 * HIDDEN), BF16),
                pltpu.VMEM((count, HIDDEN, MODEL_WIDTH), BF16),
                pltpu.VMEM((tile, 2 * HIDDEN), F32),
                pltpu.VMEM((tile, HIDDEN), F32),
                *[pltpu.VMEM((tile, w), F32) for w in acc_widths],
                pltpu.SemaphoreType.DMA((copies,)),
            ],
        ),
        out_shape=[jax.ShapeDtypeStruct((total, w), dtype) for w in widths],
        compiler_params=pltpu.CompilerParams(vmem_limit_bytes=60 * 2**20),
        cost_estimate=pl.CostEstimate(
            flops=12 * total * MODEL_WIDTH * HIDDEN * count,
            bytes_accessed=total * MODEL_WIDTH * 10,
            transcendentals=total * HIDDEN * count,
        ),
    )(place, x, dy, gates, small, s, *mats, *(carried or ()), *shards)


def norm_backward(value_rows, inverse, gain_row, upstream):
    scaled = upstream * gain_row
    inner_mean = jnp.mean(value_rows * scaled, axis=-1, keepdims=True)
    return inverse * scaled - value_rows * (inverse * inverse * inverse) * inner_mean


def layout(lengths_row, prompt_len, total_len):
    ends = jnp.sum(jnp.tril(jnp.ones((lengths_row.shape[0],) * 2, jnp.int32)) * lengths_row, axis=1)
    starts = ends - lengths_row
    places = jnp.arange(total_len, dtype=jnp.int32)
    offset = places - prompt_len
    counted = jnp.sum((offset[:, None] >= ends[None, :]).astype(jnp.int32), axis=1)
    inside = offset >= 0
    segment = jnp.where(inside, counted, -1)
    picked = jnp.arange(lengths_row.shape[0], dtype=jnp.int32)[None, :] == counted[:, None]
    begin = jnp.sum(jnp.where(picked, starts[None, :], 0), axis=1)
    position = jnp.where(inside, prompt_len + offset - begin, places)
    return (segment, position)


def pad_lanes(x, at=0, width=LANES):
    return jnp.pad(x, ((0, 0), (at, width - at - x.shape[1])))


def stack_rows(grads):
    rows = []
    for grad in grads:
        for m in range(0, grad.shape[1], HIDDEN):
            rows.append(grad[:, m : m + HIDDEN])
    return jnp.concatenate(rows, axis=0)


def unstack_rows(flat, shapes):
    out, at = [], 0
    for height, width in shapes:
        parts = []
        for _ in range(width // HIDDEN):
            parts.append(flat[:, at : at + height])
            at += height
        out.append(jnp.concatenate(parts, axis=2) if len(parts) > 1 else parts[0])
    return out


def reduce_adapters(flat, n_seq, n_dp, n_wt, index_now):
    rows = flat.shape[0]
    mine = scatter_seq(flat.reshape(n_seq, rows // n_seq, HIDDEN), n_seq)
    tag = jnp.full((8, HIDDEN), index_now.astype(F32))
    everyone = lax.all_gather(jnp.concatenate([mine, tag], 0), ("dp", "wt"), axis=0)
    share = ADAPTER_COUNT // n_wt
    first_row = lax.axis_index("wt") * share
    names = everyone[:, -1, 0].astype(jnp.int32)
    picks = (names[None, :] == first_row + jnp.arange(share)[:, None]).astype(F32)
    kept = jnp.sum(picks[:, :, None, None] * everyone[None, :, :-8], axis=1)
    full = gather_seq(kept.reshape(share * (rows // n_seq), HIDDEN), n_seq)
    full = full.reshape(n_seq, share, rows // n_seq, HIDDEN)
    return jnp.swapaxes(full, 0, 1).reshape(share, rows, HIDDEN)


def shards(
    tokens,
    cotangent,
    routes,
    lengths,
    group_adapter_index,
    attention_norm_gain,
    query_weight,
    key_value_weight,
    output_weight,
    mixture_norm_gain,
    router_weight,
    expert_gate_up_weight,
    expert_down_weight,
    attention_first_factors,
    query_second_factor,
    key_value_second_factors,
    output_first_factor,
    output_second_factor,
    mixture_first_factors,
    router_second_factor,
    gate_up_second_factors,
    down_first_factor,
    down_second_factor,
):
    n_seq, n_dp, n_wt = (lax.axis_size(a) for a in ("seq", "dp", "wt"))
    seq, dp, wt = (lax.axis_index(a) for a in ("seq", "dp", "wt"))
    local = tokens.shape[1]
    total = local * n_seq
    prompt_len = max(PROMPT_LEAST, PROMPT_DEV * n_seq)
    exp_dev = expert_gate_up_weight.shape[0]
    experts_all = exp_dev * n_seq
    kv_local = KV_HEADS // n_seq
    group = HEADS // KV_HEADS
    q_width = MODEL_WIDTH // n_seq
    k_width = KEY_FEATURES // n_seq
    rank = ADAPTER_RANK
    index_now = group_adapter_index[0]

    def chosen(bank):
        return lax.dynamic_index_in_dim(bank, index_now, 0, keepdims=False)

    def own(x, size, axis=1, at=0):
        return lax.dynamic_slice_in_dim(x, at + seq * size, size, axis)

    attn_first = chosen(attention_first_factors)
    query_second = own(chosen(query_second_factor), q_width)
    kv_second = chosen(key_value_second_factors)
    out_first = chosen(output_first_factor)
    out_second = chosen(output_second_factor)
    mix_first = chosen(mixture_first_factors)
    router_second = chosen(router_second_factor)
    gate_up_second = chosen(gate_up_second_factors)
    down_first = chosen(down_first_factor)
    down_second = chosen(down_second_factor)

    bounds = [0]
    for size in CHUNKS:
        bounds.append(bounds[-1] + size)
    expert_shards = []
    for lo, hi in zip(bounds[:-1], bounds[1:]):
        packed = pack_experts(expert_gate_up_weight[lo:hi], expert_down_weight[lo:hi])
        column = [packed]
        for _ in range(1, n_wt):
            column.append(shift(column[-1], "wt", n_wt, 1))
        pieces = []
        for k in range(n_dp):
            pieces += [(k, b, shift(x, "dp", n_dp, k) if k else x) for b, x in enumerate(column)]
        expert_shards.append(pieces)
    order = [
        (dp + n_dp - k) % n_dp * n_wt + (wt + n_wt - b) % n_wt for k, b, _ in expert_shards[0]
    ]

    hidden = gather_seq(tokens[0], n_seq).reshape(total, MODEL_WIDTH)
    named = jnp.arange(LANES, dtype=jnp.int32)[None, None, :]
    mask = jnp.any(routes[0][:, :, None] == named, axis=1).astype(BF16)
    upstream_all = gather_seq(jnp.concatenate([cotangent[0], mask], axis=1), n_seq)
    upstream_all = upstream_all.reshape(total, MODEL_WIDTH + LANES)
    d_out_all = upstream_all[:, :MODEL_WIDTH]
    routed = upstream_all[:, MODEL_WIDTH : MODEL_WIDTH + experts_all] > 0.5

    mine = jnp.concatenate(
        [
            own(query_weight, q_width),
            own(key_value_weight, k_width),
            own(key_value_weight, k_width, at=KEY_FEATURES),
            pad_lanes(router_weight),
        ],
        axis=1,
    )
    gathered = lax.all_gather(mine, ("dp", "wt"), axis=0, tiled=True)
    qkv_width = q_width + 2 * k_width
    qkv_weight = gathered[:, :qkv_width]
    router_full = gathered[:, qkv_width : qkv_width + experts_all]
    half = MODEL_WIDTH // 2
    core = seq % 2
    out_mine = lax.all_gather(
        lax.dynamic_slice_in_dim(output_weight, core * half, half, 1), ("dp", "wt"), axis=0, tiled=True
    )
    out_other = swap_core(out_mine, n_seq)
    out_weight = jnp.where(
        core == 0,
        jnp.concatenate([out_mine, out_other], 1),
        jnp.concatenate([out_other, out_mine], 1),
    )

    gain_first = attention_norm_gain.astype(F32)
    gain_second = mixture_norm_gain.astype(F32)
    hidden_f = hidden.astype(F32)
    inverse_a = lax.rsqrt(jnp.mean(hidden_f * hidden_f, axis=-1, keepdims=True) + EPS)
    normed = (hidden_f * inverse_a * gain_first).astype(BF16)
    small_a = dot(normed, attn_first).astype(BF16)
    second = jnp.zeros((3 * rank, qkv_width), BF16)
    second = second.at[:rank, :q_width].set(query_second)
    second = second.at[rank : 2 * rank, q_width : q_width + k_width].set(own(kv_second[0], k_width))
    second = second.at[2 * rank :, q_width + k_width :].set(own(kv_second[1], k_width))
    qkv = dot(qkv_weight, normed, ((0,), (1,))) + dot(second, small_a, ((0,), (1,)))
    segment, position = layout(lengths[0], prompt_len, total)
    freq = jnp.exp(jnp.arange(HEAD // 2, dtype=F32) * (-2.0 * math.log(10000.0) / HEAD))
    angle = freq[:, None] * position.astype(F32)[None, :]
    cosine, sine = jnp.cos(angle), jnp.sin(angle)

    def rotate(x, scale=1.0):
        x = x.reshape(-1, 2, HEAD // 2, total)
        a, b = x[:, 0], x[:, 1]
        x = jnp.concatenate([a * cosine - b * sine, b * cosine + a * sine], axis=1)
        return (x.astype(BF16) * jnp.asarray(scale, BF16)).reshape(-1, HEAD, total)

    qt = rotate(qkv[:q_width], HEAD**-0.5).reshape(kv_local, group, HEAD, total)
    kt = rotate(qkv[q_width : q_width + k_width])
    vt = qkv[q_width + k_width :].astype(BF16).reshape(kv_local, HEAD, total)
    ot, probs, inverse_l = attend(qt, kt, vt, segment, prompt_len)
    att = gather_seq(ot.reshape(q_width, total), n_seq).reshape(MODEL_WIDTH, total)

    small_o = dot_tn(att, out_first).astype(BF16)
    residual = hidden_f + dot_tn(att, out_weight) + dot(small_o, out_second)
    inverse_m = lax.rsqrt(jnp.mean(residual * residual, axis=-1, keepdims=True) + EPS)
    normed_m = (residual * inverse_m * gain_second).astype(BF16)
    mix_router = jnp.concatenate([mix_first, router_full], axis=1)
    states = dot(normed_m, mix_router)
    small_m = states[:, : 3 * rank].astype(BF16)
    logits = states[:, 3 * rank :] + dot(small_m[:, :rank], router_second)
    logits = jnp.where(routed, logits, NEG)
    peak = jnp.max(logits, axis=-1, keepdims=True)
    weights = jnp.where(routed, jnp.exp(logits - peak), 0.0)
    gating = weights / jnp.sum(weights, axis=-1, keepdims=True)

    d_rank = dot_nt(d_out_all, down_second).astype(BF16)
    gus = jnp.zeros((LANES, 2 * HIDDEN), BF16)
    gus = gus.at[:rank, :HIDDEN].set(gate_up_second[0])
    gus = gus.at[rank : 2 * rank, HIDDEN:].set(gate_up_second[1])
    back = jnp.zeros((2 * HIDDEN, LANES), BF16)
    back = back.at[:, SMALL_AT : SMALL_AT + 2 * rank].set(gus[: 2 * rank].T)
    mats = (
        gus,
        jnp.pad(down_first.T, ((0, LANES - rank), (0, 0))),
        pad_lanes(down_first),
        jnp.pad(down_second, ((0, LANES - rank), (0, 0))),
        back,
    )
    gates = pad_lanes(gating)
    small_pad = pad_lanes(small_m[:, rank:])
    rank_pad = pad_lanes(d_rank)
    carried = None
    for n, pieces in enumerate(expert_shards):
        place = jnp.stack([(seq * exp_dev + bounds[n]).astype(jnp.int32)] + order)
        carried = run_experts(
            place.astype(jnp.int32), normed_m, d_out_all, gates, small_pad, rank_pad, mats, carried,
            [x for _, _, x in pieces], experts_all, n == len(expert_shards) - 1, 256,
        )
    part_out, part_back, small_d, weighted_inner, d_both = carried
    small_d = small_d[:, :rank]

    def own_rows(x):
        return lax.dynamic_slice_in_dim(x, seq * local, local, 0)

    back_sum = scatter_seq(part_back.reshape(n_seq, local, MODEL_WIDTH + LANES), n_seq)
    upstream = cotangent[0].astype(F32)
    residual_own = own_rows(residual)
    gating_own = own_rows(gating)
    small_m_own = own_rows(small_m)
    d_gating = (
        back_sum[:, MODEL_WIDTH : MODEL_WIDTH + experts_all]
        + back_sum[:, MODEL_WIDTH + experts_all : MODEL_WIDTH + 2 * experts_all]
    )
    d_logits = gating_own * (d_gating - jnp.sum(d_gating * gating_own, axis=-1, keepdims=True))
    d_logits_low = d_logits.astype(BF16)
    d_small_m = jnp.concatenate(
        [dot_nt(d_logits_low, router_second), back_sum[:, MODEL_WIDTH + SMALL_AT :]], axis=1
    ).astype(BF16)
    d_normed_m = back_sum[:, :MODEL_WIDTH] + dot_nt(
        jnp.concatenate([d_small_m, d_logits_low], axis=1), mix_router
    )
    d_residual = upstream + norm_backward(
        residual_own, own_rows(inverse_m), gain_second, d_normed_m
    )
    d_branch = d_residual.astype(BF16)
    d_small_o = dot_nt(d_branch, out_second).astype(BF16)
    d_att = (dot_nt(out_weight, d_branch) + dot_nt(out_first, d_small_o)).astype(BF16)
    d_att = lax.all_to_all(d_att, "seq", split_axis=0, concat_axis=1, tiled=True)
    dqt, dkt, dvt = attend_back(
        qt, kt, vt, ot, d_att.reshape(kv_local, group, HEAD, total), probs, inverse_l, cosine, sine
    )
    d_qkv = jnp.concatenate(
        [dqt.reshape(q_width, total), dkt.reshape(k_width, total), dvt.reshape(k_width, total)], 0
    )
    d_small_a = dot(d_qkv, second, ((0,), (1,))).astype(BF16)
    d_normed = dot(d_qkv, qkv_weight, ((0,), (1,))) + dot_nt(d_small_a, attn_first)
    d_normed = scatter_seq(d_normed.astype(BF16).reshape(n_seq, local, MODEL_WIDTH), n_seq)
    input_grad = d_residual + norm_backward(
        tokens[0].astype(F32), own_rows(inverse_a), gain_first, d_normed
    )
    output_rows = residual_own + scatter_seq(part_out.reshape(n_seq, local, MODEL_WIDTH), n_seq)

    grad_second = dot(small_a, d_qkv, ((0,), (1,)))

    def spread(x, width, full):
        return lax.dynamic_update_slice_in_dim(
            jnp.zeros((x.shape[0], full), F32), x, seq * width, 1
        )

    grad_q_b = spread(grad_second[:rank, :q_width], q_width, MODEL_WIDTH)
    grad_k_b = spread(grad_second[rank : 2 * rank, q_width : q_width + k_width], k_width, KEY_FEATURES)
    grad_v_b = spread(grad_second[2 * rank :, q_width + k_width :], k_width, KEY_FEATURES)
    grad_gu = dot_tn(small_m[:, rank:], d_both)
    att_own = lax.dynamic_slice_in_dim(att, seq * local, local, 1)
    grads = [
        dot_tn(d_small_a, normed),
        grad_q_b,
        grad_k_b,
        grad_v_b,
        dot(d_small_o, att_own, ((0,), (1,))),
        dot_tn(own_rows(small_o), d_branch),
        dot_tn(d_small_m, own_rows(normed_m)),
        pad_lanes(dot_tn(small_m_own[:, :rank], d_logits_low), width=HIDDEN),
        grad_gu[:rank, :HIDDEN],
        grad_gu[rank:, HIDDEN:],
        dot_tn(d_rank, weighted_inner),
        dot_tn(small_d, d_out_all),
    ]
    flat = reduce_adapters(stack_rows(grads), n_seq, n_dp, n_wt, index_now)
    attn_a, q_b, k_b, v_b, o_a, o_b, moe_a, r_b, gate_b, up_b, down_a, down_b = unstack_rows(
        flat, [g.shape for g in grads]
    )

    def flip(x):
        return jnp.swapaxes(x, 1, 2)

    return (
        output_rows[None].astype(BF16),
        input_grad[None],
        flip(attn_a),
        q_b,
        jnp.stack([k_b, v_b], axis=1),
        flip(o_a),
        o_b,
        flip(moe_a),
        r_b[:, :, :experts_all],
        jnp.stack([gate_b, up_b], axis=1),
        flip(down_a),
        down_b,
    )


def solution(mesh):
    split = P(("dp", "wt"), "seq", None)
    rows = P(("dp", "wt"), None)
    bank = P("wt", None, None)
    placed = (
        split, split, split, rows, P(("dp", "wt")), P(), rows, rows, rows, P(), rows,
        P("seq", ("dp", "wt"), None), P("seq", ("dp", "wt"), None),
    ) + (P(),) * 10
    wide = P("wt", None, None, None)
    return jax.shard_map(
        shards,
        mesh=mesh,
        in_specs=placed,
        out_specs=(split, split, bank, bank, wide, bank, bank, bank, bank, wide, bank, bank),
        check_vma=False,
    )
```

time: 1940 us -> 738 us (0.38)
  waiting for transfers between devices: 791 us -> 273 us
  matrix products: 377 us -> 88.8 us
  local copies, waits for them, and re-layouts: 323 us -> 104 us
  blocking collectives: 206 us -> 0 us
  Pallas kernels: 0 us -> 162 us
  other arithmetic: 156 us -> 58.2 us
  starting transfers between devices: 60.5 us -> 24.8 us
    all_to_all x13 -> x1, waiting for transfers between devices: 485 us -> 2.6 us  [shards(): lax.all_to_all(d_att, 'seq', split_axis=0, concat_axis=1, tiled=True)]
    dot_general x74 -> x26, matrix products: 377 us -> 88.8 us  [dot(): return lax.dot_general(a, b, (dims, ((), ())), preferred_element_type=F32)]
    ppermute x0 -> x32, waiting for transfers between devices: none -> 261 us  [the longest x7 151 us: shift(): return lax.ppermute(x, axis, [(i, (i + k) % count) for i in range(count)])]
    pallas_call x0 -> x3, Pallas kernels: none -> 162 us  [the longest x1 107 us: run_experts(): pl.pallas_call(functools.partial(expert_kernel, first, last, len(shards),...]
    all_gather x5 -> x3, waiting for transfers between devices: 168 us -> 9.24 us  [the longest x1 9.21 us: reduce_adapters(): lax.all_gather(jnp.concatenate([mine, tag], 0), ('dp', 'wt'), axis=0)]
    all_to_all x1 -> x0, blocking collectives: 134 us -> none  [shards(): lax.all_to_all(grad_send, 'seq', split_axis=0, concat_axis=1, tiled=True)]
    psum x1 -> x0, waiting for transfers between devices: 134 us -> none  [shards(): lax.psum((spread(grad_qkv_a), spread(grad_q_b), spread(grad_kv_b), spread...]
    gather x5 -> x0, local copies, waits for them, and re-layouts: 82.9 us -> none  [the longest x1 25.2 us: shards(): back_rows.reshape(experts_all * capacity, MODEL_WIDTH)[slots]]
  transfers between devices with their start and end apart: 19 -> 36, of which waited for: 13 -> 17; matrix products, arithmetic and copies ran while one was open for 18% -> 26% of each run, Pallas kernels for 0% -> 4%
where the time goes in v1:
time: 738 us; the launch traced here: 727 us
  waiting for transfers between devices  273 us (37%)
  Pallas kernels  162 us (22%)
  local copies, waits for them, and re-layouts  104 us (14%)
  matrix products  88.8 us (12%)
  other arithmetic  58.2 us (8%)
  starting transfers between devices  24.8 us (3%)
  between operations  16.2 us (2%)
    ppermute x7, waiting for transfers between devices, shift(): return lax.ppermute(x, axis, [(i, (i + k) % count) for i in range(count)])  151 us
    pallas_call x1, Pallas kernels, run_experts(): pl.pallas_call(functools.partial(expert_kernel, first, last, len(shards),...  107 us
    ppermute x8, waiting for transfers between devices, shift_chip(): return lax.ppermute(x, 'seq', pairs)  104 us
    dot_general x26, matrix products, dot(): return lax.dot_general(a, b, (dims, ((), ())), preferred_element_type=F32)  88.8 us
    pallas_call x1, Pallas kernels, attend_back(): pl.pallas_call(attend_back_kernel, grid=(kv, blocks), in_specs=[q_spec, k...  29 us
    pallas_call x1, Pallas kernels, attend(): pl.pallas_call(functools.partial(attend_kernel, prompt_len // QB), grid=(...  26.1 us
    dynamic_update_slice x15, local copies, waits for them, and re-layouts, gather_seq(): out = lax.dynamic_update_slice_in_dim(out, piece[None], at, 0)  20 us
    unnamed x174, local copies, waits for them, and re-layouts  19.6 us
  transfers between devices with their start and end apart: 36, of which 17 were waited for; matrix products, arithmetic and copies ran while one was open for 26% of the time, Pallas kernels for 4%

profile of v1, /device:TPU:0, one launch (start us, length us, event | category | flops | bytes accessed | tf_op | source)
XLA Modules:
  0.0 727.2 jit_solution(12070878619190477385)
XLA Ops:
  62.2 6.0 collective-permute-done.8
  71.0 4.2 fusion
  75.8 3.5 fusion.2
  80.8 3.5 fusion.113
  84.3 5.6 fusion.4
  90.0 37.6 %collective-permute-done.10.refs_1_ = bf16[5,576,512]{2,1,0:T(8,128)(2,1)} collective-permute-done((bf16[5,576,512]{2,1,0:T(8,128)(2,1)}, bf16[5,576,512]{2,1,0:T(8,128)(2,1)}, u32[]{:S(2)}, u32[]{:S(2)}) %collective-permute-start.10) | collective-permute-done | bytes 2949152 | tf_op jit(solution)/shard_map/ppermute | solution.py:90
  127.8 7.4 %convolution_add_fusion.1 = f32[640,1536]{1,0:T(8,128)S(1)} fusion(f32[640,1536]{1,0:T(8,128)} %fusion.113, bf16[1536,1536]{1,0:T(8,128)(2,1)} %fusion.4, bf16[1536,768]{1,0:T(8,128)(2,1)} %all-gather.5.cloned.1.call-done), kind=kOutput, calls=%fused_computation.16 | convolution fusion | flops 3020881920 | bytes 14548992 | tf_op jit(solution)/shard_map/dot_general | solution.py:33
  140.8 26.1 %shard_map.310 = (bf16[2,3,64,1536]{3,2,1,0:T(8,128)(2,1)S(1)}, bf16[2,6,1536,768]{3,2,1,0:T(8,128)(2,1)}, f32[2,6,1,768]{3,2,1,0:T(1,128)S(1)}) custom-call(bf16[2,3,64,1536]{3,2,1,0:T(8,128)(2,1)S(1)} %maximum_multiply_fusion.q_ref, bf16[2,64,1536]{2,1,0:T(8,128)(2,1)S(1)} %pad_maximum_fusion.2.k_ref, bf16[2,64,1536]{2,1,0:T(8,128)(2,1)S(1)} %bitcast.263, ...), custom_call_target="tpu_custom_call" | custom-call | flops 1811939328 | bytes 28311552 | tf_op jit(solution)/shard_map/pallas_call | solution.py:153
  178.9 15.9 %collective-permute-done.4 = bf16[384,1536]{1,0:T(8,128)(2,1)} collective-permute-done((bf16[384,1536]{1,0:T(8,128)(2,1)S(1)}, bf16[384,1536]{1,0:T(8,128)(2,1)}, u32[]{:S(2)}, u32[]{:S(2)}) %collective-permute-start.4) | collective-permute-done | bytes 1179680 | tf_op jit(solution)/shard_map/ppermute | solution.py:51
  207.3 4.8 collective-permute-done.11.refs_2_
  219.5 5.9 fusion.59
  225.4 21.2 %multiply_reduce_fusion = (f32[1536]{0:T(1024)S(1)}, f32[1536,1536]{1,0:T(8,128)}) fusion(f32[1536,1536]{1,0:T(8,128)} %fusion.59, bf16[1536,1536]{1,0:T(8,128)(2,1)} %bitcast.26, bf16[1536,768]{1,0:T(8,128)(2,1)} %collective-permute-done.6, bf16[1536,768]{1,0:T(8,128)(2,1)} %all-gather.7.cloned.1.call-done, pred[]{:T(512)S(6)} %eq.125, ...), kind=kOutput, calls=%fused_computation.12 | convolution fusion | flops 7280785920 | bytes 33036288 | tf_op jit(solution)/shard_map/dot_general | solution.py:33
  246.6 33.5 %collective-permute-done.12.refs_3_ = bf16[5,576,512]{2,1,0:T(8,128)(2,1)S(1)} collective-permute-done((bf16[5,576,512]{2,1,0:T(8,128)(2,1)}, bf16[5,576,512]{2,1,0:T(8,128)(2,1)S(1)}, u32[]{:S(2)}, u32[]{:S(2)}) %collective-permute-start.12) | collective-permute-done | bytes 2949152 | tf_op jit(solution)/shard_map/ppermute | solution.py:90
  281.5 4.6 multiply_convert_fusion.x_ref
  295.1 12.6 %collective-permute-done.15.refs_6_ = bf16[5,576,512]{2,1,0:T(8,128)(2,1)} collective-permute-done((bf16[5,576,512]{2,1,0:T(8,128)(2,1)}, bf16[5,576,512]{2,1,0:T(8,128)(2,1)}, u32[]{:S(2)}, u32[]{:S(2)}) %collective-permute-start.15) | collective-permute-done | bytes 2949152 | tf_op jit(solution)/shard_map/ppermute | solution.py:90
  307.7 62.8 %collective-permute-done.16.refs_7_ = bf16[5,576,512]{2,1,0:T(8,128)(2,1)} collective-permute-done((bf16[5,576,512]{2,1,0:T(8,128)(2,1)S(1)}, bf16[5,576,512]{2,1,0:T(8,128)(2,1)}, u32[]{:S(2)}, u32[]{:S(2)}) %collective-permute-start.16) | collective-permute-done | bytes 2949152 | tf_op jit(solution)/shard_map/ppermute | solution.py:90
  370.5 107.0 %shard_map.311 = (bf16[1536,1536]{1,0:T(8,128)(2,1)}, bf16[1536,1664]{1,0:T(8,128)(2,1)}, bf16[1536,128]{1,0:T(8,128)(2,1)}, bf16[1536,512]{1,0:T(8,128)(2,1)}, bf16[1536,1024]{1,0:T(8,128)(2,1)}) custom-call(s32[9]{0:T(128)} %stack.57.place_ref, bf16[1536,1536]{1,0:T(8,128)(2,1)} %copy-done.18, bf16[1536,1536]{1,0:T(8,128)(2,1)} %slice.465.dy_ref, ...), custom_call_target="tpu_custom_call" | custom-call | flops 72477573120 | bytes 23592960 | tf_op jit(solution)/shard_map/pallas_call | solution.py:375
  489.0 3.9 fusion.41
  497.3 21.4 %collective-permute-done.21 = bf16[384,1664]{1,0:T(8,128)(2,1)} collective-permute-done((bf16[384,1664]{1,0:T(8,128)(2,1)}, bf16[384,1664]{1,0:T(8,128)(2,1)}, u32[]{:S(2)}, u32[]{:S(2)}) %collective-permute-start.21) | collective-permute-done | bytes 1277984 | tf_op jit(solution)/shard_map/ppermute | solution.py:51
  526.4 3.4 multiply_reduce_fusion.2
  529.8 13.8 %collective-permute-done.18 = bf16[384,1536]{1,0:T(8,128)(2,1)} collective-permute-done((bf16[384,1536]{1,0:T(8,128)(2,1)}, bf16[384,1536]{1,0:T(8,128)(2,1)}, u32[]{:S(2)}, u32[]{:S(2)}) %collective-permute-start.18) | collective-permute-done | bytes 1179680 | tf_op jit(solution)/shard_map/ppermute | solution.py:51
  543.6 4.8 subtract_add_fusion
  551.4 6.0 fusion.7
  557.4 4.5 all-to-all-start
  562.0 3.5 fusion.103
  587.5 29.0 %shard_map.312 = (bf16[2,3,64,1536]{3,2,1,0:T(8,128)(2,1)S(1)}, bf16[2,64,1536]{2,1,0:T(8,128)(2,1)S(1)}, bf16[2,64,1536]{2,1,0:T(8,128)(2,1)S(1)}) custom-call(bf16[2,3,64,1536]{3,2,1,0:T(8,128)(2,1)S(1)} %copy-done.2, bf16[2,64,1536]{2,1,0:T(8,128)(2,1)S(1)} %pad_maximum_fusion.2.k_ref, bf16[2,64,1536]{2,1,0:T(8,128)(2,1)S(1)} %bitcast.264, ...), custom_call_target="tpu_custom_call" | custom-call | flops 3623878656 | bytes 28311552 | tf_op jit(solution)/shard_map/pallas_call | solution.py:239
  628.3 9.0 %collective-permute-done.27 = f32[144,512]{1,0:T(8,128)} collective-permute-done((f32[144,512]{1,0:T(8,128)}, f32[144,512]{1,0:T(8,128)}, u32[]{:S(2)}, u32[]{:S(2)}) %collective-permute-start.27) | collective-permute-done | bytes 294944 | tf_op jit(solution)/shard_map/ppermute | solution.py:51
  639.3 5.5 fusion.24
  653.6 27.4 %collective-permute-done.24 = bf16[384,1536]{1,0:T(8,128)(2,1)} collective-permute-done((bf16[384,1536]{1,0:T(8,128)(2,1)}, bf16[384,1536]{1,0:T(8,128)(2,1)}, u32[]{:S(2)}, u32[]{:S(2)}) %collective-permute-start.24) | collective-permute-done | bytes 1179680 | tf_op jit(solution)/shard_map/ppermute | solution.py:51
  683.9 9.2 %all-gather.9.cloned.1.call-done = f32[1216,512]{1,0:T(8,128)} async-done(((f32[152,512]{1,0:T(8,128)}), f32[1216,512]{1,0:T(8,128)}) %all-gather.9.cloned.1.call-update) | async-done | bytes 2490384 | tf_op jit(solution)/shard_map/all_gather | solution.py:450
  698.4 4.0 fusion.14
  702.4 10.2 %collective-permute-done.30 = f32[288,512]{1,0:T(8,128)S(1)} collective-permute-done((f32[288,512]{1,0:T(8,128)S(1)}, f32[288,512]{1,0:T(8,128)S(1)}, u32[]{:S(2)}, u32[]{:S(2)}) %collective-permute-start.30) | collective-permute-done | bytes 589856 | tf_op jit(solution)/shard_map/ppermute | solution.py:51
  (378 shorter events, 193.4 us)
Async XLA Ops:
  7.2 120.6 %all-gather.5.cloned.1.call-start = ((), (), s32[]{:S(2)}) async-start(), calls=%async_computation.1 | async-start | bytes 2654208 | tf_op jit(solution)/shard_map/all_gather | solution.py:551
  10.8 191.3 %all-gather.7.cloned.1.call-start = ((), (), s32[]{:S(2)}) async-start(), calls=%async_computation.2 | async-start | bytes 2654208 | tf_op jit(solution)/shard_map/all_gather | solution.py:557
  10.8 45.1 %collective-permute-start = (bf16[384,1536]{1,0:T(8,128)(2,1)}, bf16[384,1536]{1,0:T(8,128)(2,1)}, u32[]{:S(2)}, u32[]{:S(2)}) collective-permute-start(bf16[384,1536]{1,0:T(8,128)(2,1)} %bitcast.289), channel_id=1, source_target_pairs={{0,4},{4,0},{8,12},{12,8},{1,5},{5,1},{9,13},{13,9},{2,6},{6,2},{1... | collective-permute-start | bytes 3538952 | tf_op jit(solution)/shard_map/ppermute | solution.py:45
  11.4 46.1 %collective-permute-start.1 = (bf16[384,1536]{1,0:T(8,128)(2,1)}, bf16[384,1536]{1,0:T(8,128)(2,1)}, u32[]{:S(2)}, u32[]{:S(2)}) collective-permute-start(bf16[384,1536]{1,0:T(8,128)(2,1)} %bitcast.290), channel_id=1, source_target_pairs={{0,8},{4,12},{8,0},{12,4},{1,9},{5,13},{9,1},{13,5},{2,10},{6,14},... | collective-permute-start | bytes 3538952 | tf_op jit(solution)/shard_map/ppermute | solution.py:51
  18.1 50.2 %collective-permute-start.7 = (bf16[384,1664]{1,0:T(8,128)(2,1)}, bf16[384,1664]{1,0:T(8,128)(2,1)}, u32[]{:S(2)}, u32[]{:S(2)}) collective-permute-start(bf16[384,1664]{1,0:T(8,128)(2,1)} %pad_maximum_fusion.1), channel_id=1, source_target_pairs={{0,4},{4,0},{8,12},{12,8},{1,5},{5,1},{9,13},{13,9},{2,6},{6,2},{1... | collective-permute-start | bytes 3833864 | tf_op jit(solution)/shard_map/ppermute | solution.py:45
  18.2 50.0 %collective-permute-start.8 = (bf16[384,1664]{1,0:T(8,128)(2,1)}, bf16[384,1664]{1,0:T(8,128)(2,1)}, u32[]{:S(2)}, u32[]{:S(2)}) collective-permute-start(bf16[384,1664]{1,0:T(8,128)(2,1)} %pad_maximum_fusion.1), channel_id=1, source_target_pairs={{0,8},{4,12},{8,0},{12,4},{1,9},{5,13},{9,1},{13,5},{2,10},{6,14},... | collective-permute-start | bytes 3833864 | tf_op jit(solution)/shard_map/ppermute | solution.py:51
  23.0 104.6 %collective-permute-start.10 = (bf16[5,576,512]{2,1,0:T(8,128)(2,1)}, bf16[5,576,512]{2,1,0:T(8,128)(2,1)}, u32[]{:S(2)}, u32[]{:S(2)}) collective-permute-start(bf16[5,576,512]{2,1,0:T(8,128)(2,1)} %slice_dynamic-update-slice_fusion.2.refs_0_), channel_id=1, source_target_pairs={{0,1},{1,2},{2,3},{3,0},{4,5},{5,6},{6,7},{7,4},{8,9},{9,10},{10,1... | collective-permute-start | bytes 8847368 | tf_op jit(solution)/shard_map/ppermute | solution.py:90
  56.0 239.1 %collective-permute-start.13 = (bf16[5,576,512]{2,1,0:T(8,128)(2,1)}, bf16[5,576,512]{2,1,0:T(8,128)(2,1)}, u32[]{:S(2)}, u32[]{:S(2)}) collective-permute-start(bf16[5,576,512]{2,1,0:T(8,128)(2,1)} %slice_dynamic-update-slice_fusion.2.refs_0_), channel_id=1, source_target_pairs={{0,16},{16,0},{1,17},{17,1},{2,18},{18,2},{3,19},{19,3},{4,20},{20... | collective-permute-start | bytes 8847368 | tf_op jit(solution)/shard_map/ppermute | solution.py:90
  57.5 12.2 %collective-permute-start.2 = (bf16[384,1536]{1,0:T(8,128)(2,1)}, bf16[384,1536]{1,0:T(8,128)(2,1)S(1)}, u32[]{:S(2)}, u32[]{:S(2)}) collective-permute-start(bf16[384,1536]{1,0:T(8,128)(2,1)} %collective-permute-done.1), channel_id=1, source_target_pairs={{0,4},{4,0},{8,12},{12,8},{1,5},{5,1},{9,13},{13,9},{2,6},{6,2},{1... | collective-permute-start | bytes 3538952 | tf_op jit(solution)/shard_map/ppermute | solution.py:45
  68.2 101.8 %collective-permute-start.9 = (bf16[384,1664]{1,0:T(8,128)(2,1)}, bf16[384,1664]{1,0:T(8,128)(2,1)}, u32[]{:S(2)}, u32[]{:S(2)}) collective-permute-start(bf16[384,1664]{1,0:T(8,128)(2,1)} %collective-permute-done.8), channel_id=1, source_target_pairs={{0,4},{4,0},{8,12},{12,8},{1,5},{5,1},{9,13},{13,9},{2,6},{6,2},{1... | collective-permute-start | bytes 3833864 | tf_op jit(solution)/shard_map/ppermute | solution.py:45
  127.6 84.6 %collective-permute-start.11 = (bf16[5,576,512]{2,1,0:T(8,128)(2,1)}, bf16[5,576,512]{2,1,0:T(8,128)(2,1)}, u32[]{:S(2)}, u32[]{:S(2)}) collective-permute-start(bf16[5,576,512]{2,1,0:T(8,128)(2,1)} %collective-permute-done.10.refs_1_), channel_id=1, source_target_pairs={{0,1},{1,2},{2,3},{3,0},{4,5},{5,6},{6,7},{7,4},{8,9},{9,10},{10,1... | collective-permute-start | bytes 8847368 | tf_op jit(solution)/shard_map/ppermute | solution.py:90
  167.0 27.9 %collective-permute-start.4 = (bf16[384,1536]{1,0:T(8,128)(2,1)S(1)}, bf16[384,1536]{1,0:T(8,128)(2,1)}, u32[]{:S(2)}, u32[]{:S(2)}) collective-permute-start(bf16[384,1536]{1,0:T(8,128)(2,1)S(1)} %bitcast.260), channel_id=1, source_target_pairs={{0,8},{4,12},{8,0},{12,4},{1,9},{5,13},{9,1},{13,5},{2,10},{6,14},... | collective-permute-start | bytes 3538952 | tf_op jit(solution)/shard_map/ppermute | solution.py:51
  170.0 32.2 %collective-permute-start.3 = (bf16[384,1536]{1,0:T(8,128)(2,1)S(1)}, bf16[384,1536]{1,0:T(8,128)(2,1)}, u32[]{:S(2)}, u32[]{:S(2)}) collective-permute-start(bf16[384,1536]{1,0:T(8,128)(2,1)S(1)} %bitcast.261), channel_id=1, source_target_pairs={{0,4},{4,0},{8,12},{12,8},{1,5},{5,1},{9,13},{13,9},{2,6},{6,2},{1... | collective-permute-start | bytes 3538952 | tf_op jit(solution)/shard_map/ppermute | solution.py:45
  177.5 117.6 %collective-permute-start.14 = (bf16[5,576,512]{2,1,0:T(8,128)(2,1)}, bf16[5,576,512]{2,1,0:T(8,128)(2,1)}, u32[]{:S(2)}, u32[]{:S(2)}) collective-permute-start(bf16[5,576,512]{2,1,0:T(8,128)(2,1)} %collective-permute-done.10.refs_1_), channel_id=1, source_target_pairs={{0,16},{16,0},{1,17},{17,1},{2,18},{18,2},{3,19},{19,3},{4,20},{20... | collective-permute-start | bytes 8847368 | tf_op jit(solution)/shard_map/ppermute | solution.py:90
  194.8 17.7 %collective-permute-start.5 = (bf16[384,1536]{1,0:T(8,128)(2,1)}, bf16[384,1536]{1,0:T(8,128)(2,1)}, u32[]{:S(2)}, u32[]{:S(2)}) collective-permute-start(bf16[384,1536]{1,0:T(8,128)(2,1)} %collective-permute-done.4), channel_id=1, source_target_pairs={{0,4},{4,0},{8,12},{12,8},{1,5},{5,1},{9,13},{13,9},{2,6},{6,2},{1... | collective-permute-start | bytes 3538952 | tf_op jit(solution)/shard_map/ppermute | solution.py:45
  202.1 23.3 %collective-permute-start.6 = (bf16[1536,768]{1,0:T(8,128)(2,1)}, bf16[1536,768]{1,0:T(8,128)(2,1)}, u32[]{:S(2)}, u32[]{:S(2)}) collective-permute-start(bf16[1536,768]{1,0:T(8,128)(2,1)} %all-gather.7.cloned.1.call-done), channel_id=1, source_target_pairs={{0,4},{4,0},{8,12},{12,8},{1,5},{5,1},{9,13},{13,9},{2,6},{6,2},{1... | collective-permute-start | bytes 7077896 | tf_op jit(solution)/shard_map/ppermute | solution.py:45
  212.1 67.9 %collective-permute-start.12 = (bf16[5,576,512]{2,1,0:T(8,128)(2,1)}, bf16[5,576,512]{2,1,0:T(8,128)(2,1)S(1)}, u32[]{:S(2)}, u32[]{:S(2)}) collective-permute-start(bf16[5,576,512]{2,1,0:T(8,128)(2,1)} %collective-permute-done.11.refs_2_), channel_id=1, source_target_pairs={{0,1},{1,2},{2,3},{3,0},{4,5},{5,6},{6,7},{7,4},{8,9},{9,10},{10,1... | collective-permute-start | bytes 8847368 | tf_op jit(solution)/shard_map/ppermute | solution.py:90
  212.5 95.1 %collective-permute-start.15 = (bf16[5,576,512]{2,1,0:T(8,128)(2,1)}, bf16[5,576,512]{2,1,0:T(8,128)(2,1)}, u32[]{:S(2)}, u32[]{:S(2)}) collective-permute-start(bf16[5,576,512]{2,1,0:T(8,128)(2,1)} %collective-permute-done.11.refs_2_), channel_id=1, source_target_pairs={{0,16},{16,0},{1,17},{17,1},{2,18},{18,2},{3,19},{19,3},{4,20},{20... | collective-permute-start | bytes 8847368 | tf_op jit(solution)/shard_map/ppermute | solution.py:90
  280.1 90.4 %collective-permute-start.16 = (bf16[5,576,512]{2,1,0:T(8,128)(2,1)S(1)}, bf16[5,576,512]{2,1,0:T(8,128)(2,1)}, u32[]{:S(2)}, u32[]{:S(2)}) collective-permute-start(bf16[5,576,512]{2,1,0:T(8,128)(2,1)S(1)} %collective-permute-done.12.refs_3_), channel_id=1, source_target_pairs={{0,16},{16,0},{1,17},{17,1},{2,18},{18,2},{3,19},{19,3},{4,20},{20... | collective-permute-start | bytes 8847368 | tf_op jit(solution)/shard_map/ppermute | solution.py:90
  480.8 16.5 %collective-permute-start.22 = (bf16[384,1664]{1,0:T(8,128)(2,1)}, bf16[384,1664]{1,0:T(8,128)(2,1)}, u32[]{:S(2)}, u32[]{:S(2)}) collective-permute-start(bf16[384,1664]{1,0:T(8,128)(2,1)} %get-tuple-element.183), channel_id=1, source_target_pairs={{0,4},{4,0},{8,12},{12,8},{1,5},{5,1},{9,13},{13,9},{2,6},{6,2},{1... | collective-permute-start | bytes 3833864 | tf_op jit(solution)/shard_map/ppermute | solution.py:45
  484.5 8.3 %collective-permute-start.17 = (bf16[384,1536]{1,0:T(8,128)(2,1)}, bf16[384,1536]{1,0:T(8,128)(2,1)}, u32[]{:S(2)}, u32[]{:S(2)}) collective-permute-start(bf16[384,1536]{1,0:T(8,128)(2,1)} %get-tuple-element.186), channel_id=1, source_target_pairs={{0,4},{4,0},{8,12},{12,8},{1,5},{5,1},{9,13},{13,9},{2,6},{6,2},{1... | collective-permute-start | bytes 3538952 | tf_op jit(solution)/shard_map/ppermute | solution.py:45
  487.5 31.2 %collective-permute-start.21 = (bf16[384,1664]{1,0:T(8,128)(2,1)}, bf16[384,1664]{1,0:T(8,128)(2,1)}, u32[]{:S(2)}, u32[]{:S(2)}) collective-permute-start(bf16[384,1664]{1,0:T(8,128)(2,1)} %fusion.9), channel_id=1, source_target_pairs={{0,8},{4,12},{8,0},{12,4},{1,9},{5,13},{9,1},{13,5},{2,10},{6,14},... | collective-permute-start | bytes 3833864 | tf_op jit(solution)/shard_map/ppermute | solution.py:51
  488.7 41.1 %collective-permute-start.19 = (bf16[384,1536]{1,0:T(8,128)(2,1)}, bf16[384,1536]{1,0:T(8,128)(2,1)}, u32[]{:S(2)}, u32[]{:S(2)}) collective-permute-start(bf16[384,1536]{1,0:T(8,128)(2,1)} %get-tuple-element.187), channel_id=1, source_target_pairs={{0,4},{4,0},{8,12},{12,8},{1,5},{5,1},{9,13},{13,9},{2,6},{6,2},{1... | collective-permute-start | bytes 3538952 | tf_op jit(solution)/shard_map/ppermute | solution.py:45
  495.7 47.9 %collective-permute-start.18 = (bf16[384,1536]{1,0:T(8,128)(2,1)}, bf16[384,1536]{1,0:T(8,128)(2,1)}, u32[]{:S(2)}, u32[]{:S(2)}) collective-permute-start(bf16[384,1536]{1,0:T(8,128)(2,1)} %fusion.23), channel_id=1, source_target_pairs={{0,8},{4,12},{8,0},{12,4},{1,9},{5,13},{9,1},{13,5},{2,10},{6,14},... | collective-permute-start | bytes 3538952 | tf_op jit(solution)/shard_map/ppermute | solution.py:51
  557.4 20.4 %all-to-all-start = ((bf16[4,384,384]{2,1,0:T(8,128)(2,1)}), bf16[4,384,384]{2,1,0:T(8,128)(2,1)}, u32[]{:S(2)}, u32[]{:S(2)}) async-start(bf16[4,384,384]{2,1,0:T(8,128)(2,1)} %bitcast.314), calls=%async_computation | async-start | bytes 2359296 | tf_op jit(solution)/shard_map/all_to_all | solution.py:660
  561.9 131.2 %all-gather.9.cloned.1.call-start = ((), (), s32[]{:S(2)}) async-start(), calls=%async_computation.3 | async-start | bytes 2801664 | tf_op jit(solution)/shard_map/all_gather | solution.py:450
  627.9 9.4 %collective-permute-start.27 = (f32[144,512]{1,0:T(8,128)}, f32[144,512]{1,0:T(8,128)}, u32[]{:S(2)}, u32[]{:S(2)}) collective-permute-start(f32[144,512]{1,0:T(8,128)} %bitcast_add_fusion.2), channel_id=1, source_target_pairs={{0,8},{4,12},{8,0},{12,4},{1,9},{5,13},{9,1},{13,5},{2,10},{6,14},... | collective-permute-start | bytes 884744 | tf_op jit(solution)/shard_map/ppermute | solution.py:51
  647.5 3.8 collective-permute-start.23
  647.5 6.0 collective-permute-start.25
  652.6 28.3 %collective-permute-start.24 = (bf16[384,1536]{1,0:T(8,128)(2,1)}, bf16[384,1536]{1,0:T(8,128)(2,1)}, u32[]{:S(2)}, u32[]{:S(2)}) collective-permute-start(bf16[384,1536]{1,0:T(8,128)(2,1)} %fusion.19), channel_id=1, source_target_pairs={{0,8},{4,12},{8,0},{12,4},{1,9},{5,13},{9,1},{13,5},{2,10},{6,14},... | collective-permute-start | bytes 3538952 | tf_op jit(solution)/shard_map/ppermute | solution.py:51
  696.8 16.2 %collective-permute-start.29 = (f32[288,512]{1,0:T(8,128)S(1)}, f32[288,512]{1,0:T(8,128)S(1)}, u32[]{:S(2)}, u32[]{:S(2)}) collective-permute-start(f32[288,512]{1,0:T(8,128)S(1)} %bitcast.306), channel_id=1, source_target_pairs={{0,4},{4,0},{8,12},{12,8},{1,5},{5,1},{9,13},{13,9},{2,6},{6,2},{1... | collective-permute-start | bytes 1769480 | tf_op jit(solution)/shard_map/ppermute | solution.py:45
  696.8 15.7 %collective-permute-start.30 = (f32[288,512]{1,0:T(8,128)S(1)}, f32[288,512]{1,0:T(8,128)S(1)}, u32[]{:S(2)}, u32[]{:S(2)}) collective-permute-start(f32[288,512]{1,0:T(8,128)S(1)} %bitcast.307), channel_id=1, source_target_pairs={{0,8},{4,12},{8,0},{12,4},{1,9},{5,13},{9,1},{13,5},{2,10},{6,14},... | collective-permute-start | bytes 1769480 | tf_op jit(solution)/shard_map/ppermute | solution.py:51
  (76 other events, 721.6 us)
Sparse Core Ops, SparseCore 0:
  10.9 79.0 all-gather.4
  92.1 70.1 all-gather.6
  639.4 53.7 all-gather.8

commit v2 on v1

v2 whole, which is shorter than its diff:
```python
import functools
import math

import jax
import jax.numpy as jnp
from jax import lax
from jax.experimental import pallas as pl
from jax.experimental.pallas import tpu as pltpu
from jax.sharding import PartitionSpec as P

MODEL_WIDTH = 1536
HEADS = 24
KV_HEADS = 8
HEAD = 64
HIDDEN = 512
ADAPTER_RANK = 16
ADAPTER_COUNT = 8
PROMPT_LEAST = 1024
PROMPT_DEV = 128
KEY_FEATURES = 512
LANES = 128
SMALL_AT = 96

EPS = 1e-05
NEG = -1e30
F32 = jnp.float32
BF16 = jnp.bfloat16
FIRST_EXPERTS = 3
TILE = 256
DOWN_AT = 80


def dot(a, b, dims=((1,), (0,))):
    return lax.dot_general(a, b, (dims, ((), ())), preferred_element_type=F32)


def dot_nt(a, b):
    return dot(a, b, ((1,), (1,)))


def dot_tn(a, b):
    return dot(a, b, ((0,), (0,)))


def swap_core(x, n_seq):
    return lax.ppermute(x, "seq", [(i, i ^ 1) for i in range(n_seq)])


def shift_chip(x, n_seq, k):
    n_y = n_seq // 2
    pairs = [(y * 2 + c, (y + k) % n_y * 2 + c) for y in range(n_y) for c in range(2)]
    return lax.ppermute(x, "seq", pairs)


def seq_pieces(x, n_seq):
    n_y = n_seq // 2
    me = lax.axis_index("seq")
    y, c = me // 2, me % 2
    far = [shift_chip(x, n_seq, k) for k in range(1, n_y)]
    pieces = [(me, x), (me ^ 1, swap_core(x, n_seq))]
    for k, piece in enumerate(far, 1):
        chip = (y + n_y - k) % n_y * 2
        pieces += [(chip + c, piece), (chip + 1 - c, swap_core(piece, n_seq))]
    return pieces


def gather_seq(x, n_seq):
    out = jnp.zeros((n_seq,) + x.shape, x.dtype)
    for at, piece in seq_pieces(x, n_seq):
        out = lax.dynamic_update_slice_in_dim(out, piece[None], at, 0)
    return out


def core_sum(x, n_seq):
    c = lax.axis_index("seq") % 2
    got = swap_core(lax.dynamic_index_in_dim(x, 1 - c, 0, keepdims=False), n_seq)
    kept = lax.dynamic_index_in_dim(x, c, 0, keepdims=False)
    return kept.astype(F32) + got.astype(F32)


def scatter_piece(x, n_seq, k):
    both = core_sum(x, n_seq)
    return shift_chip(both.astype(x.dtype), n_seq, k).astype(F32) if k else both


def chip_turns(n_seq):
    n_y = n_seq // 2
    y = lax.axis_index("seq") // 2
    return [(k, (y + k) % n_y) for k in [*range(1, n_y), 0]]


def scatter_seq(x, n_seq):
    x = x.reshape((n_seq // 2, 2) + x.shape[1:])
    return sum(
        scatter_piece(lax.dynamic_index_in_dim(x, chip, 0, keepdims=False), n_seq, k)
        for k, chip in chip_turns(n_seq)
    )


def spread_seq(x, n_seq):
    n_y = n_seq // 2
    me = lax.axis_index("seq")
    y, c = me // 2, me % 2
    x = x.reshape((n_y, 2) + x.shape[1:])
    out = jnp.zeros((n_seq,) + x.shape[2:], x.dtype)
    for k, chip in chip_turns(n_seq):
        pair = lax.dynamic_index_in_dim(x, chip, 0, keepdims=False)
        if k:
            pair = shift_chip(pair, n_seq, k)
        other = swap_core(lax.dynamic_index_in_dim(pair, 1 - c, 0, keepdims=False), n_seq)
        same = lax.dynamic_index_in_dim(pair, c, 0, keepdims=False)
        at = (y + n_y - k) % n_y * 2
        out = lax.dynamic_update_slice_in_dim(out, same[None], at + c, 0)
        out = lax.dynamic_update_slice_in_dim(out, other[None], at + 1 - c, 0)
    return out


def shift(x, axis, count, k):
    return lax.ppermute(x, axis, [(i, (i + k) % count) for i in range(count)])


def column_fold(x, op):
    rows, width = x.shape
    return op(x.reshape(rows // 8, 8, width), axis=0)


def attend_kernel(
    prompt_blocks, q_ref, k_ref, v_ref, segq_ref, segk_ref, o_ref, p_ref, inv_ref, krow, scores
):
    i = pl.program_id(1)
    group, qb = q_ref.shape[1], q_ref.shape[3]
    width = group * qb

    @pl.when(i == 0)
    def _():
        krow[...] = k_ref[0].astype(F32).T.astype(BF16)

    q = jnp.concatenate([q_ref[0, h] for h in range(group)], axis=1)
    segq = jnp.concatenate([segq_ref[...]] * group, axis=1)
    placeq = i * qb + lax.broadcasted_iota(jnp.int32, (1, width), 1) % qb

    def score(j, peak, masked):
        rows = pl.ds(pl.multiple_of(j * qb, qb), qb)
        s = dot(krow[rows, :], q)
        if masked:
            segk = segk_ref[rows, :]
            placek = j * qb + lax.broadcasted_iota(jnp.int32, (qb, 1), 0)
            keep = (placek <= placeq) & ((segk < 0) | (segk == segq))
            s = jnp.where(keep, s, NEG)
        scores[rows, :] = s
        return jnp.maximum(peak, column_fold(s, jnp.max))

    free = jnp.minimum(i, prompt_blocks)
    peak = jnp.full((8, width), NEG, F32)
    peak = lax.fori_loop(0, free, lambda j, m: score(j, m, False), peak)
    peak = lax.fori_loop(free, i + 1, lambda j, m: score(j, m, True), peak)
    peak = jnp.max(peak, axis=0, keepdims=True)

    def weigh(j, carry):
        total, acc = carry
        rows = pl.ds(pl.multiple_of(j * qb, qb), qb)
        p = jnp.exp(scores[rows, :] - peak)
        low = p.astype(BF16)
        p_ref[0, 0, rows, :] = low
        return total + column_fold(p, jnp.sum), acc + dot(v_ref[0, :, rows], low)

    total, acc = lax.fori_loop(
        0, i + 1, weigh, (jnp.zeros((8, width), F32), jnp.zeros((HEAD, width), F32))
    )
    inverse = 1.0 / jnp.sum(total, axis=0, keepdims=True)
    inv_ref[0, 0] = inverse
    out = (acc * inverse).astype(BF16)
    for h in range(group):
        o_ref[0, h] = out[:, h * qb : (h + 1) * qb]


def attend(qt, kt, vt, segment, prompt_len, block):
    kv, group, _, total = qt.shape
    blocks = total // block
    width = group * block
    pairs = kv * group * total * total // 2
    return pl.pallas_call(
        functools.partial(attend_kernel, prompt_len // block),
        grid=(kv, blocks),
        in_specs=[
            pl.BlockSpec((1, group, HEAD, block), lambda b, i: (b, 0, 0, i)),
            pl.BlockSpec((1, HEAD, total), lambda b, i: (b, 0, 0)),
            pl.BlockSpec((1, HEAD, total), lambda b, i: (b, 0, 0)),
            pl.BlockSpec((1, block), lambda b, i: (0, i)),
            pl.BlockSpec((total, 1), lambda b, i: (0, 0)),
        ],
        out_specs=[
            pl.BlockSpec((1, group, HEAD, block), lambda b, i: (b, 0, 0, i)),
            pl.BlockSpec((1, 1, total, width), lambda b, i: (b, i, 0, 0)),
            pl.BlockSpec((1, 1, 1, width), lambda b, i: (b, i, 0, 0)),
        ],
        out_shape=[
            jax.ShapeDtypeStruct(qt.shape, BF16),
            jax.ShapeDtypeStruct((kv, blocks, total, width), BF16),
            jax.ShapeDtypeStruct((kv, blocks, 1, width), F32),
        ],
        scratch_shapes=[pltpu.VMEM((total, HEAD), BF16), pltpu.VMEM((total, width), F32)],
        compiler_params=pltpu.CompilerParams(vmem_limit_bytes=40 * 2**20),
        cost_estimate=pl.CostEstimate(
            flops=pairs * HEAD * 4, bytes_accessed=pairs * 4, transcendentals=pairs
        ),
    )(qt, kt, vt, segment[None, :], segment[:, None])


def unrotate(grad, cosine, sine):
    half = HEAD // 2
    first, second = grad[:half], grad[half:]
    return jnp.concatenate(
        [first * cosine + second * sine, second * cosine - first * sine], axis=0
    )


def attend_back_kernel(
    q_ref, k_ref, v_ref, o_ref, do_ref, p_ref, inv_ref, cosq_ref, sinq_ref, cos_ref, sin_ref,
    dq_ref, dk_ref, dv_ref, vrow, dk_acc, dv_acc,
):
    i = pl.program_id(1)
    group, qb = q_ref.shape[1], q_ref.shape[3]
    width = group * qb

    @pl.when(i == 0)
    def _():
        vrow[...] = v_ref[0].astype(F32).T.astype(BF16)
        dk_acc[...] = jnp.zeros_like(dk_acc)
        dv_acc[...] = jnp.zeros_like(dv_acc)

    def side(ref, *at):
        return jnp.concatenate([ref[(0, *at, h)].astype(F32) for h in range(group)], axis=1)

    do = side(do_ref, 0) * inv_ref[0, 0]
    centre = jnp.sum(side(o_ref) * do, axis=0, keepdims=True)
    do_low = do.astype(BF16)
    do_rows = do.T.astype(BF16)
    q_rows = side(q_ref).T.astype(BF16)

    def step(j, acc):
        rows = pl.ds(pl.multiple_of(j * qb, qb), qb)
        p = p_ref[0, 0, rows, :]
        dp = dot(vrow[rows, :], do_low)
        ds = (p.astype(F32) * (dp - centre)).astype(BF16)
        dk_acc[rows, :] += dot(ds, q_rows)
        dv_acc[rows, :] += dot(p, do_rows)
        return acc + dot(k_ref[0, :, rows], ds)

    dq = lax.fori_loop(0, i + 1, step, jnp.zeros((HEAD, width), F32)) * HEAD**-0.5
    for h in range(group):
        part = dq[:, h * qb : (h + 1) * qb]
        dq_ref[0, h] = unrotate(part, cosq_ref[...], sinq_ref[...]).astype(BF16)

    @pl.when(i == pl.num_programs(1) - 1)
    def _():
        dk_ref[0] = unrotate(dk_acc[...].T, cos_ref[...], sin_ref[...]).astype(BF16)
        dv_ref[0] = dv_acc[...].T.astype(BF16)


def attend_back(qt, kt, vt, ot, do, p, inverse, cosine, sine):
    kv, group, _, total = qt.shape
    blocks, block = do.shape[0], do.shape[-1]
    width = group * block
    pairs = kv * group * total * total // 2
    q_spec = pl.BlockSpec((1, group, HEAD, block), lambda b, i: (b, 0, 0, i))
    k_spec = pl.BlockSpec((1, HEAD, total), lambda b, i: (b, 0, 0))
    return pl.pallas_call(
        attend_back_kernel,
        grid=(kv, blocks),
        in_specs=[
            q_spec, k_spec, k_spec, q_spec,
            pl.BlockSpec((1, 1, group, HEAD, block), lambda b, i: (i, b, 0, 0, 0)),
            pl.BlockSpec((1, 1, total, width), lambda b, i: (b, i, 0, 0)),
            pl.BlockSpec((1, 1, 1, width), lambda b, i: (b, i, 0, 0)),
            pl.BlockSpec((HEAD // 2, block), lambda b, i: (0, i)),
            pl.BlockSpec((HEAD // 2, block), lambda b, i: (0, i)),
            pl.BlockSpec((HEAD // 2, total), lambda b, i: (0, 0)),
            pl.BlockSpec((HEAD // 2, total), lambda b, i: (0, 0)),
        ],
        out_specs=[q_spec, k_spec, k_spec],
        out_shape=[
            jax.ShapeDtypeStruct(qt.shape, BF16),
            jax.ShapeDtypeStruct(kt.shape, BF16),
            jax.ShapeDtypeStruct(vt.shape, BF16),
        ],
        scratch_shapes=[
            pltpu.VMEM((total, HEAD), BF16),
            pltpu.VMEM((total, HEAD), F32),
            pltpu.VMEM((total, HEAD), F32),
        ],
        compiler_params=pltpu.CompilerParams(vmem_limit_bytes=40 * 2**20),
        cost_estimate=pl.CostEstimate(
            flops=pairs * HEAD * 8, bytes_accessed=pairs * 4, transcendentals=0
        ),
    )(qt, kt, vt, ot, do, p, inverse, cosine, sine, cosine, sine)


def pack_experts(gate_up, down):
    parts = [gate_up[..., :HIDDEN], gate_up[..., HIDDEN:]]
    parts += [down[..., m : m + HIDDEN] for m in range(0, MODEL_WIDTH, HIDDEN)]
    return jnp.concatenate(parts, axis=1)


def expert_kernel(
    starts, rows, hidden_rows, experts_all, first, last, place_ref, x_ref, dy_ref, gate_ref,
    zbias_ref, sbias_ref, dfa_ref, back_ref, *refs,
):
    refs = list(refs)
    carried = [None] * 5 if first else [refs.pop(0) for _ in range(5)]
    shards = [refs.pop(0) for _ in starts]
    outs = [refs.pop(0) for _ in range(5)]
    w_up, w_down, *accs, sem = refs
    count = w_up.shape[0]
    tile = x_ref.shape[0]

    def copies(e):
        pairs = []
        for b, (start, shard) in enumerate(zip(starts, shards)):
            index = place_ref[2 + b]
            up_rows = pl.ds(pl.multiple_of(index * rows, rows), rows)
            down_rows = pl.ds(pl.multiple_of(index * hidden_rows, hidden_rows), hidden_rows)
            for m in range(2):
                pairs.append((shard.at[start + e, pl.ds(m * rows, rows), :],
                              w_up.at[e, up_rows, pl.ds(m * HIDDEN, HIDDEN)]))
            for m in range(MODEL_WIDTH // HIDDEN):
                pairs.append((shard.at[start + e, pl.ds(2 * rows + m * hidden_rows, hidden_rows), :],
                              w_down.at[e, down_rows, pl.ds(m * HIDDEN, HIDDEN)]))
        return [pltpu.make_async_copy(a, b, sem.at[e, n]) for n, (a, b) in enumerate(pairs)]

    lane = lax.broadcasted_iota(jnp.int32, (tile, LANES), 1)

    def add(n, e, value):
        base = carried[n] if e == 0 else accs[n]
        if base is not None:
            value = base[...].astype(F32) + value
        if e < count - 1:
            accs[n][...] = value
        elif n == 2 and last:
            accs[n][...] = value
        elif n == 1 and last:
            outs[n][:, :MODEL_WIDTH] = value.astype(outs[n].dtype)
        else:
            outs[n][...] = value.astype(outs[n].dtype)

    def step(e):
        name = place_ref[0] + e
        both = dot(x_ref[...], w_up[e]) + zbias_ref[...]
        gate_in, up = both[:, :HIDDEN], both[:, HIDDEN:]
        sigma = jax.nn.sigmoid(gate_in)
        silu = gate_in * sigma
        inner = silu * up
        d_down = dot_nt(dy_ref[...], w_down[e]) + sbias_ref[...]
        d_gating = jnp.sum(inner * d_down, axis=1, keepdims=True)
        gating = jnp.sum(jnp.where(lane == name, gate_ref[...], 0.0), axis=1, keepdims=True)
        add(2, e, jnp.where((lane == name) | (lane == name + experts_all), d_gating, 0.0))
        gated = gating * inner
        add(3, e, gated)
        add(0, e, dot(gated.astype(BF16), w_down[e]))
        d_inner = gating * d_down
        d_gate = d_inner * up * (sigma + silu * (1.0 - sigma))
        d_both = jnp.concatenate([d_gate, d_inner * silu], axis=1)
        add(4, e, d_both)
        add(1, e, dot_nt(d_both.astype(BF16), w_up[e]))

    @pl.when(pl.program_id(0) == 0)
    def _():
        for e in range(count):
            for copy in copies(e):
                copy.start()
        for e in range(count):
            for copy in copies(e):
                copy.wait()
            step(e)

    @pl.when(pl.program_id(0) > 0)
    def _():
        for e in range(count):
            step(e)

    if last:
        aux = accs[2][...] + dot(outs[3][...], dfa_ref[...]) + dot(outs[4][...], back_ref[...])
        high = aux.astype(BF16)
        rest = (aux - high.astype(F32)).astype(BF16)
        is_rest = (lane >= experts_all) & (lane < 2 * experts_all)
        outs[1][:, MODEL_WIDTH:] = jnp.where(is_rest, rest, high)
        outs[2][...] = aux


def run_experts(place, x, dy, gates, zbias, sbias, mats, carried, shards, starts, count, experts_all, rows_out, last):
    rows = MODEL_WIDTH // len(shards)
    hidden_rows = HIDDEN // len(shards)
    first = carried is None
    acc_widths = (MODEL_WIDTH, MODEL_WIDTH, LANES, HIDDEN, 2 * HIDDEN)
    widths = (MODEL_WIDTH, MODEL_WIDTH + LANES if last else MODEL_WIDTH, *acc_widths[2:])
    dtypes = (BF16, BF16, F32, BF16, BF16)

    def tiled(width):
        return pl.BlockSpec((TILE, width), lambda t, place: (place[1] + t, 0))

    def out_tiled(width):
        return pl.BlockSpec((TILE, width), lambda t, _: (t, 0))

    in_widths = (MODEL_WIDTH, MODEL_WIDTH, LANES, 2 * HIDDEN, HIDDEN)
    specs = [tiled(w) for w in in_widths]
    specs += [pl.BlockSpec(m.shape, lambda t, _: (0, 0)) for m in mats]
    specs += [] if first else [tiled(w) for w in acc_widths]
    specs += [pl.BlockSpec(memory_space=pl.ANY)] * len(shards)
    copies = len(shards) * (2 + MODEL_WIDTH // HIDDEN)
    return pl.pallas_call(
        functools.partial(
            expert_kernel, tuple(starts), rows, hidden_rows, experts_all, first, last
        ),
        grid_spec=pltpu.PrefetchScalarGridSpec(
            num_scalar_prefetch=1,
            grid=(rows_out // TILE,),
            in_specs=specs,
            out_specs=[out_tiled(w) for w in widths],
            scratch_shapes=[
                pltpu.VMEM((count, MODEL_WIDTH, 2 * HIDDEN), BF16),
                pltpu.VMEM((count, HIDDEN, MODEL_WIDTH), BF16),
                *[pltpu.VMEM((TILE, w), F32) for w in acc_widths],
                pltpu.SemaphoreType.DMA((count, copies)),
            ],
        ),
        out_shape=[jax.ShapeDtypeStruct((rows_out, w), t) for w, t in zip(widths, dtypes)],
        compiler_params=pltpu.CompilerParams(vmem_limit_bytes=60 * 2**20),
        cost_estimate=pl.CostEstimate(
            flops=12 * rows_out * MODEL_WIDTH * HIDDEN * count,
            bytes_accessed=rows_out * MODEL_WIDTH * 10,
            transcendentals=rows_out * HIDDEN * count,
        ),
    )(place, x, dy, gates, zbias, sbias, *mats, *(carried or ()), *shards)


def norm_backward(value_rows, inverse, gain_row, upstream):
    scaled = upstream * gain_row
    inner_mean = jnp.mean(value_rows * scaled, axis=-1, keepdims=True)
    return inverse * scaled - value_rows * (inverse * inverse * inverse) * inner_mean


def layout(lengths_row, prompt_len, total_len):
    ends = jnp.sum(jnp.tril(jnp.ones((lengths_row.shape[0],) * 2, jnp.int32)) * lengths_row, axis=1)
    starts = ends - lengths_row
    places = jnp.arange(total_len, dtype=jnp.int32)
    offset = places - prompt_len
    counted = jnp.sum((offset[:, None] >= ends[None, :]).astype(jnp.int32), axis=1)
    inside = offset >= 0
    segment = jnp.where(inside, counted, -1)
    picked = jnp.arange(lengths_row.shape[0], dtype=jnp.int32)[None, :] == counted[:, None]
    begin = jnp.sum(jnp.where(picked, starts[None, :], 0), axis=1)
    position = jnp.where(inside, prompt_len + offset - begin, places)
    return (segment, position)


def pad_lanes(x, at=0, width=LANES):
    return jnp.pad(x, ((0, 0), (at, width - at - x.shape[1])))


def gather_groups(x, n_dp, n_wt):
    row = jnp.stack([shift(x, "dp", n_dp, k) if k else x for k in range(n_dp)])
    return jnp.concatenate([shift(row, "wt", n_wt, b) if b else row for b in range(n_wt)])


def reduce_seq(flat, n_seq):
    rows, width = flat.shape
    return scatter_seq(flat.reshape(n_seq, rows // n_seq, width), n_seq)


def tagged(mine, index_now):
    return jnp.concatenate([mine, jnp.full((8, mine.shape[1]), index_now.astype(F32))], 0)


def by_adapter(everyone, names, n_seq, n_wt):
    share = ADAPTER_COUNT // n_wt
    part, width = everyone.shape[1:]
    first_row = lax.axis_index("wt") * share
    picks = (names[None, :] == first_row + jnp.arange(share)[:, None]).astype(F32)
    kept = jnp.sum(picks[:, :, None, None] * everyone[None].astype(F32), axis=1)
    pieces = seq_pieces(kept.reshape(share * part, width), n_seq)
    place = jnp.arange(n_seq)[None, :, None, None]
    full = sum(jnp.where(place == at, x.reshape(share, 1, part, width), 0.0) for at, x in pieces)
    return full.reshape(share, n_seq * part, width)


def shards(
    tokens,
    cotangent,
    routes,
    lengths,
    group_adapter_index,
    attention_norm_gain,
    query_weight,
    key_value_weight,
    output_weight,
    mixture_norm_gain,
    router_weight,
    expert_gate_up_weight,
    expert_down_weight,
    attention_first_factors,
    query_second_factor,
    key_value_second_factors,
    output_first_factor,
    output_second_factor,
    mixture_first_factors,
    router_second_factor,
    gate_up_second_factors,
    down_first_factor,
    down_second_factor,
):
    n_seq, n_dp, n_wt = (lax.axis_size(a) for a in ("seq", "dp", "wt"))
    seq, dp, wt = (lax.axis_index(a) for a in ("seq", "dp", "wt"))
    local = tokens.shape[1]
    total = local * n_seq
    prompt_len = max(PROMPT_LEAST, PROMPT_DEV * n_seq)
    exp_dev = expert_gate_up_weight.shape[0]
    experts_all = exp_dev * n_seq
    kv_local = KV_HEADS // n_seq
    group = HEADS // KV_HEADS
    q_width = MODEL_WIDTH // n_seq
    k_width = KEY_FEATURES // n_seq
    rank = ADAPTER_RANK
    index_now = group_adapter_index[0]

    def chosen(bank):
        return lax.dynamic_index_in_dim(bank, index_now, 0, keepdims=False)

    def own(x, size, axis=1, at=0):
        return lax.dynamic_slice_in_dim(x, at + seq * size, size, axis)

    attn_first = chosen(attention_first_factors)
    query_second = own(chosen(query_second_factor), q_width)
    kv_second = chosen(key_value_second_factors)
    out_first = chosen(output_first_factor)
    out_second = chosen(output_second_factor)
    mix_first = chosen(mixture_first_factors)
    router_second = chosen(router_second_factor)
    gate_up_second = chosen(gate_up_second_factors)
    down_first = chosen(down_first_factor)
    down_second = chosen(down_second_factor)

    def own_rows(x):
        return lax.dynamic_slice_in_dim(x, seq * local, local, 0)

    split = FIRST_EXPERTS
    tie = lax.optimization_barrier

    def across(x):
        return [shift(x, "dp", n_dp, k) for k in range(1, n_dp)]

    came = pack_experts(expert_gate_up_weight, expert_down_weight)
    pieces = [(0, 0, came)]
    for b in range(1, n_wt - 1):
        came, *moved = tie((shift(came, "wt", n_wt, 1), *across(came)))
        pieces += [(k, b - 1, x) for k, x in enumerate(moved, 1)] + [(0, b, came)]
    ahead, *moved = tie((shift(came[:split], "wt", n_wt, 1), *across(came)))
    pieces += [(k, n_wt - 2, x) for k, x in enumerate(moved, 1)]
    behind = shift(came[split:], "wt", n_wt, 1)
    ahead = [ahead, *across(ahead)]
    behind = [behind, *across(behind)]

    hidden = gather_seq(tokens[0], n_seq).reshape(total, MODEL_WIDTH)

    def gather_weights(x):
        return lax.all_gather(x, ("dp", "wt"), axis=0, tiled=True)

    mine = jnp.concatenate(
        [
            own(query_weight, q_width),
            own(key_value_weight, k_width),
            own(key_value_weight, k_width, at=KEY_FEATURES),
            pad_lanes(router_weight),
        ],
        axis=1,
    )
    gathered = gather_weights(mine)
    qkv_width = q_width + 2 * k_width
    qkv_weight = gathered[:, :qkv_width]
    router_full = gathered[:, qkv_width : qkv_width + experts_all]
    half = MODEL_WIDTH // 2
    core = seq % 2
    out_mine = gather_weights(lax.dynamic_slice_in_dim(output_weight, core * half, half, 1))
    out_other = swap_core(out_mine, n_seq)
    out_weight = jnp.where(
        core == 0,
        jnp.concatenate([out_mine, out_other], 1),
        jnp.concatenate([out_other, out_mine], 1),
    )

    gain_first = attention_norm_gain.astype(F32)
    gain_second = mixture_norm_gain.astype(F32)
    hidden_f = hidden.astype(F32)
    inverse_a = lax.rsqrt(jnp.mean(hidden_f * hidden_f, axis=-1, keepdims=True) + EPS)
    normed = (hidden_f * inverse_a * gain_first).astype(BF16)
    small_a = dot(normed, attn_first).astype(BF16)
    second = jnp.zeros((3 * rank, qkv_width), BF16)
    second = second.at[:rank, :q_width].set(query_second)
    second = second.at[rank : 2 * rank, q_width : q_width + k_width].set(own(kv_second[0], k_width))
    second = second.at[2 * rank :, q_width + k_width :].set(own(kv_second[1], k_width))
    qkv = dot(qkv_weight, normed, ((0,), (1,))) + dot(second, small_a, ((0,), (1,)))
    segment, position = layout(lengths[0], prompt_len, total)
    freq = jnp.exp(jnp.arange(HEAD // 2, dtype=F32) * (-2.0 * math.log(10000.0) / HEAD))
    angle = freq[:, None] * position.astype(F32)[None, :]
    cosine, sine = jnp.cos(angle), jnp.sin(angle)

    def rotate(x, scale=1.0):
        x = x.reshape(-1, 2, HEAD // 2, total)
        a, b = x[:, 0], x[:, 1]
        x = jnp.concatenate([a * cosine - b * sine, b * cosine + a * sine], axis=1)
        return (x.astype(BF16) * jnp.asarray(scale, BF16)).reshape(-1, HEAD, total)

    qt = rotate(qkv[:q_width], HEAD**-0.5).reshape(kv_local, group, HEAD, total)
    kt = rotate(qkv[q_width : q_width + k_width])
    vt = qkv[q_width + k_width :].astype(BF16).reshape(kv_local, HEAD, total)
    ot, probs, inverse_l = attend(qt, kt, vt, segment, prompt_len, local)
    att = gather_seq(ot.reshape(q_width, total), n_seq).reshape(MODEL_WIDTH, total)

    named = jnp.arange(LANES, dtype=jnp.int32)[None, None, :]
    mask = jnp.any(routes[0][:, :, None] == named, axis=1).astype(BF16)
    d_out = jnp.concatenate([cotangent[0], mask], axis=1)
    d_out, _ = lax.optimization_barrier((d_out, hidden))
    d_out = gather_seq(d_out, n_seq).reshape(total, MODEL_WIDTH + LANES)
    d_out_all = d_out[:, :MODEL_WIDTH]
    routed = d_out[:, MODEL_WIDTH : MODEL_WIDTH + experts_all] > 0.5

    small_o = dot_tn(att, out_first).astype(BF16)
    residual = hidden_f + dot_tn(att, out_weight) + dot(small_o, out_second)
    inverse_m = lax.rsqrt(jnp.mean(residual * residual, axis=-1, keepdims=True) + EPS)
    normed_m = (residual * inverse_m * gain_second).astype(BF16)
    mix_router = jnp.concatenate([mix_first, router_full], axis=1)
    states = dot(normed_m, mix_router)
    small_m = states[:, : 3 * rank].astype(BF16)
    logits = states[:, 3 * rank :] + dot(small_m[:, :rank], router_second)
    logits = jnp.where(routed, logits, NEG)
    peak = jnp.max(logits, axis=-1, keepdims=True)
    weights = jnp.where(routed, jnp.exp(logits - peak), 0.0)
    gating = weights / jnp.sum(weights, axis=-1, keepdims=True)

    d_rank = dot_nt(d_out_all, down_second).astype(BF16)
    gus = jnp.zeros((2 * rank, 2 * HIDDEN), BF16)
    gus = gus.at[:rank, :HIDDEN].set(gate_up_second[0])
    gus = gus.at[rank:, HIDDEN:].set(gate_up_second[1])
    mats = (pad_lanes(down_first, DOWN_AT), pad_lanes(gus.T, SMALL_AT))
    zbias = dot(small_m[:, rank:], gus).astype(BF16)
    sbias = dot_nt(d_rank, down_first).astype(BF16)
    gates = pad_lanes(gating)

    order = [(k, b) for k, b, _ in pieces] + [(k, n_wt - 1) for k in range(n_dp)]
    places = [(dp + n_dp - k) % n_dp * n_wt + (wt + n_wt - b) % n_wt for k, b in order]
    held = [x for _, _, x in pieces]

    def place_of(expert, row):
        return jnp.stack([x.astype(jnp.int32) for x in (seq * exp_dev + expert, row, *places)])

    carried = run_experts(
        place_of(0, seq * 0), normed_m, d_out_all, gates, zbias, sbias, mats, None, held + ahead,
        [0] * len(order), split, experts_all, total, False,
    )
    chip_rows = 2 * local
    turns, arrived, waiting = [], [], None
    for k, chip in chip_turns(n_seq):
        place = place_of(split, chip * (chip_rows // TILE))
        if waiting is not None:
            place, sent = tie((place, waiting[1].astype(BF16)))
            arrived.append(shift_chip(sent, n_seq, waiting[0]))
        parts = run_experts(
            place, normed_m, d_out_all, gates, zbias, sbias, mats, carried, held + behind,
            [split] * len(held) + [0] * len(behind), exp_dev - split, experts_all, chip_rows, True,
        )
        parts = list(parts)
        if arrived:
            arrived[-1], parts[1] = tie((arrived[-1], parts[1]))
        turns.append((k, chip, parts))
        waiting = (k, core_sum(parts[1].reshape(2, local, -1), n_seq))
    back_sum = waiting[1] + sum(x.astype(F32) for x in arrived)

    upstream = cotangent[0].astype(F32)
    residual_own = own_rows(residual)
    gating_own = own_rows(gating)
    small_m_own = own_rows(small_m)
    d_gating = (
        back_sum[:, MODEL_WIDTH : MODEL_WIDTH + experts_all]
        + back_sum[:, MODEL_WIDTH + experts_all : MODEL_WIDTH + 2 * experts_all]
    )
    d_logits = gating_own * (d_gating - jnp.sum(d_gating * gating_own, axis=-1, keepdims=True))
    d_logits_low = d_logits.astype(BF16)
    d_small_m = jnp.concatenate(
        [dot_nt(d_logits_low, router_second), back_sum[:, MODEL_WIDTH + SMALL_AT :]], axis=1
    ).astype(BF16)
    small_d = back_sum[:, MODEL_WIDTH + DOWN_AT : MODEL_WIDTH + DOWN_AT + rank].astype(BF16)
    d_normed_m = back_sum[:, :MODEL_WIDTH] + dot_nt(
        jnp.concatenate([d_small_m, d_logits_low], axis=1), mix_router
    )
    d_residual = upstream + norm_backward(
        residual_own, own_rows(inverse_m), gain_second, d_normed_m
    )
    d_branch = d_residual.astype(BF16)
    d_small_o = dot_nt(d_branch, out_second).astype(BF16)
    d_att = (dot_nt(out_weight, d_branch) + dot_nt(out_first, d_small_o)).astype(BF16)
    d_att = spread_seq(d_att.reshape(n_seq, q_width, local), n_seq)

    def of_chip(x, chip, axis=0):
        return lax.dynamic_slice_in_dim(x, chip * chip_rows, chip_rows, axis)

    grad_gu = sum(dot_tn(of_chip(small_m[:, rank:], chip), parts[4]) for _, chip, parts in turns)
    grad_down = sum(dot_tn(of_chip(d_rank, chip), parts[3]) for _, chip, parts in turns)
    att_own = lax.dynamic_slice_in_dim(att, seq * local, local, 1)
    early = jnp.concatenate(
        [
            dot(d_small_o, att_own, ((0,), (1,))),
            dot_tn(own_rows(small_o), d_branch),
            dot_tn(d_small_m, own_rows(normed_m)),
            dot_tn(small_d, cotangent[0]),
            jnp.concatenate([grad_gu[:rank, :HIDDEN], grad_gu[rank:, HIDDEN:], grad_down], axis=1),
            pad_lanes(dot_tn(small_m_own[:, :rank], d_logits_low), width=MODEL_WIDTH),
        ],
        axis=0,
    )
    early = reduce_seq(early, n_seq)
    parts_out = [core_sum(parts[0].reshape(2, local, -1), n_seq) for _, _, parts in turns]
    early, d_att, *parts_sent = tie((early, d_att, *[x.astype(BF16) for x in parts_out[:-1]]))
    early = lax.all_gather(tagged(early, index_now), ("dp", "wt"), axis=0)
    sent = [shift_chip(x, n_seq, k) for x, (k, _, _) in zip(parts_sent, turns)]
    dqt, dkt, dvt = attend_back(
        qt, kt, vt, ot, d_att.reshape(n_seq, kv_local, group, HEAD, local), probs, inverse_l,
        cosine, sine,
    )
    dqt, *sent = tie((dqt, *sent))
    output_rows = residual_own + dot(small_d, down_second) + parts_out[-1]
    output_rows = output_rows + sum(x.astype(F32) for x in sent)

    d_qkv = jnp.concatenate(
        [dqt.reshape(q_width, total), dkt.reshape(k_width, total), dvt.reshape(k_width, total)], 0
    )
    d_small_a = dot(d_qkv, second, ((0,), (1,))).astype(BF16)
    grad_second = dot(small_a, d_qkv, ((0,), (1,)))

    def spread(x, width, full):
        return lax.dynamic_update_slice_in_dim(
            jnp.zeros((x.shape[0], full), F32), x, seq * width, 1
        )

    late = jnp.concatenate(
        [
            dot_tn(d_small_a, normed),
            spread(grad_second[:rank, :q_width], q_width, MODEL_WIDTH),
            jnp.concatenate(
                [
                    spread(grad_second[rank : 2 * rank, q_width : q_width + k_width], k_width, KEY_FEATURES),
                    spread(grad_second[2 * rank :, q_width + k_width :], k_width, KEY_FEATURES),
                    jnp.zeros((rank, MODEL_WIDTH - 2 * KEY_FEATURES), F32),
                ],
                axis=1,
            ),
        ],
        axis=0,
    )
    late = reduce_seq(late, n_seq)
    d_normed = None
    for k, chip in chip_turns(n_seq):
        part = dot(of_chip(d_qkv, chip, 1), qkv_weight, ((0,), (1,)))
        part = part + dot_nt(of_chip(d_small_a, chip), attn_first)
        part = core_sum(part.astype(BF16).reshape(2, local, MODEL_WIDTH), n_seq)
        if k:
            late, part = tie((late, part.astype(BF16)))
            part = shift_chip(part, n_seq, k).astype(F32)
        d_normed = part if d_normed is None else d_normed + part
    input_grad = d_residual + norm_backward(
        tokens[0].astype(F32), own_rows(inverse_a), gain_first, d_normed
    )
    names = early[:, -1, 0].astype(jnp.int32)
    early = by_adapter(early[:, :-8], names, n_seq, n_wt)
    turned = jnp.stack(
        [
            (dp + n_dp - k) % n_dp * n_wt + (wt + n_wt - b) % n_wt
            for b in range(n_wt) for k in range(n_dp)
        ]
    )
    late = by_adapter(gather_groups(late.astype(BF16), n_dp, n_wt), names[turned], n_seq, n_wt)

    def flip(x):
        return jnp.swapaxes(x, 1, 2)

    def at(flat, row, count, lo=0, hi=MODEL_WIDTH):
        return flat[:, row : row + count, lo:hi]

    low = 6 * rank
    return (
        output_rows[None].astype(BF16),
        input_grad[None],
        flip(at(late, 0, 3 * rank)),
        at(late, 3 * rank, rank),
        jnp.stack(
            [at(late, 4 * rank, rank, m, m + KEY_FEATURES) for m in (0, KEY_FEATURES)], axis=1
        ),
        flip(at(early, 0, rank)),
        at(early, rank, rank),
        flip(at(early, 2 * rank, 3 * rank)),
        at(early, low + rank, rank, 0, experts_all),
        jnp.stack([at(early, low, rank, m, m + HIDDEN) for m in (0, HIDDEN)], axis=1),
        flip(at(early, low, rank, 2 * HIDDEN, 3 * HIDDEN)),
        at(early, 5 * rank, rank),
    )


def solution(mesh):
    split = P(("dp", "wt"), "seq", None)
    rows = P(("dp", "wt"), None)
    bank = P("wt", None, None)
    placed = (
        split, split, split, rows, P(("dp", "wt")), P(), rows, rows, rows, P(), rows,
        P("seq", ("dp", "wt"), None), P("seq", ("dp", "wt"), None),
    ) + (P(),) * 10
    wide = P("wt", None, None, None)
    return jax.shard_map(
        shards,
        mesh=mesh,
        in_specs=placed,
        out_specs=(split, split, bank, bank, wide, bank, bank, bank, bank, wide, bank, bank),
        check_vma=False,
    )
```

time: 738 us -> 662 us (0.90)
  waiting for transfers between devices: 273 us -> 159 us
  local copies, waits for them, and re-layouts: 104 us -> 126 us
  starting transfers between devices: 24.8 us -> 32.6 us
    ppermute x8 -> x11, waiting for transfers between devices: 104 us -> 40.5 us  [shift_chip(): return lax.ppermute(x, 'seq', pairs)]
    ppermute x7 -> x13, waiting for transfers between devices: 151 us -> 116 us  [shift(): return lax.ppermute(x, axis, [(i, (i + k) % count) for i in range(count)])]
    broadcast_in_dim x0 -> x23, local copies, waits for them, and re-layouts: none -> 15.3 us  [the longest x22 15.2 us: by_adapter(): jnp.where(place == at, x.reshape(share, 1, part, width), 0.0)]
    slice x7 -> x12, local copies, waits for them, and re-layouts: 7.07 us -> 18.7 us  [the longest x1 4.87 us: shards(): d_out_all = d_out[:, :MODEL_WIDTH]]
    dot_general x26 -> x33, matrix products: 88.8 us -> 95.9 us  [dot(): return lax.dot_general(a, b, (dims, ((), ())), preferred_element_type=F32)]
    ppermute x7 -> x13, starting transfers between devices: 8.35 us -> 15 us  [shift(): return lax.ppermute(x, axis, [(i, (i + k) % count) for i in range(count)])]
    unnamed x174 -> x191, local copies, waits for them, and re-layouts: 19.6 us -> 24.8 us
    pallas_call x2 -> x4, Pallas kernels: 133 us -> 134 us  [the longest x3 111 us: run_experts(): pl.pallas_call(functools.partial(expert_kernel, tuple(starts), rows, hidd...]
  transfers between devices with their start and end apart: 36 -> 50, of which waited for: 17 -> 16; matrix products, arithmetic and copies ran while one was open for 26% -> 39% of each run, Pallas kernels for 4% -> 21%
where the time goes in v2:
time: 662 us; the launch traced here: 652 us
  Pallas kernels  162 us (24%)
  waiting for transfers between devices  159 us (24%)
  local copies, waits for them, and re-layouts  126 us (19%)
  matrix products  95.9 us (14%)
  other arithmetic  60.1 us (9%)
  starting transfers between devices  32.6 us (5%)
  between operations  16.2 us (2%)
    ppermute x13, waiting for transfers between devices, shift(): return lax.ppermute(x, axis, [(i, (i + k) % count) for i in range(count)])  116 us
    pallas_call x3, Pallas kernels, run_experts(): pl.pallas_call(functools.partial(expert_kernel, tuple(starts), rows, hidd...  111 us
    dot_general x33, matrix products, dot(): return lax.dot_general(a, b, (dims, ((), ())), preferred_element_type=F32)  95.9 us
    ppermute x11, waiting for transfers between devices, shift_chip(): return lax.ppermute(x, 'seq', pairs)  40.5 us
    pallas_call x1, Pallas kernels, attend_back(): pl.pallas_call(attend_back_kernel, grid=(kv, blocks), in_specs=[q_spec, k...  27.9 us
    unnamed x191, local copies, waits for them, and re-layouts  24.8 us
    pallas_call x1, Pallas kernels, attend(): pl.pallas_call(functools.partial(attend_kernel, prompt_len // block), gri...  22.9 us
    dynamic_update_slice x12, local copies, waits for them, and re-layouts, gather_seq(): out = lax.dynamic_update_slice_in_dim(out, piece[None], at, 0)  20 us
  transfers between devices with their start and end apart: 50, of which 16 were waited for; matrix products, arithmetic and copies ran while one was open for 39% of the time, Pallas kernels for 21%

profile of v2, /device:TPU:0, one launch (start us, length us, event | category | flops | bytes accessed | tf_op | source)
XLA Modules:
  0.0 651.8 jit_solution(905923169431063490)
XLA Ops:
  56.9 3.3 fusion.3
  60.9 5.6 fusion.5
  66.5 3.8 convolution_convert_fusion.3
  76.7 48.6 %collective-permute-done.10.refs_2_.refs_7_ = bf16[5,576,512]{2,1,0:T(8,128)(2,1)} collective-permute-done((bf16[5,576,512]{2,1,0:T(8,128)(2,1)}, bf16[5,576,512]{2,1,0:T(8,128)(2,1)}, u32[]{:S(2)}, u32[]{:S(2)}) %collective-permute-start.10) | collective-permute-done | bytes 2949152 | tf_op jit(solution)/shard_map/ppermute | solution.py:119
  129.6 7.7 %convolution_add_fusion = f32[640,1536]{1,0:T(8,128)S(1)} fusion(f32[640,1536]{1,0:T(8,128)} %fusion.146, bf16[1536,768]{1,0:T(8,128)(2,1)} %all-gather.5.cloned.1.call-done, bf16[1536,1536]{1,0:T(8,128)(2,1)} %bitcast.4, f32[1536]{0:T(1024)S(1)} %convert_element_type.214, f32[1536]{0:T(1024)S(1)} %rsqrt.33), kind=kOutput, calls=%fused_computation.17 | convolution fusion | flops 3030319104 | bytes 14561280 | tf_op jit(solution)/shard_map/dot_general | solution.py:34
  139.3 22.9 %shard_map.310 = (bf16[2,3,64,1536]{3,2,1,0:T(8,128)(2,1)S(1)}, bf16[2,4,1536,1152]{3,2,1,0:T(8,128)(2,1)}, f32[2,4,1,1152]{3,2,1,0:T(1,128)S(1)}) custom-call(bf16[2,3,64,1536]{3,2,1,0:T(8,128)(2,1)S(1)} %maximum_multiply_fusion.q_ref, bf16[2,64,1536]{2,1,0:T(8,128)(2,1)S(1)} %pad_maximum_fusion.2.k_ref, bf16[2,64,1536]{2,1,0:T(8,128)(2,1)S(1)} %bitcast.332, ...), custom_call_target="tpu_custom_call" | custom-call | flops 1811939328 | bytes 28311552 | tf_op jit(solution)/shard_map/pallas_call | solution.py:182
  176.3 3.7 convolution_convert_fusion.5
  179.9 10.7 %collective-permute-done.4 = bf16[384,1536]{1,0:T(8,128)(2,1)} collective-permute-done((bf16[384,1536]{1,0:T(8,128)(2,1)S(1)}, bf16[384,1536]{1,0:T(8,128)(2,1)}, u32[]{:S(2)}, u32[]{:S(2)}) %collective-permute-start.4) | collective-permute-done | bytes 1179680 | tf_op jit(solution)/shard_map/ppermute | solution.py:52
  192.4 4.9 slice.335.dy_ref
  200.1 10.3 %collective-permute-done.12.refs_4_.refs_9_ = bf16[5,576,512]{2,1,0:T(8,128)(2,1)} collective-permute-done((bf16[5,576,512]{2,1,0:T(8,128)(2,1)}, bf16[5,576,512]{2,1,0:T(8,128)(2,1)}, u32[]{:S(2)}, u32[]{:S(2)}) %collective-permute-start.12) | collective-permute-done | bytes 2949152 | tf_op jit(solution)/shard_map/ppermute | solution.py:119
  220.2 5.8 fusion.74
  226.0 19.7 %multiply_reduce_fusion = (f32[1536]{0:T(1024)S(1)}, f32[1536,1536]{1,0:T(8,128)}) fusion(f32[1536,1536]{1,0:T(8,128)} %fusion.74, bf16[1536,1536]{1,0:T(8,128)(2,1)S(1)} %bitcast.340, bf16[1536,768]{1,0:T(8,128)(2,1)} %collective-permute-done.6, bf16[1536,768]{1,0:T(8,128)(2,1)} %all-gather.7.cloned.1.call-done, pred[]{:T(512)S(6)} %eq.185, ...), kind=kOutput, calls=%fused_computation.12 | convolution fusion | flops 7280785920 | bytes 33036288 | tf_op jit(solution)/shard_map/dot_general | solution.py:34
  245.8 15.0 %collective-permute-done.14.refs_6_ = bf16[3,576,512]{2,1,0:T(8,128)(2,1)} collective-permute-done((bf16[3,576,512]{2,1,0:T(8,128)(2,1)}, bf16[3,576,512]{2,1,0:T(8,128)(2,1)}, u32[]{:S(2)}, u32[]{:S(2)}) %collective-permute-start.14) | collective-permute-done | bytes 1769504 | tf_op jit(solution)/shard_map/ppermute | solution.py:119
  260.8 16.5 %collective-permute-done.15.refs_5_.refs_10_ = bf16[5,576,512]{2,1,0:T(8,128)(2,1)} collective-permute-done((bf16[5,576,512]{2,1,0:T(8,128)(2,1)}, bf16[5,576,512]{2,1,0:T(8,128)(2,1)}, u32[]{:S(2)}, u32[]{:S(2)}) %collective-permute-start.15) | collective-permute-done | bytes 2949152 | tf_op jit(solution)/shard_map/ppermute | solution.py:119
  278.8 4.6 multiply_convert_fusion.x_ref
  295.1 3.5 convolution_convert_fusion.zbias_ref
  299.1 20.0 %collective-permute-done.16.refs_7_ = bf16[3,576,512]{2,1,0:T(8,128)(2,1)} collective-permute-done((bf16[3,576,512]{2,1,0:T(8,128)(2,1)}, bf16[3,576,512]{2,1,0:T(8,128)(2,1)}, u32[]{:S(2)}, u32[]{:S(2)}) %collective-permute-start.16) | collective-permute-done | bytes 1769504 | tf_op jit(solution)/shard_map/ppermute | solution.py:119
  319.1 58.0 %shard_map.311 = (bf16[1536,1536]{1,0:T(8,128)(2,1)}, bf16[1536,1536]{1,0:T(8,128)(2,1)}, f32[1536,128]{1,0:T(8,128)}, bf16[1536,512]{1,0:T(8,128)(2,1)}, bf16[1536,1024]{1,0:T(8,128)(2,1)}) custom-call(s32[10]{0:T(128)} %stack.126.place_ref, bf16[1536,1536]{1,0:T(8,128)(2,1)} %copy-done.11, bf16[1536,1536]{1,0:T(8,128)(2,1)} %slice.335.dy_ref, ...), custom_call_target="tpu_custom_call" | custom-call | flops 43486543872 | bytes 23592960 | tf_op jit(solution)/shard_map/pallas_call | solution.py:410
  377.2 26.4 %shard_map.312 = (bf16[768,1536]{1,0:T(8,128)(2,1)}, bf16[768,1664]{1,0:T(8,128)(2,1)}, f32[768,128]{1,0:T(8,128)}, bf16[768,512]{1,0:T(8,128)(2,1)}, bf16[768,1024]{1,0:T(8,128)(2,1)}) custom-call(s32[10]{0:T(128)} %stack.124.place_ref, bf16[1536,1536]{1,0:T(8,128)(2,1)} %copy-done.11, bf16[1536,1536]{1,0:T(8,128)(2,1)} %slice.335.dy_ref, ...), custom_call_target="tpu_custom_call" | custom-call | flops 14495514624 | bytes 11796480 | tf_op jit(solution)/shard_map/pallas_call | solution.py:410
  427.9 26.8 %shard_map.313 = (bf16[768,1536]{1,0:T(8,128)(2,1)}, bf16[768,1664]{1,0:T(8,128)(2,1)}, f32[768,128]{1,0:T(8,128)}, bf16[768,512]{1,0:T(8,128)(2,1)}, bf16[768,1024]{1,0:T(8,128)(2,1)}) custom-call(s32[10]{0:T(128)} %stack.122.place_ref, bf16[1536,1536]{1,0:T(8,128)(2,1)} %copy-done.11, bf16[1536,1536]{1,0:T(8,128)(2,1)} %slice.335.dy_ref, ...), custom_call_target="tpu_custom_call" | custom-call | flops 14495514624 | bytes 11796480 | tf_op jit(solution)/shard_map/pallas_call | solution.py:410
  454.7 3.7 collective-permute-done.20
  473.2 3.4 multiply_reduce_fusion.2
  487.3 7.9 %fusion.6 = bf16[1536,384]{1,0:T(8,128)(2,1)S(1)} fusion(f32[1536,384]{1,0:T(8,128)} %fusion.76, bf16[1536,768]{1,0:T(8,128)(2,1)} %collective-permute-done.6, bf16[1536,768]{1,0:T(8,128)(2,1)} %all-gather.7.cloned.1.call-done, pred[]{:T(512)S(6)} %eq.185, f32[384,1536]{1,0:T(8,128)} %copy-done.8), kind=kOutput, calls=%fused_computation.24 | convolution fusion | flops 1834942464 | bytes 10616833 | tf_op jit(solution)/shard_map/dot_general | solution.py:34
  505.7 5.8 collective-permute-done.26
  518.2 3.7 convolution_add_fusion.1
  525.9 27.9 %shard_map.314 = (bf16[2,3,64,1536]{3,2,1,0:T(8,128)(2,1)S(1)}, bf16[2,64,1536]{2,1,0:T(8,128)(2,1)S(1)}, bf16[2,64,1536]{2,1,0:T(8,128)(2,1)S(1)}) custom-call(bf16[2,3,64,1536]{3,2,1,0:T(8,128)(2,1)S(1)} %copy-done.2, bf16[2,64,1536]{2,1,0:T(8,128)(2,1)S(1)} %pad_maximum_fusion.2.k_ref, bf16[2,64,1536]{2,1,0:T(8,128)(2,1)S(1)} %bitcast.333, ...), custom_call_target="tpu_custom_call" | custom-call | flops 3623878656 | bytes 28311552 | tf_op jit(solution)/shard_map/pallas_call | solution.py:268
  555.8 3.9 fusion.32
  570.1 3.6 fusion.27
  576.3 3.4 collective-permute-done.32
  595.5 4.3 collective-permute-done.39
  617.0 10.6 %collective-permute-done.42 = f32[40,1536]{1,0:T(8,128)} collective-permute-done((f32[40,1536]{1,0:T(8,128)}, f32[40,1536]{1,0:T(8,128)}, u32[]{:S(2)}, u32[]{:S(2)}) %collective-permute-start.42) | collective-permute-done | bytes 245792 | tf_op jit(solution)/shard_map/ppermute | solution.py:52
  627.6 4.0 fusion.13
  (482 shorter events, 235.7 us)
Async XLA Ops:
  7.2 122.4 %all-gather.5.cloned.1.call-start = ((), (), s32[]{:S(2)}) async-start(), calls=%async_computation | async-start | bytes 2654208 | tf_op jit(solution)/shard_map/all_gather | solution.py:565
  10.8 163.0 %all-gather.7.cloned.1.call-start = ((), (), s32[]{:S(2)}) async-start(), calls=%async_computation.1 | async-start | bytes 2654208 | tf_op jit(solution)/shard_map/all_gather | solution.py:565
  10.8 36.6 %collective-permute-start = (bf16[384,1536]{1,0:T(8,128)(2,1)}, bf16[384,1536]{1,0:T(8,128)(2,1)}, u32[]{:S(2)}, u32[]{:S(2)}) collective-permute-start(bf16[384,1536]{1,0:T(8,128)(2,1)} %bitcast.347), channel_id=1, source_target_pairs={{0,4},{4,0},{8,12},{12,8},{1,5},{5,1},{9,13},{13,9},{2,6},{6,2},{1... | collective-permute-start | bytes 3538952 | tf_op jit(solution)/shard_map/ppermute | solution.py:46
  11.4 29.5 %collective-permute-start.1 = (bf16[384,1536]{1,0:T(8,128)(2,1)}, bf16[384,1536]{1,0:T(8,128)(2,1)}, u32[]{:S(2)}, u32[]{:S(2)}) collective-permute-start(bf16[384,1536]{1,0:T(8,128)(2,1)} %bitcast.348), channel_id=1, source_target_pairs={{0,8},{4,12},{8,0},{12,4},{1,9},{5,13},{9,1},{13,5},{2,10},{6,14},... | collective-permute-start | bytes 3538952 | tf_op jit(solution)/shard_map/ppermute | solution.py:52
  19.5 105.8 %collective-permute-start.10 = (bf16[5,576,512]{2,1,0:T(8,128)(2,1)}, bf16[5,576,512]{2,1,0:T(8,128)(2,1)}, u32[]{:S(2)}, u32[]{:S(2)}) collective-permute-start(bf16[5,576,512]{2,1,0:T(8,128)(2,1)} %slice_dynamic-update-slice_fusion.2.refs_0_.refs_5_), channel_id=1, source_target_pairs={{0,1},{1,2},{2,3},{3,0},{4,5},{5,6},{6,7},{7,4},{8,9},{9,10},{10,1... | collective-permute-start | bytes 8847368 | tf_op jit(solution)/shard_map/ppermute | solution.py:119
  21.1 104.2 %collective-permute-start.11 = (bf16[5,576,512]{2,1,0:T(8,128)(2,1)}, bf16[5,576,512]{2,1,0:T(8,128)(2,1)}, u32[]{:S(2)}, u32[]{:S(2)}) collective-permute-start(bf16[5,576,512]{2,1,0:T(8,128)(2,1)} %slice_dynamic-update-slice_fusion.2.refs_0_.refs_5_), channel_id=1, source_target_pairs={{0,16},{16,0},{1,17},{17,1},{2,18},{18,2},{3,19},{19,3},{4,20},{20... | collective-permute-start | bytes 8847368 | tf_op jit(solution)/shard_map/ppermute | solution.py:119
  24.3 577.8 %all-gather.9.cloned.1.call-start = ((), (), s32[]{:S(2)}) async-start(), calls=%async_computation.2 | async-start | bytes 2211840 | tf_op jit(solution)/shard_map/all_gather | solution.py:722
  54.8 72.3 %collective-permute-start.7 = (bf16[384,1664]{1,0:T(8,128)(2,1)S(1)}, bf16[384,1664]{1,0:T(8,128)(2,1)}, u32[]{:S(2)}, u32[]{:S(2)}) collective-permute-start(bf16[384,1664]{1,0:T(8,128)(2,1)S(1)} %copy-done.26), channel_id=1, source_target_pairs={{0,4},{4,0},{8,12},{12,8},{1,5},{5,1},{9,13},{13,9},{2,6},{6,2},{1... | collective-permute-start | bytes 3833864 | tf_op jit(solution)/shard_map/ppermute | solution.py:46
  55.3 71.8 %collective-permute-start.8 = (bf16[384,1664]{1,0:T(8,128)(2,1)S(1)}, bf16[384,1664]{1,0:T(8,128)(2,1)}, u32[]{:S(2)}, u32[]{:S(2)}) collective-permute-start(bf16[384,1664]{1,0:T(8,128)(2,1)S(1)} %copy-done.26), channel_id=1, source_target_pairs={{0,8},{4,12},{8,0},{12,4},{1,9},{5,13},{9,1},{13,5},{2,10},{6,14},... | collective-permute-start | bytes 3833864 | tf_op jit(solution)/shard_map/ppermute | solution.py:52
  125.3 85.1 %collective-permute-start.12 = (bf16[5,576,512]{2,1,0:T(8,128)(2,1)}, bf16[5,576,512]{2,1,0:T(8,128)(2,1)}, u32[]{:S(2)}, u32[]{:S(2)}) collective-permute-start(bf16[5,576,512]{2,1,0:T(8,128)(2,1)} %collective-permute-done.10.refs_2_.refs_7_), channel_id=1, source_target_pairs={{0,1},{1,2},{2,3},{3,0},{4,5},{5,6},{6,7},{7,4},{8,9},{9,10},{10,1... | collective-permute-start | bytes 8847368 | tf_op jit(solution)/shard_map/ppermute | solution.py:119
  125.5 84.9 %collective-permute-start.13 = (bf16[5,576,512]{2,1,0:T(8,128)(2,1)}, bf16[5,576,512]{2,1,0:T(8,128)(2,1)}, u32[]{:S(2)}, u32[]{:S(2)}) collective-permute-start(bf16[5,576,512]{2,1,0:T(8,128)(2,1)} %collective-permute-done.10.refs_2_.refs_7_), channel_id=1, source_target_pairs={{0,16},{16,0},{1,17},{17,1},{2,18},{18,2},{3,19},{19,3},{4,20},{20... | collective-permute-start | bytes 8847368 | tf_op jit(solution)/shard_map/ppermute | solution.py:119
  127.1 46.7 %collective-permute-start.9 = (bf16[384,1664]{1,0:T(8,128)(2,1)}, bf16[384,1664]{1,0:T(8,128)(2,1)}, u32[]{:S(2)}, u32[]{:S(2)}) collective-permute-start(bf16[384,1664]{1,0:T(8,128)(2,1)} %collective-permute-done.8), channel_id=1, source_target_pairs={{0,4},{4,0},{8,12},{12,8},{1,5},{5,1},{9,13},{13,9},{2,6},{6,2},{1... | collective-permute-start | bytes 3833864 | tf_op jit(solution)/shard_map/ppermute | solution.py:46
  162.1 28.5 %collective-permute-start.4 = (bf16[384,1536]{1,0:T(8,128)(2,1)S(1)}, bf16[384,1536]{1,0:T(8,128)(2,1)}, u32[]{:S(2)}, u32[]{:S(2)}) collective-permute-start(bf16[384,1536]{1,0:T(8,128)(2,1)S(1)} %bitcast.328), channel_id=1, source_target_pairs={{0,8},{4,12},{8,0},{12,4},{1,9},{5,13},{9,1},{13,5},{2,10},{6,14},... | collective-permute-start | bytes 3538952 | tf_op jit(solution)/shard_map/ppermute | solution.py:52
  164.9 32.4 %collective-permute-start.3 = (bf16[384,1536]{1,0:T(8,128)(2,1)S(1)}, bf16[384,1536]{1,0:T(8,128)(2,1)}, u32[]{:S(2)}, u32[]{:S(2)}) collective-permute-start(bf16[384,1536]{1,0:T(8,128)(2,1)S(1)} %bitcast.329), channel_id=1, source_target_pairs={{0,4},{4,0},{8,12},{12,8},{1,5},{5,1},{9,13},{13,9},{2,6},{6,2},{1... | collective-permute-start | bytes 3538952 | tf_op jit(solution)/shard_map/ppermute | solution.py:46
  173.8 52.2 %collective-permute-start.6 = (bf16[1536,768]{1,0:T(8,128)(2,1)}, bf16[1536,768]{1,0:T(8,128)(2,1)}, u32[]{:S(2)}, u32[]{:S(2)}) collective-permute-start(bf16[1536,768]{1,0:T(8,128)(2,1)} %all-gather.7.cloned.1.call-done), channel_id=1, source_target_pairs={{0,4},{4,0},{8,12},{12,8},{1,5},{5,1},{9,13},{13,9},{2,6},{6,2},{1... | collective-permute-start | bytes 7077896 | tf_op jit(solution)/shard_map/ppermute | solution.py:46
  190.6 27.9 %collective-permute-start.5 = (bf16[384,1536]{1,0:T(8,128)(2,1)}, bf16[384,1536]{1,0:T(8,128)(2,1)S(1)}, u32[]{:S(2)}, u32[]{:S(2)}) collective-permute-start(bf16[384,1536]{1,0:T(8,128)(2,1)} %collective-permute-done.4), channel_id=1, source_target_pairs={{0,4},{4,0},{8,12},{12,8},{1,5},{5,1},{9,13},{13,9},{2,6},{6,2},{1... | collective-permute-start | bytes 3538952 | tf_op jit(solution)/shard_map/ppermute | solution.py:46
  213.2 64.1 %collective-permute-start.15 = (bf16[5,576,512]{2,1,0:T(8,128)(2,1)}, bf16[5,576,512]{2,1,0:T(8,128)(2,1)}, u32[]{:S(2)}, u32[]{:S(2)}) collective-permute-start(bf16[5,576,512]{2,1,0:T(8,128)(2,1)} %collective-permute-done.12.refs_4_.refs_9_), channel_id=1, source_target_pairs={{0,16},{16,0},{1,17},{17,1},{2,18},{18,2},{3,19},{19,3},{4,20},{20... | collective-permute-start | bytes 8847368 | tf_op jit(solution)/shard_map/ppermute | solution.py:119
  217.1 43.7 %collective-permute-start.14 = (bf16[3,576,512]{2,1,0:T(8,128)(2,1)}, bf16[3,576,512]{2,1,0:T(8,128)(2,1)}, u32[]{:S(2)}, u32[]{:S(2)}) collective-permute-start(bf16[3,576,512]{2,1,0:T(8,128)(2,1)} %slice.297), channel_id=1, source_target_pairs={{0,1},{1,2},{2,3},{3,0},{4,5},{5,6},{6,7},{7,4},{8,9},{9,10},{10,1... | collective-permute-start | bytes 5308424 | tf_op jit(solution)/shard_map/ppermute | solution.py:119
  217.1 81.5 %collective-permute-start.17 = (bf16[2,576,512]{2,1,0:T(8,128)(2,1)}, bf16[2,576,512]{2,1,0:T(8,128)(2,1)}, u32[]{:S(2)}, u32[]{:S(2)}) collective-permute-start(bf16[2,576,512]{2,1,0:T(8,128)(2,1)} %slice.298), channel_id=1, source_target_pairs={{0,1},{1,2},{2,3},{3,0},{4,5},{5,6},{6,7},{7,4},{8,9},{9,10},{10,1... | collective-permute-start | bytes 3538952 | tf_op jit(solution)/shard_map/ppermute | solution.py:119
  277.3 41.9 %collective-permute-start.16 = (bf16[3,576,512]{2,1,0:T(8,128)(2,1)}, bf16[3,576,512]{2,1,0:T(8,128)(2,1)}, u32[]{:S(2)}, u32[]{:S(2)}) collective-permute-start(bf16[3,576,512]{2,1,0:T(8,128)(2,1)} %collective-permute-done.14.refs_6_), channel_id=1, source_target_pairs={{0,16},{16,0},{1,17},{17,1},{2,18},{18,2},{3,19},{19,3},{4,20},{20... | collective-permute-start | bytes 5308424 | tf_op jit(solution)/shard_map/ppermute | solution.py:119
  298.6 78.5 %collective-permute-start.18 = (bf16[2,576,512]{2,1,0:T(8,128)(2,1)}, bf16[2,576,512]{2,1,0:T(8,128)(2,1)}, u32[]{:S(2)}, u32[]{:S(2)}) collective-permute-start(bf16[2,576,512]{2,1,0:T(8,128)(2,1)} %collective-permute-done.17.refs_11_), channel_id=1, source_target_pairs={{0,16},{16,0},{1,17},{17,1},{2,18},{18,2},{3,19},{19,3},{4,20},{20... | collective-permute-start | bytes 3538952 | tf_op jit(solution)/shard_map/ppermute | solution.py:119
  406.1 18.4 %collective-permute-start.19 = (bf16[384,1664]{1,0:T(8,128)(2,1)}, bf16[384,1664]{1,0:T(8,128)(2,1)}, u32[]{:S(2)}, u32[]{:S(2)}) collective-permute-start(bf16[384,1664]{1,0:T(8,128)(2,1)} %dynamic-slice_bitcast_fusion.1), channel_id=1, source_target_pairs={{0,4},{4,0},{8,12},{12,8},{1,5},{5,1},{9,13},{13,9},{2,6},{6,2},{1... | collective-permute-start | bytes 3833864 | tf_op jit(solution)/shard_map/ppermute | solution.py:46
  427.6 30.8 %collective-permute-start.20 = (bf16[384,1664]{1,0:T(8,128)(2,1)}, bf16[384,1664]{1,0:T(8,128)(2,1)}, u32[]{:S(2)}, u32[]{:S(2)}) collective-permute-start(bf16[384,1664]{1,0:T(8,128)(2,1)} %fusion.8), channel_id=1, source_target_pairs={{0,8},{4,12},{8,0},{12,4},{1,9},{5,13},{9,1},{13,5},{2,10},{6,14},... | collective-permute-start | bytes 3833864 | tf_op jit(solution)/shard_map/ppermute | solution.py:52
  461.1 39.6 %collective-permute-start.29 = (bf16[384,1536]{1,0:T(8,128)(2,1)}, bf16[384,1536]{1,0:T(8,128)(2,1)}, u32[]{:S(2)}, u32[]{:S(2)}) collective-permute-start(bf16[384,1536]{1,0:T(8,128)(2,1)} %dynamic-slice_bitcast_fusion.4), channel_id=1, source_target_pairs={{0,4},{4,0},{8,12},{12,8},{1,5},{5,1},{9,13},{13,9},{2,6},{6,2},{1... | collective-permute-start | bytes 3538952 | tf_op jit(solution)/shard_map/ppermute | solution.py:46
  495.3 16.3 %collective-permute-start.26 = (bf16[2,384,384]{2,1,0:T(8,128)(2,1)S(1)}, bf16[2,384,384]{2,1,0:T(8,128)(2,1)S(1)}, u32[]{:S(2)}, u32[]{:S(2)}) collective-permute-start(bf16[2,384,384]{2,1,0:T(8,128)(2,1)S(1)} %dynamic-slice_bitcast_fusion.6), channel_id=1, source_target_pairs={{0,8},{4,12},{8,0},{12,4},{1,9},{5,13},{9,1},{13,5},{2,10},{6,14},... | collective-permute-start | bytes 1769480 | tf_op jit(solution)/shard_map/ppermute | solution.py:52
  516.1 37.7 %collective-permute-start.30 = (bf16[384,1536]{1,0:T(8,128)(2,1)}, bf16[384,1536]{1,0:T(8,128)(2,1)}, u32[]{:S(2)}, u32[]{:S(2)}) collective-permute-start(bf16[384,1536]{1,0:T(8,128)(2,1)} %fusion.19), channel_id=1, source_target_pairs={{0,8},{4,12},{8,0},{12,4},{1,9},{5,13},{9,1},{13,5},{2,10},{6,14},... | collective-permute-start | bytes 3538952 | tf_op jit(solution)/shard_map/ppermute | solution.py:52
  518.2 71.7 %collective-permute-start.22 = (bf16[384,1536]{1,0:T(8,128)(2,1)}, bf16[384,1536]{1,0:T(8,128)(2,1)}, u32[]{:S(2)}, u32[]{:S(2)}) collective-permute-start(bf16[384,1536]{1,0:T(8,128)(2,1)} %dynamic-slice_bitcast_fusion.5), channel_id=1, source_target_pairs={{0,4},{4,0},{8,12},{12,8},{1,5},{5,1},{9,13},{13,9},{2,6},{6,2},{1... | collective-permute-start | bytes 3538952 | tf_op jit(solution)/shard_map/ppermute | solution.py:46
  585.0 28.4 %collective-permute-start.36 = (bf16[384,1536]{1,0:T(8,128)(2,1)}, bf16[384,1536]{1,0:T(8,128)(2,1)}, u32[]{:S(2)}, u32[]{:S(2)}) collective-permute-start(bf16[384,1536]{1,0:T(8,128)(2,1)} %dynamic-slice_bitcast_fusion.2), channel_id=1, source_target_pairs={{0,4},{4,0},{8,12},{12,8},{1,5},{5,1},{9,13},{13,9},{2,6},{6,2},{1... | collective-permute-start | bytes 3538952 | tf_op jit(solution)/shard_map/ppermute | solution.py:46
  585.1 29.1 %collective-permute-start.35 = (bf16[384,1536]{1,0:T(8,128)(2,1)}, bf16[384,1536]{1,0:T(8,128)(2,1)}, u32[]{:S(2)}, u32[]{:S(2)}) collective-permute-start(bf16[384,1536]{1,0:T(8,128)(2,1)} %fusion.18), channel_id=1, source_target_pairs={{0,8},{4,12},{8,0},{12,4},{1,9},{5,13},{9,1},{13,5},{2,10},{6,14},... | collective-permute-start | bytes 3538952 | tf_op jit(solution)/shard_map/ppermute | solution.py:52
  608.4 25.5 %collective-permute-start.45 = (f32[64,1536]{1,0:T(8,128)S(1)}, f32[64,1536]{1,0:T(8,128)}, u32[]{:S(2)}, u32[]{:S(2)}) collective-permute-start(f32[64,1536]{1,0:T(8,128)S(1)} %bitcast.364), channel_id=1, source_target_pairs={{0,8},{4,12},{8,0},{12,4},{1,9},{5,13},{9,1},{13,5},{2,10},{6,14},... | collective-permute-start | bytes 1179656 | tf_op jit(solution)/shard_map/ppermute | solution.py:52
  609.1 30.6 %collective-permute-start.44 = (f32[64,1536]{1,0:T(8,128)S(1)}, f32[64,1536]{1,0:T(8,128)}, u32[]{:S(2)}, u32[]{:S(2)}) collective-permute-start(f32[64,1536]{1,0:T(8,128)S(1)} %bitcast.365), channel_id=1, source_target_pairs={{0,4},{4,0},{8,12},{12,8},{1,5},{5,1},{9,13},{13,9},{2,6},{6,2},{1... | collective-permute-start | bytes 1179656 | tf_op jit(solution)/shard_map/ppermute | solution.py:46
  613.4 18.2 %collective-permute-start.41 = (f32[40,1536]{1,0:T(8,128)}, f32[40,1536]{1,0:T(8,128)}, u32[]{:S(2)}, u32[]{:S(2)}) collective-permute-start(f32[40,1536]{1,0:T(8,128)} %reshape.969), channel_id=1, source_target_pairs={{0,4},{4,0},{8,12},{12,8},{1,5},{5,1},{9,13},{13,9},{2,6},{6,2},{1... | collective-permute-start | bytes 737288 | tf_op jit(solution)/shard_map/ppermute | solution.py:46
  (107 other events, 848.2 us)
Sparse Core Ops, SparseCore 0:
  10.9 83.8 all-gather.4
  97.5 76.2 all-gather.6
  522.8 47.4 all-gather.8

commit v3 on v2

--- a/solution.py
+++ b/solution.py
@@ -26,6 +26,7 @@
 F32 = jnp.float32
 BF16 = jnp.bfloat16
 FIRST_EXPERTS = 3
+HOLD = 1
 TILE = 256
 DOWN_AT = 80
 
@@ -297,18 +298,20 @@
 
 
 def pack_experts(gate_up, down):
+    count, _, _ = gate_up.shape
+    rows = down.shape[1]
     parts = [gate_up[..., :HIDDEN], gate_up[..., HIDDEN:]]
     parts += [down[..., m : m + HIDDEN] for m in range(0, MODEL_WIDTH, HIDDEN)]
-    return jnp.concatenate(parts, axis=1)
+    return jnp.concatenate(parts, axis=1).reshape(count, 3, 3, rows, HIDDEN)
 
 
 def expert_kernel(
-    starts, rows, hidden_rows, experts_all, first, last, place_ref, x_ref, dy_ref, gate_ref,
+    shards_count, experts_all, first, last, place_ref, x_ref, dy_ref, gate_ref,
     zbias_ref, sbias_ref, dfa_ref, back_ref, *refs,
 ):
     refs = list(refs)
     carried = [None] * 5 if first else [refs.pop(0) for _ in range(5)]
-    shards = [refs.pop(0) for _ in starts]
+    shards = [refs.pop(0) for _ in range(shards_count)]
     outs = [refs.pop(0) for _ in range(5)]
     w_up, w_down, *accs, sem = refs
     count = w_up.shape[0]
@@ -316,16 +319,9 @@
 
     def copies(e):
         pairs = []
-        for b, (start, shard) in enumerate(zip(starts, shards)):
-            index = place_ref[2 + b]
-            up_rows = pl.ds(pl.multiple_of(index * rows, rows), rows)
-            down_rows = pl.ds(pl.multiple_of(index * hidden_rows, hidden_rows), hidden_rows)
-            for m in range(2):
-                pairs.append((shard.at[start + e, pl.ds(m * rows, rows), :],
-                              w_up.at[e, up_rows, pl.ds(m * HIDDEN, HIDDEN)]))
-            for m in range(MODEL_WIDTH // HIDDEN):
-                pairs.append((shard.at[start + e, pl.ds(2 * rows + m * hidden_rows, hidden_rows), :],
-                              w_down.at[e, down_rows, pl.ds(m * HIDDEN, HIDDEN)]))
+        for b, shard in enumerate(shards):
+            pairs.append((shard.at[e, pl.ds(0, 2)], w_up.at[e, :, place_ref[2 + b]]))
+            pairs.append((shard.at[e, 2], w_down.at[e, :, place_ref[2 + b]]))
         return [pltpu.make_async_copy(a, b, sem.at[e, n]) for n, (a, b) in enumerate(pairs)]
 
     lane = lax.broadcasted_iota(jnp.int32, (tile, LANES), 1)
@@ -345,23 +341,29 @@
 
     def step(e):
         name = place_ref[0] + e
-        both = dot(x_ref[...], w_up[e]) + zbias_ref[...]
+        up_weight = jnp.concatenate(
+            [w_up[e, m].reshape(MODEL_WIDTH, HIDDEN) for m in range(2)], axis=1
+        )
+        down_weight = jnp.concatenate(
+            [w_down[e, m].reshape(HIDDEN, HIDDEN) for m in range(MODEL_WIDTH // HIDDEN)], axis=1
+        )
+        both = dot(x_ref[...], up_weight) + zbias_ref[...]
         gate_in, up = both[:, :HIDDEN], both[:, HIDDEN:]
         sigma = jax.nn.sigmoid(gate_in)
         silu = gate_in * sigma
         inner = silu * up
-        d_down = dot_nt(dy_ref[...], w_down[e]) + sbias_ref[...]
+        d_down = dot_nt(dy_ref[...], down_weight) + sbias_ref[...]
         d_gating = jnp.sum(inner * d_down, axis=1, keepdims=True)
         gating = jnp.sum(jnp.where(lane == name, gate_ref[...], 0.0), axis=1, keepdims=True)
         add(2, e, jnp.where((lane == name) | (lane == name + experts_all), d_gating, 0.0))
         gated = gating * inner
         add(3, e, gated)
-        add(0, e, dot(gated.astype(BF16), w_down[e]))
+        add(0, e, dot(gated.astype(BF16), down_weight))
         d_inner = gating * d_down
         d_gate = d_inner * up * (sigma + silu * (1.0 - sigma))
         d_both = jnp.concatenate([d_gate, d_inner * silu], axis=1)
         add(4, e, d_both)
-        add(1, e, dot_nt(d_both.astype(BF16), w_up[e]))
+        add(1, e, dot_nt(d_both.astype(BF16), up_weight))
 
     @pl.when(pl.program_id(0) == 0)
     def _():
@@ -387,9 +389,8 @@
         outs[2][...] = aux
 
 
-def run_experts(place, x, dy, gates, zbias, sbias, mats, carried, shards, starts, count, experts_all, rows_out, last):
-    rows = MODEL_WIDTH // len(shards)
-    hidden_rows = HIDDEN // len(shards)
+def run_experts(place, x, dy, gates, zbias, sbias, mats, carried, shards, experts_all, rows_out, last):
+    count, _, _, rows, _ = shards[0].shape
     first = carried is None
     acc_widths = (MODEL_WIDTH, MODEL_WIDTH, LANES, HIDDEN, 2 * HIDDEN)
     widths = (MODEL_WIDTH, MODEL_WIDTH + LANES if last else MODEL_WIDTH, *acc_widths[2:])
@@ -404,12 +405,12 @@
     in_widths = (MODEL_WIDTH, MODEL_WIDTH, LANES, 2 * HIDDEN, HIDDEN)
     specs = [tiled(w) for w in in_widths]
     specs += [pl.BlockSpec(m.shape, lambda t, _: (0, 0)) for m in mats]
-    specs += [] if first else [tiled(w) for w in acc_widths]
+    specs += [] if first else [out_tiled(w) for w in acc_widths]
     specs += [pl.BlockSpec(memory_space=pl.ANY)] * len(shards)
-    copies = len(shards) * (2 + MODEL_WIDTH // HIDDEN)
+    copies = len(shards) * 2
     return pl.pallas_call(
         functools.partial(
-            expert_kernel, tuple(starts), rows, hidden_rows, experts_all, first, last
+            expert_kernel, len(shards), experts_all, first, last
         ),
         grid_spec=pltpu.PrefetchScalarGridSpec(
             num_scalar_prefetch=1,
@@ -417,8 +418,8 @@
             in_specs=specs,
             out_specs=[out_tiled(w) for w in widths],
             scratch_shapes=[
-                pltpu.VMEM((count, MODEL_WIDTH, 2 * HIDDEN), BF16),
-                pltpu.VMEM((count, HIDDEN, MODEL_WIDTH), BF16),
+                pltpu.VMEM((count, 2, len(shards), 3, rows, HIDDEN), BF16),
+                pltpu.VMEM((count, 3, len(shards), rows, HIDDEN), BF16),
                 *[pltpu.VMEM((TILE, w), F32) for w in acc_widths],
                 pltpu.SemaphoreType.DMA((count, copies)),
             ],
@@ -548,16 +549,31 @@
     def across(x):
         return [shift(x, "dp", n_dp, k) for k in range(1, n_dp)]
 
-    came = pack_experts(expert_gate_up_weight, expert_down_weight)
-    pieces = [(0, 0, came)]
-    for b in range(1, n_wt - 1):
-        came, *moved = tie((shift(came, "wt", n_wt, 1), *across(came)))
-        pieces += [(k, b - 1, x) for k, x in enumerate(moved, 1)] + [(0, b, came)]
-    ahead, *moved = tie((shift(came[:split], "wt", n_wt, 1), *across(came)))
-    pieces += [(k, n_wt - 2, x) for k, x in enumerate(moved, 1)]
-    behind = shift(came[split:], "wt", n_wt, 1)
-    ahead = [ahead, *across(ahead)]
-    behind = [behind, *across(behind)]
+    class Ring:
+        def __init__(self, packed, begin):
+            self.pieces, self.steps = [packed], 0
+            self.came, self.moved = shift(begin, "wt", n_wt, 1), across(packed)
+
+        def advance(self, gate=None):
+            if self.steps == n_wt - 1:
+                return
+            self.steps += 1
+            self.came, *self.moved, _ = tie((self.came, *self.moved, 0 if gate is None else gate))
+            self.pieces += [*self.moved, self.came]
+            self.moved = across(self.came)
+            self.came = shift(self.came, "wt", n_wt, 1) if self.steps < n_wt - 1 else self.came
+
+        def finish(self):
+            while self.steps < n_wt - 1:
+                self.advance()
+            return self.pieces + self.moved
+
+    order = [(0, 0)]
+    for b in range(n_wt - 1):
+        order += [(k, b) for k in range(1, n_dp)] + [(0, b + 1)]
+    order += [(k, n_wt - 1) for k in range(1, n_dp)]
+    ahead = pack_experts(expert_gate_up_weight[:split], expert_down_weight[:split])
+    ahead = Ring(ahead, ahead)
 
     hidden = gather_seq(tokens[0], n_seq).reshape(total, MODEL_WIDTH)
 
@@ -598,6 +614,10 @@
     second = second.at[rank : 2 * rank, q_width : q_width + k_width].set(own(kv_second[0], k_width))
     second = second.at[2 * rank :, q_width + k_width :].set(own(kv_second[1], k_width))
     qkv = dot(qkv_weight, normed, ((0,), (1,))) + dot(second, small_a, ((0,), (1,)))
+    ahead.advance(normed)
+    behind = pack_experts(expert_gate_up_weight[split:], expert_down_weight[split:])
+    begin, _ = tie((behind, ahead.pieces[-1]))
+    behind = Ring(behind, begin)
     segment, position = layout(lengths[0], prompt_len, total)
     freq = jnp.exp(jnp.arange(HEAD // 2, dtype=F32) * (-2.0 * math.log(10000.0) / HEAD))
     angle = freq[:, None] * position.astype(F32)[None, :]
@@ -613,8 +633,11 @@
     kt = rotate(qkv[q_width : q_width + k_width])
     vt = qkv[q_width + k_width :].astype(BF16).reshape(kv_local, HEAD, total)
     ot, probs, inverse_l = attend(qt, kt, vt, segment, prompt_len, local)
+    ahead.advance(ot)
     att = gather_seq(ot.reshape(q_width, total), n_seq).reshape(MODEL_WIDTH, total)
 
+    behind.advance(att)
+    ahead.advance(att)
     named = jnp.arange(LANES, dtype=jnp.int32)[None, None, :]
     mask = jnp.any(routes[0][:, :, None] == named, axis=1).astype(BF16)
     d_out = jnp.concatenate([cotangent[0], mask], axis=1)
@@ -625,8 +648,10 @@
 
     small_o = dot_tn(att, out_first).astype(BF16)
     residual = hidden_f + dot_tn(att, out_weight) + dot(small_o, out_second)
+    behind.advance(residual)
     inverse_m = lax.rsqrt(jnp.mean(residual * residual, axis=-1, keepdims=True) + EPS)
     normed_m = (residual * inverse_m * gain_second).astype(BF16)
+    ahead = ahead.finish()
     mix_router = jnp.concatenate([mix_first, router_full], axis=1)
     states = dot(normed_m, mix_router)
     small_m = states[:, : 3 * rank].astype(BF16)
@@ -645,27 +670,33 @@
     sbias = dot_nt(d_rank, down_first).astype(BF16)
     gates = pad_lanes(gating)
 
-    order = [(k, b) for k, b, _ in pieces] + [(k, n_wt - 1) for k in range(n_dp)]
     places = [(dp + n_dp - k) % n_dp * n_wt + (wt + n_wt - b) % n_wt for k, b in order]
-    held = [x for _, _, x in pieces]
 
     def place_of(expert, row):
         return jnp.stack([x.astype(jnp.int32) for x in (seq * exp_dev + expert, row, *places)])
 
-    carried = run_experts(
-        place_of(0, seq * 0), normed_m, d_out_all, gates, zbias, sbias, mats, None, held + ahead,
-        [0] * len(order), split, experts_all, total, False,
-    )
     chip_rows = 2 * local
+    firsts = []
+    for k, chip in chip_turns(n_seq):
+        firsts.append(
+            list(run_experts(
+                place_of(0, chip * (chip_rows // TILE)), normed_m, d_out_all, gates, zbias, sbias,
+                mats, None, ahead, experts_all, chip_rows, False,
+            ))
+        )
+        if len(firsts) == 1:
+            behind.advance(firsts[0][2])
+    behind = behind.finish()
     turns, arrived, waiting = [], [], None
-    for k, chip in chip_turns(n_seq):
+    firsts[0][2], _ = tie((firsts[0][2], firsts[-1][2]))
+    for (k, chip), carried in zip(chip_turns(n_seq), firsts):
         place = place_of(split, chip * (chip_rows // TILE))
         if waiting is not None:
             place, sent = tie((place, waiting[1].astype(BF16)))
             arrived.append(shift_chip(sent, n_seq, waiting[0]))
         parts = run_experts(
-            place, normed_m, d_out_all, gates, zbias, sbias, mats, carried, held + behind,
-            [split] * len(held) + [0] * len(behind), exp_dev - split, experts_all, chip_rows, True,
+            place, normed_m, d_out_all, gates, zbias, sbias, mats, carried, behind,
+            experts_all, chip_rows, True,
         )
         parts = list(parts)
         if arrived:

time: 662 us -> 625 us (0.944)
  waiting for transfers between devices: 159 us -> 100 us
  starting transfers between devices: 32.6 us -> 46.1 us
  local copies, waits for them, and re-layouts: 126 us -> 135 us
  matrix products: 95.9 us -> 88.3 us
    ppermute x13 -> x18, waiting for transfers between devices: 116 us -> 76.2 us  [shift(): return lax.ppermute(x, axis, [(i, (i + k) % count) for i in range(count)])]
    ppermute x11, waiting for transfers between devices: 40.5 us -> 23.7 us  [shift_chip(): return lax.ppermute(x, 'seq', pairs)]
    ppermute x13 -> x18, starting transfers between devices: 15 us -> 29.5 us  [shift(): return lax.ppermute(x, axis, [(i, (i + k) % count) for i in range(count)])]
    dot_general x33, matrix products: 95.9 us -> 88.3 us  [dot(): return lax.dot_general(a, b, (dims, ((), ())), preferred_element_type=F32)]
    unnamed x191 -> x193, local copies, waits for them, and re-layouts: 24.8 us -> 31.4 us
    pallas_call x3 -> x4, Pallas kernels: 111 us -> 116 us  [run_experts(): pl.pallas_call(functools.partial(expert_kernel, len(shards), experts_all,...]
  transfers between devices with their start and end apart: 50 -> 55, of which waited for: 16 -> 11; matrix products, arithmetic and copies ran while one was open for 39% -> 41% of each run, Pallas kernels for 21% -> 23%
where the time goes in v3:
time: 625 us; the launch traced here: 615 us
  Pallas kernels  166 us (27%)
  local copies, waits for them, and re-layouts  135 us (22%)
  waiting for transfers between devices  100 us (16%)
  matrix products  88.3 us (14%)
  other arithmetic  63.2 us (10%)
  starting transfers between devices  46.1 us (7%)
  between operations  16.1 us (3%)
    pallas_call x4, Pallas kernels, run_experts(): pl.pallas_call(functools.partial(expert_kernel, len(shards), experts_all,...  116 us
    dot_general x33, matrix products, dot(): return lax.dot_general(a, b, (dims, ((), ())), preferred_element_type=F32)  88.3 us
    ppermute x18, waiting for transfers between devices, shift(): return lax.ppermute(x, axis, [(i, (i + k) % count) for i in range(count)])  76.2 us
    unnamed x193, local copies, waits for them, and re-layouts  31.4 us
    ppermute x18, starting transfers between devices, shift(): return lax.ppermute(x, axis, [(i, (i + k) % count) for i in range(count)])  29.5 us
    pallas_call x1, Pallas kernels, attend_back(): pl.pallas_call(attend_back_kernel, grid=(kv, blocks), in_specs=[q_spec, k...  27.6 us
    ppermute x11, waiting for transfers between devices, shift_chip(): return lax.ppermute(x, 'seq', pairs)  23.7 us
    pallas_call x1, Pallas kernels, attend(): pl.pallas_call(functools.partial(attend_kernel, prompt_len // block), gri...  22.8 us
  transfers between devices with their start and end apart: 55, of which 11 were waited for; matrix products, arithmetic and copies ran while one was open for 41% of the time, Pallas kernels for 23%

profile of v3, /device:TPU:0, one launch (start us, length us, event | category | flops | bytes accessed | tf_op | source)
XLA Modules:
  0.0 614.7 jit_solution(14236126845467175278)
XLA Ops:
  59.4 3.4 fusion.3
  64.5 5.7 fusion.1
  70.2 3.5 fusion.5
  73.7 14.1 %collective-permute-done.10.refs_2_ = bf16[3,3,3,64,512]{4,3,2,1,0:T(8,128)(2,1)} collective-permute-done((bf16[3,3,3,64,512]{4,3,2,1,0:T(8,128)(2,1)}, bf16[3,3,3,64,512]{4,3,2,1,0:T(8,128)(2,1)}, u32[]{:S(2)}, u32[]{:S(2)}) %collective-permute-start.10) | collective-permute-done | bytes 1769504 | tf_op jit(solution)/shard_map/ppermute | solution.py:120
  101.0 7.4 %convolution_add_fusion = f32[640,1536]{1,0:T(8,128)S(1)} fusion(f32[640,1536]{1,0:T(8,128)} %fusion.143, bf16[1536,1536]{1,0:T(8,128)(2,1)} %fusion.1, bf16[1536,768]{1,0:T(8,128)(2,1)} %all-gather.5.cloned.1.call-done), kind=kOutput, calls=%fused_computation.17 | convolution fusion | flops 3020881920 | bytes 14548992 | tf_op jit(solution)/shard_map/dot_general | solution.py:35
  113.2 22.8 %shard_map.310 = (bf16[2,3,64,1536]{3,2,1,0:T(8,128)(2,1)S(1)}, bf16[2,4,1536,1152]{3,2,1,0:T(8,128)(2,1)}, f32[2,4,1,1152]{3,2,1,0:T(1,128)S(1)}) custom-call(bf16[2,3,64,1536]{3,2,1,0:T(8,128)(2,1)S(1)} %maximum_multiply_fusion.q_ref, bf16[2,64,1536]{2,1,0:T(8,128)(2,1)S(1)} %pad_maximum_fusion.2.k_ref, bf16[2,64,1536]{2,1,0:T(8,128)(2,1)S(1)} %bitcast.337, ...), custom_call_target="tpu_custom_call" | custom-call | flops 1811939328 | bytes 28311552 | tf_op jit(solution)/shard_map/pallas_call | solution.py:183
  145.5 4.6 collective-permute-done.12.refs_4_
  152.3 8.1 %collective-permute-start.17 = (bf16[2,3,3,64,512]{4,3,2,1,0:T(8,128)(2,1)}, bf16[2,3,3,64,512]{4,3,2,1,0:T(8,128)(2,1)}, u32[]{:S(2)}, u32[]{:S(2)}) collective-permute-start(bf16[2,3,3,64,512]{4,3,2,1,0:T(8,128)(2,1)} %bitcast.383), channel_id=1, source_target_pairs={{0,1},{1,2},{2,3},{3,0},{4,5},{5,6},{6,7},{7,4},{8,9},{9,10},{10,1... | collective-permute-start | bytes 3538952 | tf_op jit(solution)/shard_map/ppermute | solution.py:120
  162.8 3.7 convolution_convert_fusion.5
  169.0 4.8 slice.361.dy_ref
  179.3 9.4 %collective-permute-done.17.refs_7_ = bf16[2,3,3,64,512]{4,3,2,1,0:T(8,128)(2,1)} collective-permute-done((bf16[2,3,3,64,512]{4,3,2,1,0:T(8,128)(2,1)}, bf16[2,3,3,64,512]{4,3,2,1,0:T(8,128)(2,1)}, u32[]{:S(2)}, u32[]{:S(2)}) %collective-permute-start.17) | collective-permute-done | bytes 1179680 | tf_op jit(solution)/shard_map/ppermute | solution.py:120
  192.5 5.8 fusion.71
  198.2 19.7 %multiply_reduce_fusion = (f32[1536]{0:T(1024)S(1)}, f32[1536,1536]{1,0:T(8,128)}) fusion(f32[1536,1536]{1,0:T(8,128)} %fusion.71, bf16[1536,1536]{1,0:T(8,128)(2,1)S(1)} %bitcast.345, bf16[1536,768]{1,0:T(8,128)(2,1)} %collective-permute-done.6, bf16[1536,768]{1,0:T(8,128)(2,1)} %all-gather.7.cloned.1.call-done, pred[]{:T(512)S(6)} %eq.187, ...), kind=kOutput, calls=%fused_computation.12 | convolution fusion | flops 7280785920 | bytes 33036288 | tf_op jit(solution)/shard_map/dot_general | solution.py:35
  218.0 8.6 %collective-permute-done.14.refs_6_ = bf16[3,3,3,64,512]{4,3,2,1,0:T(8,128)(2,1)} collective-permute-done((bf16[3,3,3,64,512]{4,3,2,1,0:T(8,128)(2,1)}, bf16[3,3,3,64,512]{4,3,2,1,0:T(8,128)(2,1)}, u32[]{:S(2)}, u32[]{:S(2)}) %collective-permute-start.14) | collective-permute-done | bytes 1769504 | tf_op jit(solution)/shard_map/ppermute | solution.py:120
  228.4 4.6 multiply_convert_fusion.x_ref
  244.7 3.5 convolution_convert_fusion.zbias_ref
  249.0 35.1 %collective-permute-done.16.refs_7_ = bf16[3,3,3,64,512]{4,3,2,1,0:T(8,128)(2,1)} collective-permute-done((bf16[3,3,3,64,512]{4,3,2,1,0:T(8,128)(2,1)}, bf16[3,3,3,64,512]{4,3,2,1,0:T(8,128)(2,1)}, u32[]{:S(2)}, u32[]{:S(2)}) %collective-permute-start.16) | collective-permute-done | bytes 1769504 | tf_op jit(solution)/shard_map/ppermute | solution.py:120
  284.1 31.9 %shard_map.311 = (bf16[768,1536]{1,0:T(8,128)(2,1)}, bf16[768,1536]{1,0:T(8,128)(2,1)}, f32[768,128]{1,0:T(8,128)}, bf16[768,512]{1,0:T(8,128)(2,1)}, bf16[768,1024]{1,0:T(8,128)(2,1)}) custom-call(s32[10]{0:T(128)} %stack.140.place_ref, bf16[1536,1536]{1,0:T(8,128)(2,1)} %copy-done.10, bf16[1536,1536]{1,0:T(8,128)(2,1)} %slice.361.dy_ref, ...), custom_call_target="tpu_custom_call" | custom-call | flops 21743271936 | bytes 11796480 | tf_op jit(solution)/shard_map/pallas_call | solution.py:411
  316.1 32.4 %shard_map.312 = (bf16[768,1536]{1,0:T(8,128)(2,1)}, bf16[768,1536]{1,0:T(8,128)(2,1)}, f32[768,128]{1,0:T(8,128)}, bf16[768,512]{1,0:T(8,128)(2,1)}, bf16[768,1024]{1,0:T(8,128)(2,1)}) custom-call(s32[10]{0:T(128)} %stack.141.place_ref, bf16[1536,1536]{1,0:T(8,128)(2,1)} %copy-done.10, bf16[1536,1536]{1,0:T(8,128)(2,1)} %slice.361.dy_ref, ...), custom_call_target="tpu_custom_call" | custom-call | flops 21743271936 | bytes 11796480 | tf_op jit(solution)/shard_map/pallas_call | solution.py:411
  348.5 25.3 %shard_map.313 = (bf16[768,1536]{1,0:T(8,128)(2,1)}, bf16[768,1664]{1,0:T(8,128)(2,1)}, f32[768,128]{1,0:T(8,128)}, bf16[768,512]{1,0:T(8,128)(2,1)}, bf16[768,1024]{1,0:T(8,128)(2,1)}) custom-call(s32[10]{0:T(128)} %stack.138.place_ref, bf16[1536,1536]{1,0:T(8,128)(2,1)} %copy-done.10, bf16[1536,1536]{1,0:T(8,128)(2,1)} %slice.361.dy_ref, ...), custom_call_target="tpu_custom_call" | custom-call | flops 14495514624 | bytes 11796480 | tf_op jit(solution)/shard_map/pallas_call | solution.py:411
  385.0 25.9 %shard_map.314 = (bf16[768,1536]{1,0:T(8,128)(2,1)}, bf16[768,1664]{1,0:T(8,128)(2,1)}, f32[768,128]{1,0:T(8,128)}, bf16[768,512]{1,0:T(8,128)(2,1)}, bf16[768,1024]{1,0:T(8,128)(2,1)}) custom-call(s32[10]{0:T(128)} %stack.136.place_ref, bf16[1536,1536]{1,0:T(8,128)(2,1)} %copy-done.10, bf16[1536,1536]{1,0:T(8,128)(2,1)} %slice.361.dy_ref, ...), custom_call_target="tpu_custom_call" | custom-call | flops 14495514624 | bytes 11796480 | tf_op jit(solution)/shard_map/pallas_call | solution.py:411
  410.9 4.7 collective-permute-done.25
  445.9 5.2 fusion.6
  456.3 11.1 %collective-permute-done.31 = bf16[2,384,384]{2,1,0:T(8,128)(2,1)S(1)} collective-permute-done((bf16[2,384,384]{2,1,0:T(8,128)(2,1)S(1)}, bf16[2,384,384]{2,1,0:T(8,128)(2,1)S(1)}, u32[]{:S(2)}, u32[]{:S(2)}) %collective-permute-start.31) | collective-permute-done | bytes 589856 | tf_op jit(solution)/shard_map/ppermute | solution.py:53
  467.7 3.5 collective-permute-done.29
  495.1 27.6 %shard_map.315 = (bf16[2,3,64,1536]{3,2,1,0:T(8,128)(2,1)S(1)}, bf16[2,64,1536]{2,1,0:T(8,128)(2,1)S(1)}, bf16[2,64,1536]{2,1,0:T(8,128)(2,1)S(1)}) custom-call(bf16[2,3,64,1536]{3,2,1,0:T(8,128)(2,1)S(1)} %copy-done.2, bf16[2,64,1536]{2,1,0:T(8,128)(2,1)S(1)} %pad_maximum_fusion.2.k_ref, bf16[2,64,1536]{2,1,0:T(8,128)(2,1)S(1)} %bitcast.338, ...), custom_call_target="tpu_custom_call" | custom-call | flops 3623878656 | bytes 28311552 | tf_op jit(solution)/shard_map/pallas_call | solution.py:269
  532.4 3.6 fusion.30
  543.2 3.7 collective-permute-done.37
  558.4 4.2 fusion.23
  562.6 4.4 collective-permute-done.44
  567.7 3.6 concatenate.116
  590.1 4.0 fusion.13
  (496 shorter events, 242.6 us)
Async XLA Ops:
  7.2 93.8 %all-gather.5.cloned.1.call-start = ((), (), s32[]{:S(2)}) async-start(), calls=%async_computation | async-start | bytes 2654208 | tf_op jit(solution)/shard_map/all_gather | solution.py:581
  10.8 149.6 %all-gather.7.cloned.1.call-start = ((), (), s32[]{:S(2)}) async-start(), calls=%async_computation.1 | async-start | bytes 2654208 | tf_op jit(solution)/shard_map/all_gather | solution.py:581
  10.9 42.7 %collective-permute-start = (bf16[384,1536]{1,0:T(8,128)(2,1)}, bf16[384,1536]{1,0:T(8,128)(2,1)}, u32[]{:S(2)}, u32[]{:S(2)}) collective-permute-start(bf16[384,1536]{1,0:T(8,128)(2,1)} %bitcast.352), channel_id=1, source_target_pairs={{0,4},{4,0},{8,12},{12,8},{1,5},{5,1},{9,13},{13,9},{2,6},{6,2},{1... | collective-permute-start | bytes 3538952 | tf_op jit(solution)/shard_map/ppermute | solution.py:47
  11.4 34.9 %collective-permute-start.1 = (bf16[384,1536]{1,0:T(8,128)(2,1)}, bf16[384,1536]{1,0:T(8,128)(2,1)}, u32[]{:S(2)}, u32[]{:S(2)}) collective-permute-start(bf16[384,1536]{1,0:T(8,128)(2,1)} %bitcast.353), channel_id=1, source_target_pairs={{0,8},{4,12},{8,0},{12,4},{1,9},{5,13},{9,1},{13,5},{2,10},{6,14},... | collective-permute-start | bytes 3538952 | tf_op jit(solution)/shard_map/ppermute | solution.py:53
  18.8 68.9 %collective-permute-start.10 = (bf16[3,3,3,64,512]{4,3,2,1,0:T(8,128)(2,1)}, bf16[3,3,3,64,512]{4,3,2,1,0:T(8,128)(2,1)}, u32[]{:S(2)}, u32[]{:S(2)}) collective-permute-start(bf16[3,3,3,64,512]{4,3,2,1,0:T(8,128)(2,1)} %bitcast.55.refs_0_), channel_id=1, source_target_pairs={{0,1},{1,2},{2,3},{3,0},{4,5},{5,6},{6,7},{7,4},{8,9},{9,10},{10,1... | collective-permute-start | bytes 5308424 | tf_op jit(solution)/shard_map/ppermute | solution.py:120
  20.4 67.4 %collective-permute-start.11 = (bf16[3,3,3,64,512]{4,3,2,1,0:T(8,128)(2,1)}, bf16[3,3,3,64,512]{4,3,2,1,0:T(8,128)(2,1)}, u32[]{:S(2)}, u32[]{:S(2)}) collective-permute-start(bf16[3,3,3,64,512]{4,3,2,1,0:T(8,128)(2,1)} %bitcast.55.refs_0_), channel_id=1, source_target_pairs={{0,16},{16,0},{1,17},{17,1},{2,18},{18,2},{3,19},{19,3},{4,20},{20... | collective-permute-start | bytes 5308424 | tf_op jit(solution)/shard_map/ppermute | solution.py:120
  23.6 549.7 %all-gather.9.cloned.1.call-start = ((), (), s32[]{:S(2)}) async-start(), calls=%async_computation.2 | async-start | bytes 2211840 | tf_op jit(solution)/shard_map/all_gather | solution.py:753
  62.8 35.7 %collective-permute-start.7 = (bf16[384,1664]{1,0:T(8,128)(2,1)S(1)}, bf16[384,1664]{1,0:T(8,128)(2,1)}, u32[]{:S(2)}, u32[]{:S(2)}) collective-permute-start(bf16[384,1664]{1,0:T(8,128)(2,1)S(1)} %copy-done.19), channel_id=1, source_target_pairs={{0,4},{4,0},{8,12},{12,8},{1,5},{5,1},{9,13},{13,9},{2,6},{6,2},{1... | collective-permute-start | bytes 3833864 | tf_op jit(solution)/shard_map/ppermute | solution.py:47
  63.4 35.0 %collective-permute-start.8 = (bf16[384,1664]{1,0:T(8,128)(2,1)S(1)}, bf16[384,1664]{1,0:T(8,128)(2,1)}, u32[]{:S(2)}, u32[]{:S(2)}) collective-permute-start(bf16[384,1664]{1,0:T(8,128)(2,1)S(1)} %copy-done.19), channel_id=1, source_target_pairs={{0,8},{4,12},{8,0},{12,4},{1,9},{5,13},{9,1},{13,5},{2,10},{6,14},... | collective-permute-start | bytes 3833864 | tf_op jit(solution)/shard_map/ppermute | solution.py:53
  87.8 62.4 %collective-permute-start.12 = (bf16[3,3,3,64,512]{4,3,2,1,0:T(8,128)(2,1)}, bf16[3,3,3,64,512]{4,3,2,1,0:T(8,128)(2,1)}, u32[]{:S(2)}, u32[]{:S(2)}) collective-permute-start(bf16[3,3,3,64,512]{4,3,2,1,0:T(8,128)(2,1)} %collective-permute-done.10.refs_2_), channel_id=1, source_target_pairs={{0,1},{1,2},{2,3},{3,0},{4,5},{5,6},{6,7},{7,4},{8,9},{9,10},{10,1... | collective-permute-start | bytes 5308424 | tf_op jit(solution)/shard_map/ppermute | solution.py:120
  89.1 63.2 %collective-permute-start.13 = (bf16[3,3,3,64,512]{4,3,2,1,0:T(8,128)(2,1)}, bf16[3,3,3,64,512]{4,3,2,1,0:T(8,128)(2,1)}, u32[]{:S(2)}, u32[]{:S(2)}) collective-permute-start(bf16[3,3,3,64,512]{4,3,2,1,0:T(8,128)(2,1)} %collective-permute-done.10.refs_2_), channel_id=1, source_target_pairs={{0,16},{16,0},{1,17},{17,1},{2,18},{18,2},{3,19},{19,3},{4,20},{20... | collective-permute-start | bytes 5308424 | tf_op jit(solution)/shard_map/ppermute | solution.py:120
  98.5 61.9 %collective-permute-start.9 = (bf16[384,1664]{1,0:T(8,128)(2,1)}, bf16[384,1664]{1,0:T(8,128)(2,1)}, u32[]{:S(2)}, u32[]{:S(2)}) collective-permute-start(bf16[384,1664]{1,0:T(8,128)(2,1)} %collective-permute-done.8), channel_id=1, source_target_pairs={{0,4},{4,0},{8,12},{12,8},{1,5},{5,1},{9,13},{13,9},{2,6},{6,2},{1... | collective-permute-start | bytes 3833864 | tf_op jit(solution)/shard_map/ppermute | solution.py:47
  136.1 30.4 %collective-permute-start.4 = (bf16[384,1536]{1,0:T(8,128)(2,1)S(1)}, bf16[384,1536]{1,0:T(8,128)(2,1)}, u32[]{:S(2)}, u32[]{:S(2)}) collective-permute-start(bf16[384,1536]{1,0:T(8,128)(2,1)S(1)} %bitcast.333), channel_id=1, source_target_pairs={{0,8},{4,12},{8,0},{12,4},{1,9},{5,13},{9,1},{13,5},{2,10},{6,14},... | collective-permute-start | bytes 3538952 | tf_op jit(solution)/shard_map/ppermute | solution.py:53
  139.0 34.8 %collective-permute-start.3 = (bf16[384,1536]{1,0:T(8,128)(2,1)S(1)}, bf16[384,1536]{1,0:T(8,128)(2,1)}, u32[]{:S(2)}, u32[]{:S(2)}) collective-permute-start(bf16[384,1536]{1,0:T(8,128)(2,1)S(1)} %bitcast.334), channel_id=1, source_target_pairs={{0,4},{4,0},{8,12},{12,8},{1,5},{5,1},{9,13},{13,9},{2,6},{6,2},{1... | collective-permute-start | bytes 3538952 | tf_op jit(solution)/shard_map/ppermute | solution.py:47
  150.1 29.1 %collective-permute-start.18 = (bf16[2,3,3,64,512]{4,3,2,1,0:T(8,128)(2,1)}, bf16[2,3,3,64,512]{4,3,2,1,0:T(8,128)(2,1)}, u32[]{:S(2)}, u32[]{:S(2)}) collective-permute-start(bf16[2,3,3,64,512]{4,3,2,1,0:T(8,128)(2,1)} %bitcast.382), channel_id=1, source_target_pairs={{0,16},{16,0},{1,17},{17,1},{2,18},{18,2},{3,19},{19,3},{4,20},{20... | collective-permute-start | bytes 3538952 | tf_op jit(solution)/shard_map/ppermute | solution.py:120
  152.3 36.4 %collective-permute-start.17 = (bf16[2,3,3,64,512]{4,3,2,1,0:T(8,128)(2,1)}, bf16[2,3,3,64,512]{4,3,2,1,0:T(8,128)(2,1)}, u32[]{:S(2)}, u32[]{:S(2)}) collective-permute-start(bf16[2,3,3,64,512]{4,3,2,1,0:T(8,128)(2,1)} %bitcast.383), channel_id=1, source_target_pairs={{0,1},{1,2},{2,3},{3,0},{4,5},{5,6},{6,7},{7,4},{8,9},{9,10},{10,1... | collective-permute-start | bytes 3538952 | tf_op jit(solution)/shard_map/ppermute | solution.py:120
  160.4 37.9 %collective-permute-start.6 = (bf16[1536,768]{1,0:T(8,128)(2,1)}, bf16[1536,768]{1,0:T(8,128)(2,1)}, u32[]{:S(2)}, u32[]{:S(2)}) collective-permute-start(bf16[1536,768]{1,0:T(8,128)(2,1)} %all-gather.7.cloned.1.call-done), channel_id=1, source_target_pairs={{0,4},{4,0},{8,12},{12,8},{1,5},{5,1},{9,13},{13,9},{2,6},{6,2},{1... | collective-permute-start | bytes 7077896 | tf_op jit(solution)/shard_map/ppermute | solution.py:47
  173.8 52.8 %collective-permute-start.14 = (bf16[3,3,3,64,512]{4,3,2,1,0:T(8,128)(2,1)}, bf16[3,3,3,64,512]{4,3,2,1,0:T(8,128)(2,1)}, u32[]{:S(2)}, u32[]{:S(2)}) collective-permute-start(bf16[3,3,3,64,512]{4,3,2,1,0:T(8,128)(2,1)} %collective-permute-done.12.refs_4_), channel_id=1, source_target_pairs={{0,1},{1,2},{2,3},{3,0},{4,5},{5,6},{6,7},{7,4},{8,9},{9,10},{10,1... | collective-permute-start | bytes 5308424 | tf_op jit(solution)/shard_map/ppermute | solution.py:120
  179.1 47.5 %collective-permute-start.15 = (bf16[3,3,3,64,512]{4,3,2,1,0:T(8,128)(2,1)}, bf16[3,3,3,64,512]{4,3,2,1,0:T(8,128)(2,1)}, u32[]{:S(2)}, u32[]{:S(2)}) collective-permute-start(bf16[3,3,3,64,512]{4,3,2,1,0:T(8,128)(2,1)} %collective-permute-done.12.refs_4_), channel_id=1, source_target_pairs={{0,16},{16,0},{1,17},{17,1},{2,18},{18,2},{3,19},{19,3},{4,20},{20... | collective-permute-start | bytes 5308424 | tf_op jit(solution)/shard_map/ppermute | solution.py:120
  188.6 59.6 %collective-permute-start.19 = (bf16[2,3,3,64,512]{4,3,2,1,0:T(8,128)(2,1)}, bf16[2,3,3,64,512]{4,3,2,1,0:T(8,128)(2,1)}, u32[]{:S(2)}, u32[]{:S(2)}) collective-permute-start(bf16[2,3,3,64,512]{4,3,2,1,0:T(8,128)(2,1)} %collective-permute-done.17.refs_7_), channel_id=1, source_target_pairs={{0,1},{1,2},{2,3},{3,0},{4,5},{5,6},{6,7},{7,4},{8,9},{9,10},{10,1... | collective-permute-start | bytes 3538952 | tf_op jit(solution)/shard_map/ppermute | solution.py:120
  189.0 59.2 %collective-permute-start.20 = (bf16[2,3,3,64,512]{4,3,2,1,0:T(8,128)(2,1)}, bf16[2,3,3,64,512]{4,3,2,1,0:T(8,128)(2,1)}, u32[]{:S(2)}, u32[]{:S(2)}) collective-permute-start(bf16[2,3,3,64,512]{4,3,2,1,0:T(8,128)(2,1)} %collective-permute-done.17.refs_7_), channel_id=1, source_target_pairs={{0,16},{16,0},{1,17},{17,1},{2,18},{18,2},{3,19},{19,3},{4,20},{20... | collective-permute-start | bytes 3538952 | tf_op jit(solution)/shard_map/ppermute | solution.py:120
  226.6 57.5 %collective-permute-start.16 = (bf16[3,3,3,64,512]{4,3,2,1,0:T(8,128)(2,1)}, bf16[3,3,3,64,512]{4,3,2,1,0:T(8,128)(2,1)}, u32[]{:S(2)}, u32[]{:S(2)}) collective-permute-start(bf16[3,3,3,64,512]{4,3,2,1,0:T(8,128)(2,1)} %collective-permute-done.14.refs_6_), channel_id=1, source_target_pairs={{0,16},{16,0},{1,17},{17,1},{2,18},{18,2},{3,19},{19,3},{4,20},{20... | collective-permute-start | bytes 5308424 | tf_op jit(solution)/shard_map/ppermute | solution.py:120
  248.2 67.7 %collective-permute-start.21 = (bf16[2,3,3,64,512]{4,3,2,1,0:T(8,128)(2,1)}, bf16[2,3,3,64,512]{4,3,2,1,0:T(8,128)(2,1)}, u32[]{:S(2)}, u32[]{:S(2)}) collective-permute-start(bf16[2,3,3,64,512]{4,3,2,1,0:T(8,128)(2,1)} %collective-permute-done.19.refs_9_), channel_id=1, source_target_pairs={{0,1},{1,2},{2,3},{3,0},{4,5},{5,6},{6,7},{7,4},{8,9},{9,10},{10,1... | collective-permute-start | bytes 3538952 | tf_op jit(solution)/shard_map/ppermute | solution.py:120
  248.2 67.7 %collective-permute-start.22 = (bf16[2,3,3,64,512]{4,3,2,1,0:T(8,128)(2,1)}, bf16[2,3,3,64,512]{4,3,2,1,0:T(8,128)(2,1)}, u32[]{:S(2)}, u32[]{:S(2)}) collective-permute-start(bf16[2,3,3,64,512]{4,3,2,1,0:T(8,128)(2,1)} %collective-permute-done.19.refs_9_), channel_id=1, source_target_pairs={{0,16},{16,0},{1,17},{17,1},{2,18},{18,2},{3,19},{19,3},{4,20},{20... | collective-permute-start | bytes 3538952 | tf_op jit(solution)/shard_map/ppermute | solution.py:120
  316.0 32.5 %collective-permute-start.23 = (bf16[2,3,3,64,512]{4,3,2,1,0:T(8,128)(2,1)}, bf16[2,3,3,64,512]{4,3,2,1,0:T(8,128)(2,1)}, u32[]{:S(2)}, u32[]{:S(2)}) collective-permute-start(bf16[2,3,3,64,512]{4,3,2,1,0:T(8,128)(2,1)} %collective-permute-done.21.refs_11_), channel_id=1, source_target_pairs={{0,16},{16,0},{1,17},{17,1},{2,18},{18,2},{3,19},{19,3},{4,20},{20... | collective-permute-start | bytes 3538952 | tf_op jit(solution)/shard_map/ppermute | solution.py:120
  384.9 30.8 %collective-permute-start.25 = (bf16[384,1664]{1,0:T(8,128)(2,1)}, bf16[384,1664]{1,0:T(8,128)(2,1)}, u32[]{:S(2)}, u32[]{:S(2)}) collective-permute-start(bf16[384,1664]{1,0:T(8,128)(2,1)} %fusion.8), channel_id=1, source_target_pairs={{0,8},{4,12},{8,0},{12,4},{1,9},{5,13},{9,1},{13,5},{2,10},{6,14},... | collective-permute-start | bytes 3833864 | tf_op jit(solution)/shard_map/ppermute | solution.py:53
  418.4 33.2 %collective-permute-start.34 = (bf16[384,1536]{1,0:T(8,128)(2,1)}, bf16[384,1536]{1,0:T(8,128)(2,1)}, u32[]{:S(2)}, u32[]{:S(2)}) collective-permute-start(bf16[384,1536]{1,0:T(8,128)(2,1)} %dynamic-slice_bitcast_fusion.4), channel_id=1, source_target_pairs={{0,4},{4,0},{8,12},{12,8},{1,5},{5,1},{9,13},{13,9},{2,6},{6,2},{1... | collective-permute-start | bytes 3538952 | tf_op jit(solution)/shard_map/ppermute | solution.py:47
  454.4 16.8 %collective-permute-start.29 = (f32[32,1536]{1,0:T(8,128)S(1)}, f32[32,1536]{1,0:T(8,128)S(1)}, u32[]{:S(2)}, u32[]{:S(2)}) collective-permute-start(f32[32,1536]{1,0:T(8,128)S(1)} %bitcast_add_fusion.1), channel_id=1, source_target_pairs={{0,8},{4,12},{8,0},{12,4},{1,9},{5,13},{9,1},{13,5},{2,10},{6,14},... | collective-permute-start | bytes 589832 | tf_op jit(solution)/shard_map/ppermute | solution.py:53
  473.1 49.6 %collective-permute-start.35 = (bf16[384,1536]{1,0:T(8,128)(2,1)}, bf16[384,1536]{1,0:T(8,128)(2,1)}, u32[]{:S(2)}, u32[]{:S(2)}) collective-permute-start(bf16[384,1536]{1,0:T(8,128)(2,1)} %fusion.19), channel_id=1, source_target_pairs={{0,8},{4,12},{8,0},{12,4},{1,9},{5,13},{9,1},{13,5},{2,10},{6,14},... | collective-permute-start | bytes 3538952 | tf_op jit(solution)/shard_map/ppermute | solution.py:53
  491.0 66.6 %collective-permute-start.27 = (bf16[384,1536]{1,0:T(8,128)(2,1)}, bf16[384,1536]{1,0:T(8,128)(2,1)}, u32[]{:S(2)}, u32[]{:S(2)}) collective-permute-start(bf16[384,1536]{1,0:T(8,128)(2,1)} %dynamic-slice_bitcast_fusion.5), channel_id=1, source_target_pairs={{0,4},{4,0},{8,12},{12,8},{1,5},{5,1},{9,13},{13,9},{2,6},{6,2},{1... | collective-permute-start | bytes 3538952 | tf_op jit(solution)/shard_map/ppermute | solution.py:47
  551.3 35.8 %collective-permute-start.41 = (bf16[384,1536]{1,0:T(8,128)(2,1)}, bf16[384,1536]{1,0:T(8,128)(2,1)}, u32[]{:S(2)}, u32[]{:S(2)}) collective-permute-start(bf16[384,1536]{1,0:T(8,128)(2,1)} %dynamic-slice_bitcast_fusion.2), channel_id=1, source_target_pairs={{0,4},{4,0},{8,12},{12,8},{1,5},{5,1},{9,13},{13,9},{2,6},{6,2},{1... | collective-permute-start | bytes 3538952 | tf_op jit(solution)/shard_map/ppermute | solution.py:47
  551.3 36.0 %collective-permute-start.40 = (bf16[384,1536]{1,0:T(8,128)(2,1)}, bf16[384,1536]{1,0:T(8,128)(2,1)}, u32[]{:S(2)}, u32[]{:S(2)}) collective-permute-start(bf16[384,1536]{1,0:T(8,128)(2,1)} %fusion.18), channel_id=1, source_target_pairs={{0,8},{4,12},{8,0},{12,4},{1,9},{5,13},{9,1},{13,5},{2,10},{6,14},... | collective-permute-start | bytes 3538952 | tf_op jit(solution)/shard_map/ppermute | solution.py:53
  (112 other events, 814.6 us)
Sparse Core Ops, SparseCore 0:
  10.9 79.6 all-gather.4
  93.3 66.2 all-gather.6
  491.9 47.8 all-gather.8

commit v4 on v3

--- a/solution.py
+++ b/solution.py
@@ -479,9 +479,13 @@
     picks = (names[None, :] == first_row + jnp.arange(share)[:, None]).astype(F32)
     kept = jnp.sum(picks[:, :, None, None] * everyone[None].astype(F32), axis=1)
     pieces = seq_pieces(kept.reshape(share * part, width), n_seq)
-    place = jnp.arange(n_seq)[None, :, None, None]
-    full = sum(jnp.where(place == at, x.reshape(share, 1, part, width), 0.0) for at, x in pieces)
-    return full.reshape(share, n_seq * part, width)
+    stacked = jnp.stack([x.reshape(share, part, width) for _, x in pieces])
+    me, n_y = lax.axis_index("seq"), n_seq // 2
+    blocks = []
+    for j in range(n_seq):
+        turn = (me // 2 + n_y - j // 2) % n_y * 2 + (me + j) % 2
+        blocks.append(lax.dynamic_index_in_dim(stacked, turn, 0, keepdims=False))
+    return jnp.concatenate(blocks, axis=1)
 
 
 def shards(
@@ -728,20 +732,24 @@
     d_branch = d_residual.astype(BF16)
     d_small_o = dot_nt(d_branch, out_second).astype(BF16)
     d_att = (dot_nt(out_weight, d_branch) + dot_nt(out_first, d_small_o)).astype(BF16)
+    d_att_own = d_att
     d_att = spread_seq(d_att.reshape(n_seq, q_width, local), n_seq)
 
     def of_chip(x, chip, axis=0):
         return lax.dynamic_slice_in_dim(x, chip * chip_rows, chip_rows, axis)
 
+    d_small_o_late, d_branch_late, d_small_m_late, small_d_late, _ = tie(
+        (d_small_o, d_branch, d_small_m, small_d, d_att_own)
+    )
     grad_gu = sum(dot_tn(of_chip(small_m[:, rank:], chip), parts[4]) for _, chip, parts in turns)
     grad_down = sum(dot_tn(of_chip(d_rank, chip), parts[3]) for _, chip, parts in turns)
     att_own = lax.dynamic_slice_in_dim(att, seq * local, local, 1)
     early = jnp.concatenate(
         [
-            dot(d_small_o, att_own, ((0,), (1,))),
-            dot_tn(own_rows(small_o), d_branch),
-            dot_tn(d_small_m, own_rows(normed_m)),
-            dot_tn(small_d, cotangent[0]),
+            dot(d_small_o_late, att_own, ((0,), (1,))),
+            dot_tn(own_rows(small_o), d_branch_late),
+            dot_tn(d_small_m_late, own_rows(normed_m)),
+            dot_tn(small_d_late, cotangent[0]),
             jnp.concatenate([grad_gu[:rank, :HIDDEN], grad_gu[rank:, HIDDEN:], grad_down], axis=1),
             pad_lanes(dot_tn(small_m_own[:, :rank], d_logits_low), width=MODEL_WIDTH),
         ],

time: 625 us -> 620 us (level); the launches traced: 615 us -> 621 us
  local copies, waits for them, and re-layouts: 135 us -> 111 us
  starting transfers between devices: 46.1 us -> 66.8 us
  waiting for transfers between devices: 100 us -> 114 us
    ppermute x11, starting transfers between devices: 11.6 us -> 33.8 us  [shift_chip(): return lax.ppermute(x, 'seq', pairs)]
    broadcast_in_dim x22 -> x0, local copies, waits for them, and re-layouts: 17 us -> none  [by_adapter(): jnp.where(place == at, x.reshape(share, 1, part, width), 0.0)]
    ppermute x11, waiting for transfers between devices: 23.7 us -> 34.1 us  [shift_chip(): return lax.ppermute(x, 'seq', pairs)]
    unnamed x193 -> x158, local copies, waits for them, and re-layouts: 31.4 us -> 26 us
  transfers between devices with their start and end apart: 55 -> 55, of which waited for: 11 -> 14; matrix products, arithmetic and copies ran while one was open for 41% -> 37% of each run, Pallas kernels for 23% -> 23%
where the time goes in v4:
time: 620 us; the launch traced here: 621 us
  Pallas kernels  166 us (27%)
  waiting for transfers between devices  114 us (18%)
  local copies, waits for them, and re-layouts  111 us (18%)
  matrix products  87.4 us (14%)
  starting transfers between devices  66.8 us (11%)
  other arithmetic  60 us (10%)
  between operations  16 us (3%)
    pallas_call x4, Pallas kernels, run_experts(): pl.pallas_call(functools.partial(expert_kernel, len(shards), experts_all,...  115 us
    dot_general x33, matrix products, dot(): return lax.dot_general(a, b, (dims, ((), ())), preferred_element_type=F32)  87.4 us
    ppermute x18, waiting for transfers between devices, shift(): return lax.ppermute(x, axis, [(i, (i + k) % count) for i in range(count)])  79.6 us
    ppermute x11, waiting for transfers between devices, shift_chip(): return lax.ppermute(x, 'seq', pairs)  34.1 us
    ppermute x11, starting transfers between devices, shift_chip(): return lax.ppermute(x, 'seq', pairs)  33.8 us
    ppermute x18, starting transfers between devices, shift(): return lax.ppermute(x, axis, [(i, (i + k) % count) for i in range(count)])  28 us
    pallas_call x1, Pallas kernels, attend_back(): pl.pallas_call(attend_back_kernel, grid=(kv, blocks), in_specs=[q_spec, k...  27.6 us
    unnamed x158, local copies, waits for them, and re-layouts  26 us
  transfers between devices with their start and end apart: 55, of which 14 were waited for; matrix products, arithmetic and copies ran while one was open for 37% of the time, Pallas kernels for 23%

profile of v4, /device:TPU:0, one launch (start us, length us, event | category | flops | bytes accessed | tf_op | source)
XLA Modules:
  0.0 621.0 jit_solution(9462231800461317700)
XLA Ops:
  62.6 5.7 fusion.1
  68.3 3.5 fusion.5
  71.8 16.0 %collective-permute-done.10.refs_2_ = bf16[3,3,3,64,512]{4,3,2,1,0:T(8,128)(2,1)} collective-permute-done((bf16[3,3,3,64,512]{4,3,2,1,0:T(8,128)(2,1)}, bf16[3,3,3,64,512]{4,3,2,1,0:T(8,128)(2,1)}, u32[]{:S(2)}, u32[]{:S(2)}) %collective-permute-start.10) | collective-permute-done | bytes 1769504 | tf_op jit(solution)/shard_map/ppermute | solution.py:120
  100.9 7.4 %convolution_add_fusion = f32[640,1536]{1,0:T(8,128)S(1)} fusion(f32[640,1536]{1,0:T(8,128)} %fusion.132, bf16[1536,1536]{1,0:T(8,128)(2,1)} %fusion.1, bf16[1536,768]{1,0:T(8,128)(2,1)} %all-gather.5.cloned.1.call-done), kind=kOutput, calls=%fused_computation.17 | convolution fusion | flops 3020881920 | bytes 14548992 | tf_op jit(solution)/shard_map/dot_general | solution.py:35
  113.1 22.8 %shard_map.310 = (bf16[2,3,64,1536]{3,2,1,0:T(8,128)(2,1)S(1)}, bf16[2,4,1536,1152]{3,2,1,0:T(8,128)(2,1)}, f32[2,4,1,1152]{3,2,1,0:T(1,128)S(1)}) custom-call(bf16[2,3,64,1536]{3,2,1,0:T(8,128)(2,1)S(1)} %maximum_multiply_fusion.q_ref, bf16[2,64,1536]{2,1,0:T(8,128)(2,1)S(1)} %pad_maximum_fusion.7.k_ref, bf16[2,64,1536]{2,1,0:T(8,128)(2,1)S(1)} %bitcast.323, ...), custom_call_target="tpu_custom_call" | custom-call | flops 1811939328 | bytes 28311552 | tf_op jit(solution)/shard_map/pallas_call | solution.py:183
  145.3 5.0 collective-permute-done.12.refs_4_
  152.4 8.1 %collective-permute-start.17 = (bf16[2,3,3,64,512]{4,3,2,1,0:T(8,128)(2,1)}, bf16[2,3,3,64,512]{4,3,2,1,0:T(8,128)(2,1)}, u32[]{:S(2)}, u32[]{:S(2)}) collective-permute-start(bf16[2,3,3,64,512]{4,3,2,1,0:T(8,128)(2,1)} %bitcast.373), channel_id=1, source_target_pairs={{0,1},{1,2},{2,3},{3,0},{4,5},{5,6},{6,7},{7,4},{8,9},{9,10},{10,1... | collective-permute-start | bytes 3538952 | tf_op jit(solution)/shard_map/ppermute | solution.py:120
  162.9 3.7 convolution_convert_fusion.5
  169.1 4.8 slice.363.dy_ref
  179.4 9.4 %collective-permute-done.17.refs_7_ = bf16[2,3,3,64,512]{4,3,2,1,0:T(8,128)(2,1)} collective-permute-done((bf16[2,3,3,64,512]{4,3,2,1,0:T(8,128)(2,1)}, bf16[2,3,3,64,512]{4,3,2,1,0:T(8,128)(2,1)}, u32[]{:S(2)}, u32[]{:S(2)}) %collective-permute-start.17) | collective-permute-done | bytes 1179680 | tf_op jit(solution)/shard_map/ppermute | solution.py:120
  192.6 5.8 fusion.65
  198.3 19.7 %multiply_reduce_fusion = (f32[1536]{0:T(1024)S(1)}, f32[1536,1536]{1,0:T(8,128)}) fusion(f32[1536,1536]{1,0:T(8,128)} %fusion.65, bf16[1536,1536]{1,0:T(8,128)(2,1)S(1)} %bitcast.331, bf16[1536,768]{1,0:T(8,128)(2,1)} %collective-permute-done.6, bf16[1536,768]{1,0:T(8,128)(2,1)} %all-gather.7.cloned.1.call-done, pred[]{:T(512)S(6)} %eq.147, ...), kind=kOutput, calls=%fused_computation.12 | convolution fusion | flops 7280785920 | bytes 33036288 | tf_op jit(solution)/shard_map/dot_general | solution.py:35
  218.0 8.6 %collective-permute-done.14.refs_6_ = bf16[3,3,3,64,512]{4,3,2,1,0:T(8,128)(2,1)} collective-permute-done((bf16[3,3,3,64,512]{4,3,2,1,0:T(8,128)(2,1)}, bf16[3,3,3,64,512]{4,3,2,1,0:T(8,128)(2,1)}, u32[]{:S(2)}, u32[]{:S(2)}) %collective-permute-start.14) | collective-permute-done | bytes 1769504 | tf_op jit(solution)/shard_map/ppermute | solution.py:120
  228.5 4.6 multiply_convert_fusion.x_ref
  244.8 3.6 convolution_convert_fusion.zbias_ref
  249.0 35.2 %collective-permute-done.16.refs_7_ = bf16[3,3,3,64,512]{4,3,2,1,0:T(8,128)(2,1)} collective-permute-done((bf16[3,3,3,64,512]{4,3,2,1,0:T(8,128)(2,1)}, bf16[3,3,3,64,512]{4,3,2,1,0:T(8,128)(2,1)}, u32[]{:S(2)}, u32[]{:S(2)}) %collective-permute-start.16) | collective-permute-done | bytes 1769504 | tf_op jit(solution)/shard_map/ppermute | solution.py:120
  284.2 31.9 %shard_map.311 = (bf16[768,1536]{1,0:T(8,128)(2,1)}, bf16[768,1536]{1,0:T(8,128)(2,1)}, f32[768,128]{1,0:T(8,128)}, bf16[768,512]{1,0:T(8,128)(2,1)}, bf16[768,1024]{1,0:T(8,128)(2,1)}) custom-call(s32[10]{0:T(128)} %stack.146.place_ref, bf16[1536,1536]{1,0:T(8,128)(2,1)} %copy-done.8, bf16[1536,1536]{1,0:T(8,128)(2,1)} %slice.363.dy_ref, ...), custom_call_target="tpu_custom_call" | custom-call | flops 21743271936 | bytes 11796480 | tf_op jit(solution)/shard_map/pallas_call | solution.py:411
  316.1 32.3 %shard_map.312 = (bf16[768,1536]{1,0:T(8,128)(2,1)}, bf16[768,1536]{1,0:T(8,128)(2,1)}, f32[768,128]{1,0:T(8,128)}, bf16[768,512]{1,0:T(8,128)(2,1)}, bf16[768,1024]{1,0:T(8,128)(2,1)}) custom-call(s32[10]{0:T(128)} %stack.147.place_ref, bf16[1536,1536]{1,0:T(8,128)(2,1)} %copy-done.8, bf16[1536,1536]{1,0:T(8,128)(2,1)} %slice.363.dy_ref, ...), custom_call_target="tpu_custom_call" | custom-call | flops 21743271936 | bytes 11796480 | tf_op jit(solution)/shard_map/pallas_call | solution.py:411
  348.4 25.3 %shard_map.313 = (bf16[768,1536]{1,0:T(8,128)(2,1)}, bf16[768,1664]{1,0:T(8,128)(2,1)}, f32[768,128]{1,0:T(8,128)}, bf16[768,512]{1,0:T(8,128)(2,1)}, bf16[768,1024]{1,0:T(8,128)(2,1)}) custom-call(s32[10]{0:T(128)} %stack.144.place_ref, bf16[1536,1536]{1,0:T(8,128)(2,1)} %copy-done.8, bf16[1536,1536]{1,0:T(8,128)(2,1)} %slice.363.dy_ref, ...), custom_call_target="tpu_custom_call" | custom-call | flops 14495514624 | bytes 11796480 | tf_op jit(solution)/shard_map/pallas_call | solution.py:411
  383.7 23.5 %collective-permute-start.25 = (bf16[384,1664]{1,0:T(8,128)(2,1)}, bf16[384,1664]{1,0:T(8,128)(2,1)}, u32[]{:S(2)}, u32[]{:S(2)}) collective-permute-start(bf16[384,1664]{1,0:T(8,128)(2,1)} %fusion.8), channel_id=1, source_target_pairs={{0,8},{4,12},{8,0},{12,4},{1,9},{5,13},{9,1},{13,5},{2,10},{6,14},... | collective-permute-start | bytes 3833864 | tf_op jit(solution)/shard_map/ppermute | solution.py:53
  407.2 25.9 %shard_map.314 = (bf16[768,1536]{1,0:T(8,128)(2,1)}, bf16[768,1664]{1,0:T(8,128)(2,1)}, f32[768,128]{1,0:T(8,128)}, bf16[768,512]{1,0:T(8,128)(2,1)}, bf16[768,1024]{1,0:T(8,128)(2,1)}) custom-call(s32[10]{0:T(128)} %stack.142.place_ref, bf16[1536,1536]{1,0:T(8,128)(2,1)} %copy-done.8, bf16[1536,1536]{1,0:T(8,128)(2,1)} %slice.363.dy_ref, ...), custom_call_target="tpu_custom_call" | custom-call | flops 14495514624 | bytes 11796480 | tf_op jit(solution)/shard_map/pallas_call | solution.py:411
  454.9 4.0 fusion.124
  461.7 5.2 fusion.6
  477.9 11.1 %collective-permute-done.31 = bf16[2,384,384]{2,1,0:T(8,128)(2,1)S(1)} collective-permute-done((bf16[2,384,384]{2,1,0:T(8,128)(2,1)S(1)}, bf16[2,384,384]{2,1,0:T(8,128)(2,1)S(1)}, u32[]{:S(2)}, u32[]{:S(2)}) %collective-permute-start.31) | collective-permute-done | bytes 589856 | tf_op jit(solution)/shard_map/ppermute | solution.py:53
  489.3 3.5 collective-permute-done.29
  503.1 27.6 %shard_map.315 = (bf16[2,3,64,1536]{3,2,1,0:T(8,128)(2,1)S(1)}, bf16[2,64,1536]{2,1,0:T(8,128)(2,1)S(1)}, bf16[2,64,1536]{2,1,0:T(8,128)(2,1)S(1)}) custom-call(bf16[2,3,64,1536]{3,2,1,0:T(8,128)(2,1)S(1)} %copy-done.2, bf16[2,64,1536]{2,1,0:T(8,128)(2,1)S(1)} %pad_maximum_fusion.7.k_ref, bf16[2,64,1536]{2,1,0:T(8,128)(2,1)S(1)} %bitcast.324, ...), custom_call_target="tpu_custom_call" | custom-call | flops 3623878656 | bytes 28311552 | tf_op jit(solution)/shard_map/pallas_call | solution.py:269
  540.5 3.6 fusion.27
  549.8 5.1 collective-permute-done.37
  561.1 4.4 collective-permute-start.44
  565.4 4.2 fusion.23
  589.3 10.6 %collective-permute-done.47 = f32[40,1536]{1,0:T(8,128)} collective-permute-done((f32[40,1536]{1,0:T(8,128)}, f32[40,1536]{1,0:T(8,128)}, u32[]{:S(2)}, u32[]{:S(2)}) %collective-permute-start.47) | collective-permute-done | bytes 245792 | tf_op jit(solution)/shard_map/ppermute | solution.py:53
  599.9 4.0 fusion.13
  (440 shorter events, 219.2 us)
Async XLA Ops:
  7.2 93.7 %all-gather.5.cloned.1.call-start = ((), (), s32[]{:S(2)}) async-start(), calls=%async_computation | async-start | bytes 2654208 | tf_op jit(solution)/shard_map/all_gather | solution.py:585
  10.8 149.7 %all-gather.7.cloned.1.call-start = ((), (), s32[]{:S(2)}) async-start(), calls=%async_computation.1 | async-start | bytes 2654208 | tf_op jit(solution)/shard_map/all_gather | solution.py:585
  10.9 40.7 %collective-permute-start = (bf16[384,1536]{1,0:T(8,128)(2,1)}, bf16[384,1536]{1,0:T(8,128)(2,1)}, u32[]{:S(2)}, u32[]{:S(2)}) collective-permute-start(bf16[384,1536]{1,0:T(8,128)(2,1)} %bitcast.338), channel_id=1, source_target_pairs={{0,4},{4,0},{8,12},{12,8},{1,5},{5,1},{9,13},{13,9},{2,6},{6,2},{1... | collective-permute-start | bytes 3538952 | tf_op jit(solution)/shard_map/ppermute | solution.py:47
  11.4 32.9 %collective-permute-start.1 = (bf16[384,1536]{1,0:T(8,128)(2,1)}, bf16[384,1536]{1,0:T(8,128)(2,1)}, u32[]{:S(2)}, u32[]{:S(2)}) collective-permute-start(bf16[384,1536]{1,0:T(8,128)(2,1)} %bitcast.339), channel_id=1, source_target_pairs={{0,8},{4,12},{8,0},{12,4},{1,9},{5,13},{9,1},{13,5},{2,10},{6,14},... | collective-permute-start | bytes 3538952 | tf_op jit(solution)/shard_map/ppermute | solution.py:53
  18.8 68.9 %collective-permute-start.10 = (bf16[3,3,3,64,512]{4,3,2,1,0:T(8,128)(2,1)}, bf16[3,3,3,64,512]{4,3,2,1,0:T(8,128)(2,1)}, u32[]{:S(2)}, u32[]{:S(2)}) collective-permute-start(bf16[3,3,3,64,512]{4,3,2,1,0:T(8,128)(2,1)} %bitcast.55.refs_0_), channel_id=1, source_target_pairs={{0,1},{1,2},{2,3},{3,0},{4,5},{5,6},{6,7},{7,4},{8,9},{9,10},{10,1... | collective-permute-start | bytes 5308424 | tf_op jit(solution)/shard_map/ppermute | solution.py:120
  20.4 67.4 %collective-permute-start.11 = (bf16[3,3,3,64,512]{4,3,2,1,0:T(8,128)(2,1)}, bf16[3,3,3,64,512]{4,3,2,1,0:T(8,128)(2,1)}, u32[]{:S(2)}, u32[]{:S(2)}) collective-permute-start(bf16[3,3,3,64,512]{4,3,2,1,0:T(8,128)(2,1)} %bitcast.55.refs_0_), channel_id=1, source_target_pairs={{0,16},{16,0},{1,17},{17,1},{2,18},{18,2},{3,19},{19,3},{4,20},{20... | collective-permute-start | bytes 5308424 | tf_op jit(solution)/shard_map/ppermute | solution.py:120
  23.7 551.0 %all-gather.9.cloned.1.call-start = ((), (), s32[]{:S(2)}) async-start(), calls=%async_computation.2 | async-start | bytes 2211840 | tf_op jit(solution)/shard_map/all_gather | solution.py:761
  60.9 37.5 %collective-permute-start.7 = (bf16[384,1664]{1,0:T(8,128)(2,1)S(1)}, bf16[384,1664]{1,0:T(8,128)(2,1)}, u32[]{:S(2)}, u32[]{:S(2)}) collective-permute-start(bf16[384,1664]{1,0:T(8,128)(2,1)S(1)} %copy-done.20), channel_id=1, source_target_pairs={{0,4},{4,0},{8,12},{12,8},{1,5},{5,1},{9,13},{13,9},{2,6},{6,2},{1... | collective-permute-start | bytes 3833864 | tf_op jit(solution)/shard_map/ppermute | solution.py:47
  61.5 37.0 %collective-permute-start.8 = (bf16[384,1664]{1,0:T(8,128)(2,1)S(1)}, bf16[384,1664]{1,0:T(8,128)(2,1)}, u32[]{:S(2)}, u32[]{:S(2)}) collective-permute-start(bf16[384,1664]{1,0:T(8,128)(2,1)S(1)} %copy-done.20), channel_id=1, source_target_pairs={{0,8},{4,12},{8,0},{12,4},{1,9},{5,13},{9,1},{13,5},{2,10},{6,14},... | collective-permute-start | bytes 3833864 | tf_op jit(solution)/shard_map/ppermute | solution.py:53
  87.8 62.5 %collective-permute-start.12 = (bf16[3,3,3,64,512]{4,3,2,1,0:T(8,128)(2,1)}, bf16[3,3,3,64,512]{4,3,2,1,0:T(8,128)(2,1)}, u32[]{:S(2)}, u32[]{:S(2)}) collective-permute-start(bf16[3,3,3,64,512]{4,3,2,1,0:T(8,128)(2,1)} %collective-permute-done.10.refs_2_), channel_id=1, source_target_pairs={{0,1},{1,2},{2,3},{3,0},{4,5},{5,6},{6,7},{7,4},{8,9},{9,10},{10,1... | collective-permute-start | bytes 5308424 | tf_op jit(solution)/shard_map/ppermute | solution.py:120
  89.1 63.3 %collective-permute-start.13 = (bf16[3,3,3,64,512]{4,3,2,1,0:T(8,128)(2,1)}, bf16[3,3,3,64,512]{4,3,2,1,0:T(8,128)(2,1)}, u32[]{:S(2)}, u32[]{:S(2)}) collective-permute-start(bf16[3,3,3,64,512]{4,3,2,1,0:T(8,128)(2,1)} %collective-permute-done.10.refs_2_), channel_id=1, source_target_pairs={{0,16},{16,0},{1,17},{17,1},{2,18},{18,2},{3,19},{19,3},{4,20},{20... | collective-permute-start | bytes 5308424 | tf_op jit(solution)/shard_map/ppermute | solution.py:120
  98.4 62.0 %collective-permute-start.9 = (bf16[384,1664]{1,0:T(8,128)(2,1)}, bf16[384,1664]{1,0:T(8,128)(2,1)}, u32[]{:S(2)}, u32[]{:S(2)}) collective-permute-start(bf16[384,1664]{1,0:T(8,128)(2,1)} %collective-permute-done.8), channel_id=1, source_target_pairs={{0,4},{4,0},{8,12},{12,8},{1,5},{5,1},{9,13},{13,9},{2,6},{6,2},{1... | collective-permute-start | bytes 3833864 | tf_op jit(solution)/shard_map/ppermute | solution.py:47
  135.9 30.6 %collective-permute-start.4 = (bf16[384,1536]{1,0:T(8,128)(2,1)S(1)}, bf16[384,1536]{1,0:T(8,128)(2,1)}, u32[]{:S(2)}, u32[]{:S(2)}) collective-permute-start(bf16[384,1536]{1,0:T(8,128)(2,1)S(1)} %bitcast.319), channel_id=1, source_target_pairs={{0,8},{4,12},{8,0},{12,4},{1,9},{5,13},{9,1},{13,5},{2,10},{6,14},... | collective-permute-start | bytes 3538952 | tf_op jit(solution)/shard_map/ppermute | solution.py:53
  138.9 35.0 %collective-permute-start.3 = (bf16[384,1536]{1,0:T(8,128)(2,1)S(1)}, bf16[384,1536]{1,0:T(8,128)(2,1)}, u32[]{:S(2)}, u32[]{:S(2)}) collective-permute-start(bf16[384,1536]{1,0:T(8,128)(2,1)S(1)} %bitcast.320), channel_id=1, source_target_pairs={{0,4},{4,0},{8,12},{12,8},{1,5},{5,1},{9,13},{13,9},{2,6},{6,2},{1... | collective-permute-start | bytes 3538952 | tf_op jit(solution)/shard_map/ppermute | solution.py:47
  150.3 29.1 %collective-permute-start.18 = (bf16[2,3,3,64,512]{4,3,2,1,0:T(8,128)(2,1)}, bf16[2,3,3,64,512]{4,3,2,1,0:T(8,128)(2,1)}, u32[]{:S(2)}, u32[]{:S(2)}) collective-permute-start(bf16[2,3,3,64,512]{4,3,2,1,0:T(8,128)(2,1)} %bitcast.372), channel_id=1, source_target_pairs={{0,16},{16,0},{1,17},{17,1},{2,18},{18,2},{3,19},{19,3},{4,20},{20... | collective-permute-start | bytes 3538952 | tf_op jit(solution)/shard_map/ppermute | solution.py:120
  152.4 36.4 %collective-permute-start.17 = (bf16[2,3,3,64,512]{4,3,2,1,0:T(8,128)(2,1)}, bf16[2,3,3,64,512]{4,3,2,1,0:T(8,128)(2,1)}, u32[]{:S(2)}, u32[]{:S(2)}) collective-permute-start(bf16[2,3,3,64,512]{4,3,2,1,0:T(8,128)(2,1)} %bitcast.373), channel_id=1, source_target_pairs={{0,1},{1,2},{2,3},{3,0},{4,5},{5,6},{6,7},{7,4},{8,9},{9,10},{10,1... | collective-permute-start | bytes 3538952 | tf_op jit(solution)/shard_map/ppermute | solution.py:120
  160.4 37.9 %collective-permute-start.6 = (bf16[1536,768]{1,0:T(8,128)(2,1)}, bf16[1536,768]{1,0:T(8,128)(2,1)}, u32[]{:S(2)}, u32[]{:S(2)}) collective-permute-start(bf16[1536,768]{1,0:T(8,128)(2,1)} %all-gather.7.cloned.1.call-done), channel_id=1, source_target_pairs={{0,4},{4,0},{8,12},{12,8},{1,5},{5,1},{9,13},{13,9},{2,6},{6,2},{1... | collective-permute-start | bytes 7077896 | tf_op jit(solution)/shard_map/ppermute | solution.py:47
  173.9 52.8 %collective-permute-start.14 = (bf16[3,3,3,64,512]{4,3,2,1,0:T(8,128)(2,1)}, bf16[3,3,3,64,512]{4,3,2,1,0:T(8,128)(2,1)}, u32[]{:S(2)}, u32[]{:S(2)}) collective-permute-start(bf16[3,3,3,64,512]{4,3,2,1,0:T(8,128)(2,1)} %collective-permute-done.12.refs_4_), channel_id=1, source_target_pairs={{0,1},{1,2},{2,3},{3,0},{4,5},{5,6},{6,7},{7,4},{8,9},{9,10},{10,1... | collective-permute-start | bytes 5308424 | tf_op jit(solution)/shard_map/ppermute | solution.py:120
  179.1 47.5 %collective-permute-start.15 = (bf16[3,3,3,64,512]{4,3,2,1,0:T(8,128)(2,1)}, bf16[3,3,3,64,512]{4,3,2,1,0:T(8,128)(2,1)}, u32[]{:S(2)}, u32[]{:S(2)}) collective-permute-start(bf16[3,3,3,64,512]{4,3,2,1,0:T(8,128)(2,1)} %collective-permute-done.12.refs_4_), channel_id=1, source_target_pairs={{0,16},{16,0},{1,17},{17,1},{2,18},{18,2},{3,19},{19,3},{4,20},{20... | collective-permute-start | bytes 5308424 | tf_op jit(solution)/shard_map/ppermute | solution.py:120
  188.7 59.6 %collective-permute-start.19 = (bf16[2,3,3,64,512]{4,3,2,1,0:T(8,128)(2,1)}, bf16[2,3,3,64,512]{4,3,2,1,0:T(8,128)(2,1)}, u32[]{:S(2)}, u32[]{:S(2)}) collective-permute-start(bf16[2,3,3,64,512]{4,3,2,1,0:T(8,128)(2,1)} %collective-permute-done.17.refs_7_), channel_id=1, source_target_pairs={{0,1},{1,2},{2,3},{3,0},{4,5},{5,6},{6,7},{7,4},{8,9},{9,10},{10,1... | collective-permute-start | bytes 3538952 | tf_op jit(solution)/shard_map/ppermute | solution.py:120
  189.1 59.2 %collective-permute-start.20 = (bf16[2,3,3,64,512]{4,3,2,1,0:T(8,128)(2,1)}, bf16[2,3,3,64,512]{4,3,2,1,0:T(8,128)(2,1)}, u32[]{:S(2)}, u32[]{:S(2)}) collective-permute-start(bf16[2,3,3,64,512]{4,3,2,1,0:T(8,128)(2,1)} %collective-permute-done.17.refs_7_), channel_id=1, source_target_pairs={{0,16},{16,0},{1,17},{17,1},{2,18},{18,2},{3,19},{19,3},{4,20},{20... | collective-permute-start | bytes 3538952 | tf_op jit(solution)/shard_map/ppermute | solution.py:120
  226.7 57.5 %collective-permute-start.16 = (bf16[3,3,3,64,512]{4,3,2,1,0:T(8,128)(2,1)}, bf16[3,3,3,64,512]{4,3,2,1,0:T(8,128)(2,1)}, u32[]{:S(2)}, u32[]{:S(2)}) collective-permute-start(bf16[3,3,3,64,512]{4,3,2,1,0:T(8,128)(2,1)} %collective-permute-done.14.refs_6_), channel_id=1, source_target_pairs={{0,16},{16,0},{1,17},{17,1},{2,18},{18,2},{3,19},{19,3},{4,20},{20... | collective-permute-start | bytes 5308424 | tf_op jit(solution)/shard_map/ppermute | solution.py:120
  248.4 67.7 %collective-permute-start.21 = (bf16[2,3,3,64,512]{4,3,2,1,0:T(8,128)(2,1)}, bf16[2,3,3,64,512]{4,3,2,1,0:T(8,128)(2,1)}, u32[]{:S(2)}, u32[]{:S(2)}) collective-permute-start(bf16[2,3,3,64,512]{4,3,2,1,0:T(8,128)(2,1)} %collective-permute-done.19.refs_9_), channel_id=1, source_target_pairs={{0,1},{1,2},{2,3},{3,0},{4,5},{5,6},{6,7},{7,4},{8,9},{9,10},{10,1... | collective-permute-start | bytes 3538952 | tf_op jit(solution)/shard_map/ppermute | solution.py:120
  248.4 67.7 %collective-permute-start.22 = (bf16[2,3,3,64,512]{4,3,2,1,0:T(8,128)(2,1)}, bf16[2,3,3,64,512]{4,3,2,1,0:T(8,128)(2,1)}, u32[]{:S(2)}, u32[]{:S(2)}) collective-permute-start(bf16[2,3,3,64,512]{4,3,2,1,0:T(8,128)(2,1)} %collective-permute-done.19.refs_9_), channel_id=1, source_target_pairs={{0,16},{16,0},{1,17},{17,1},{2,18},{18,2},{3,19},{19,3},{4,20},{20... | collective-permute-start | bytes 3538952 | tf_op jit(solution)/shard_map/ppermute | solution.py:120
  316.1 32.4 %collective-permute-start.23 = (bf16[2,3,3,64,512]{4,3,2,1,0:T(8,128)(2,1)}, bf16[2,3,3,64,512]{4,3,2,1,0:T(8,128)(2,1)}, u32[]{:S(2)}, u32[]{:S(2)}) collective-permute-start(bf16[2,3,3,64,512]{4,3,2,1,0:T(8,128)(2,1)} %collective-permute-done.21.refs_11_), channel_id=1, source_target_pairs={{0,16},{16,0},{1,17},{17,1},{2,18},{18,2},{3,19},{19,3},{4,20},{20... | collective-permute-start | bytes 3538952 | tf_op jit(solution)/shard_map/ppermute | solution.py:120
  383.7 52.5 %collective-permute-start.25 = (bf16[384,1664]{1,0:T(8,128)(2,1)}, bf16[384,1664]{1,0:T(8,128)(2,1)}, u32[]{:S(2)}, u32[]{:S(2)}) collective-permute-start(bf16[384,1664]{1,0:T(8,128)(2,1)} %fusion.8), channel_id=1, source_target_pairs={{0,8},{4,12},{8,0},{12,4},{1,9},{5,13},{9,1},{13,5},{2,10},{6,14},... | collective-permute-start | bytes 3833864 | tf_op jit(solution)/shard_map/ppermute | solution.py:53
  439.0 35.7 %collective-permute-start.34 = (bf16[384,1536]{1,0:T(8,128)(2,1)}, bf16[384,1536]{1,0:T(8,128)(2,1)}, u32[]{:S(2)}, u32[]{:S(2)}) collective-permute-start(bf16[384,1536]{1,0:T(8,128)(2,1)} %dynamic-slice_bitcast_fusion.4), channel_id=1, source_target_pairs={{0,4},{4,0},{8,12},{12,8},{1,5},{5,1},{9,13},{13,9},{2,6},{6,2},{1... | collective-permute-start | bytes 3538952 | tf_op jit(solution)/shard_map/ppermute | solution.py:47
  494.7 36.0 %collective-permute-start.35 = (bf16[384,1536]{1,0:T(8,128)(2,1)}, bf16[384,1536]{1,0:T(8,128)(2,1)}, u32[]{:S(2)}, u32[]{:S(2)}) collective-permute-start(bf16[384,1536]{1,0:T(8,128)(2,1)} %fusion.19), channel_id=1, source_target_pairs={{0,8},{4,12},{8,0},{12,4},{1,9},{5,13},{9,1},{13,5},{2,10},{6,14},... | collective-permute-start | bytes 3538952 | tf_op jit(solution)/shard_map/ppermute | solution.py:53
  499.1 66.4 %collective-permute-start.27 = (bf16[384,1536]{1,0:T(8,128)(2,1)}, bf16[384,1536]{1,0:T(8,128)(2,1)}, u32[]{:S(2)}, u32[]{:S(2)}) collective-permute-start(bf16[384,1536]{1,0:T(8,128)(2,1)} %dynamic-slice_bitcast_fusion.5), channel_id=1, source_target_pairs={{0,4},{4,0},{8,12},{12,8},{1,5},{5,1},{9,13},{13,9},{2,6},{6,2},{1... | collective-permute-start | bytes 3538952 | tf_op jit(solution)/shard_map/ppermute | solution.py:47
  557.5 28.2 %collective-permute-start.41 = (bf16[384,1536]{1,0:T(8,128)(2,1)}, bf16[384,1536]{1,0:T(8,128)(2,1)}, u32[]{:S(2)}, u32[]{:S(2)}) collective-permute-start(bf16[384,1536]{1,0:T(8,128)(2,1)} %dynamic-slice_bitcast_fusion.2), channel_id=1, source_target_pairs={{0,4},{4,0},{8,12},{12,8},{1,5},{5,1},{9,13},{13,9},{2,6},{6,2},{1... | collective-permute-start | bytes 3538952 | tf_op jit(solution)/shard_map/ppermute | solution.py:47
  557.5 29.1 %collective-permute-start.40 = (bf16[384,1536]{1,0:T(8,128)(2,1)}, bf16[384,1536]{1,0:T(8,128)(2,1)}, u32[]{:S(2)}, u32[]{:S(2)}) collective-permute-start(bf16[384,1536]{1,0:T(8,128)(2,1)} %fusion.18), channel_id=1, source_target_pairs={{0,8},{4,12},{8,0},{12,4},{1,9},{5,13},{9,1},{13,5},{2,10},{6,14},... | collective-permute-start | bytes 3538952 | tf_op jit(solution)/shard_map/ppermute | solution.py:53
  581.7 26.6 %collective-permute-start.49 = (f32[64,1536]{1,0:T(8,128)S(1)}, f32[64,1536]{1,0:T(8,128)}, u32[]{:S(2)}, u32[]{:S(2)}) collective-permute-start(f32[64,1536]{1,0:T(8,128)S(1)} %bitcast.357), channel_id=1, source_target_pairs={{0,4},{4,0},{8,12},{12,8},{1,5},{5,1},{9,13},{13,9},{2,6},{6,2},{1... | collective-permute-start | bytes 1179656 | tf_op jit(solution)/shard_map/ppermute | solution.py:47
  (96 other events, 753.7 us)
Sparse Core Ops, SparseCore 0:
  10.9 79.6 all-gather.4
  93.3 66.3 all-gather.6
  499.9 49.4 all-gather.8
